TPU v7x, 512 devices: a whole 4x8x8 slice. The times are simulated.
512 devices in a mesh: grp: 4 (over x), blk: 128 (over z, y, core).
Axes of the slice: x: 4, y: 8, z: 8, core: 2. Of those that a mesh axis runs over, the one named last changes fastest.
Arguments:
- queries: bfloat16 [65536, 4096], P(('blk', 'grp')), may hold values from -150 to 150
- keys: bfloat16 [65536, 4096], P(('blk', 'grp')), may hold values from -4 to 4
- values: bfloat16 [65536, 4096], P(('blk', 'grp')), may hold values from -6 to 6
Outputs:
- attended: bfloat16 [65536, 4096], P(('blk', 'grp'))
All inputs are finite; a program needn't handle non-finite values.
Results may differ from a plain program's by a relative error of at most 0.0033.
Values may be sent and summed in bfloat16 or wider, within the bound.
No kernel may reach another device: no remote copies, remote signals or barrier semaphores. Data moves between devices by JAX's collectives and lax.ppermute only.
A program may use at most 64 MiB of HBM per device.

v0:
```python
import math

import jax
import jax.numpy as jnp
from jax import lax
from jax.experimental import pallas as pl
from jax.experimental.pallas import tpu as pltpu
from jax.sharding import Mesh
from jax.sharding import PartitionSpec as P

HD = 128
STRIDE = 32
QUADS = 8
POS = 128
ROWS = 4
LOW = -1e30
SCALE = math.log2(math.e) / math.sqrt(HD)
SUM_ROWS = 16
PAY = 2 * POS + SUM_ROWS

f32 = jnp.float32
bf16 = jnp.bfloat16


def dot_t(a, b):
    return lax.dot_general(a, b, (((1,), (1,)), ((), ())), preferred_element_type=f32)


def dot_tl(a, b):
    return lax.dot_general(a, b, (((0,), (0,)), ((), ())), preferred_element_type=f32)


def dot(a, b):
    return lax.dot_general(a, b, (((1,), (0,)), ((), ())), preferred_element_type=f32)


def iota(shape, dim):
    return lax.broadcasted_iota(jnp.int32, shape, dim)


def one_hot(rows, cols, source):
    row = iota((rows, cols), 0)
    col = iota((rows, cols), 1)
    return jnp.where(source(row) == col, 1.0, 0.0).astype(bf16)


def div12(o):
    return (o * 5462) >> 16


def head(ref, quad, kind):
    start = (quad * 4 + kind) * HD
    return ref[:, start : start + HD]


def pack_kernel(q_ref, k_ref, v_ref, item_ref, quad_ref):
    def source(o):
        col = div12(o)
        rest = o - 12 * col
        return (rest >> 2) * POS + (rest & 3) * STRIDE + col

    perm = one_hot(384, 384, source)
    pick = one_hot(
        SUM_ROWS, 512, lambda o: (o >> 2) * POS + (o & 3) * STRIDE + STRIDE - 1
    )
    for quad in range(QUADS):
        stack = jnp.concatenate(
            [head(q_ref, quad, 1), head(k_ref, quad, 1), head(v_ref, quad, 1)], axis=0
        )
        item_ref[quad] = dot(perm, stack).astype(bf16)
        for h in range(2):
            quad_ref[quad, h * POS : (h + 1) * POS, :] = head(q_ref, quad, 2 + h)
        summary = jnp.concatenate(
            [
                head(k_ref, quad, 2),
                head(k_ref, quad, 3),
                head(v_ref, quad, 2),
                head(v_ref, quad, 3),
            ],
            axis=0,
        )
        quad_ref[quad, 2 * POS :, :] = dot(pick, summary).astype(bf16)


def rows_kernel(q_ref, k_ref, v_ref, row_ref, part_ref, stat_ref):
    key = iota((POS, POS), 0)
    pos = iota((POS, POS), 1)
    visible = jnp.logical_and((key >> 5) == (pos >> 5), key <= pos)
    for quad in range(QUADS):
        for kind in (0, 2, 3):
            s = dot_t(head(k_ref, quad, kind), head(q_ref, quad, kind)) * SCALE
            s = jnp.where(visible, s, LOW)
            m = jnp.max(s, axis=0, keepdims=True)
            p = jnp.where(visible, jnp.exp2(s - m), 0.0)
            total = jnp.sum(p, axis=0, keepdims=True)
            acc = dot_tl(head(v_ref, quad, kind), p.astype(bf16))
            if kind == 0:
                row_ref[quad] = (acc / total).T.astype(bf16)
            else:
                slot = quad * 2 + kind - 2
                part_ref[slot] = acc
                row = iota((8, POS), 0)
                stat_ref[slot] = jnp.where(row == 0, m, total)


def column_kernel(core_ref, x_ref, out_ref, q_scr, k_scr, v_scr):
    core = core_ref[0]

    def source(o):
        within = o & 31
        return (within >> 2) * 12 + (o >> 5) * 4 + (within & 3)

    split = one_hot(96, 96, source)
    for c in range(2):
        for g in range(32):
            y = dot(split, x_ref[c, g * 96 : (g + 1) * 96, :]).astype(bf16)
            k_scr[c, g * 32 : (g + 1) * 32, :] = y[32:64]
            v_scr[c, g * 32 : (g + 1) * 32, :] = y[64:96]

            @pl.when(core == c)
            def _(y=y, g=g):
                q_scr[g * 32 : (g + 1) * 32, :] = y[0:32]

    block = 256
    for qb in range(1024 // block):
        q = q_scr[qb * block : (qb + 1) * block, :]
        jq = iota((block, block), 1)
        row_q = ((jq >> 4) << 5) + (jq & 15) + 16 * core
        jk = iota((block, block), 0)
        pieces = []
        m = jnp.full((1, block), LOW, f32)
        for kb in range(qb + 1):
            for c in range(2):
                s = dot_t(k_scr[c, kb * block : (kb + 1) * block, :], q) * SCALE
                if kb == qb:
                    row_k = ((jk >> 4) << 5) + (jk & 15) + 16 * c
                    s = jnp.where(row_k <= row_q, s, LOW)
                m = jnp.maximum(m, jnp.max(s, axis=0, keepdims=True))
                pieces.append((kb, c, s))
        total = jnp.zeros((1, block), f32)
        acc = jnp.zeros((HD, block), f32)
        for kb, c, s in pieces:
            p = jnp.exp2(s - m)
            total = total + jnp.sum(p, axis=0, keepdims=True)
            acc = acc + dot_tl(v_scr[c, kb * block : (kb + 1) * block, :], p.astype(bf16))
        out_ref[qb * block : (qb + 1) * block, :] = (acc / total).T.astype(bf16)


def far_kernel(seg_ref, q_ref, kv_ref, out_ref):
    seg = seg_ref[0]
    chunk = 8
    keys = chunk * 32
    lanes = QUADS * POS
    last = seg // chunk

    for h in range(2):
        q = jnp.concatenate(
            [q_ref[e, h * POS : (h + 1) * POS, :] for e in range(QUADS)], axis=0
        )

        def step(i, carried, masked):
            m, total, acc = carried
            k = jnp.concatenate(
                [kv_ref[i * chunk + t, h * 32 : h * 32 + 32, :] for t in range(chunk)], axis=0
            )
            v = jnp.concatenate(
                [kv_ref[i * chunk + t, 64 + h * 32 : 96 + h * 32, :] for t in range(chunk)],
                axis=0,
            )
            s = dot_t(k, q) * SCALE
            if masked:
                row_k = i * keys + iota((keys, lanes), 0)
                row_q = seg * 32 + (iota((keys, lanes), 1) >> 5)
                visible = row_k < row_q
                s = jnp.where(visible, s, LOW)
            m_next = jnp.maximum(m, jnp.max(s, axis=0, keepdims=True))
            p = jnp.exp2(s - m_next)
            if masked:
                p = jnp.where(visible, p, 0.0)
            rescale = jnp.exp2(m - m_next)
            total = total * rescale + jnp.sum(p, axis=0, keepdims=True)
            acc = acc * rescale + dot_tl(v, p.astype(bf16))
            return m_next, total, acc

        carried = (
            jnp.full((1, lanes), LOW, f32),
            jnp.zeros((1, lanes), f32),
            jnp.zeros((HD, lanes), f32),
        )
        carried = lax.fori_loop(0, last, lambda i, x: step(i, x, False), carried)
        m, total, acc = step(last, carried, True)
        seen = total > 0.0
        safe = jnp.where(seen, total, 1.0)
        out = (acc / safe).astype(bf16)
        lse = jnp.where(seen, m + jnp.log2(safe), LOW)
        high = lse.astype(bf16).astype(f32)
        left = lse - high
        mid = left.astype(bf16).astype(f32)
        low = left - mid
        row = iota((SUM_ROWS, POS), 0) - 3 * h
        for e in range(QUADS):
            at = slice(e * POS, (e + 1) * POS)
            out_ref[e, h * POS : (h + 1) * POS, :] = out[:, at]
            terms = jnp.where(
                row == 0,
                high[:, at],
                jnp.where(row == 1, mid[:, at], jnp.where(row == 2, low[:, at], 0.0)),
            )
            if h == 0:
                out_ref[e, 2 * POS :, :] = terms.astype(bf16)
            else:
                out_ref[e, 2 * POS :, :] = (
                    out_ref[e, 2 * POS :, :].astype(f32) + terms
                ).astype(bf16)


def final_kernel(far_ref, col_ref, row_ref, part_ref, stat_ref, out_ref):
    back = one_hot(POS, POS, lambda o: (o & 31) * 4 + (o >> 5))
    for quad in range(QUADS):
        base = quad * 4 * HD
        out_ref[:, base : base + HD] = row_ref[quad]
        out_ref[:, base + HD : base + 2 * HD] = dot(
            back, col_ref[quad * POS : (quad + 1) * POS, :]
        ).astype(bf16)
        terms = far_ref[quad, 2 * POS :, :].astype(f32)
        for h in range(2):
            lse = (terms[3 * h : 3 * h + 1] + terms[3 * h + 1 : 3 * h + 2]) + terms[
                3 * h + 2 : 3 * h + 3
            ]
            m = stat_ref[quad * 2 + h, 0:1, :]
            total = stat_ref[quad * 2 + h, 1:2, :]
            top = jnp.maximum(m, lse)
            own = jnp.exp2(m - top)
            far = jnp.exp2(lse - top)
            scale = 1.0 / (total * own + far)
            merged = (
                part_ref[quad * 2 + h] * (own * scale)
                + far_ref[quad, h * POS : (h + 1) * POS, :].astype(f32) * (far * scale)
            )
            start = base + (2 + h) * HD
            out_ref[:, start : start + HD] = merged.T.astype(bf16)


def call(kernel, outs, args, scalars=0, scratch=(), flops=0, moved=0, exps=0):
    vmem = pl.BlockSpec(memory_space=pltpu.VMEM)
    smem = pl.BlockSpec(memory_space=pltpu.SMEM)
    shapes = [jax.ShapeDtypeStruct(s, d) for s, d in outs]
    many = len(shapes) > 1
    return pl.pallas_call(
        kernel,
        out_shape=shapes if many else shapes[0],
        in_specs=[smem] * scalars + [vmem] * (len(args) - scalars),
        out_specs=[vmem] * len(shapes) if many else vmem,
        scratch_shapes=list(scratch),
        compiler_params=pltpu.CompilerParams(vmem_limit_bytes=40 * 1024 * 1024),
        cost_estimate=pl.CostEstimate(flops=flops, bytes_accessed=moved, transcendentals=exps),
    )(*args)


def exchange(array, axes):
    return lax.all_to_all(array, axes, split_axis=0, concat_axis=0, tiled=True)


def body(queries, keys, values):
    near = ("c", "x")
    wide = ("z", "u", "w", "x")
    mib = 1 << 20
    items, quads = call(
        pack_kernel,
        [((QUADS, 384, HD), bf16), ((QUADS, PAY, HD), bf16)],
        (queries, keys, values),
        flops=2 * 8 * 384 * 384 * 128,
        moved=5 * mib,
    )
    quads = exchange(quads, near)
    summary = (
        quads[:, 2 * POS :]
        .reshape(QUADS, 2, 2, ROWS, HD)
        .transpose(1, 2, 0, 3, 4)
        .reshape(1, POS, HD)
    )
    summary = lax.all_gather(summary, "w", axis=0, tiled=True)
    summary = lax.all_gather(summary, ("z", "u"), axis=0, tiled=True)

    items = exchange(items.reshape(768, ROWS, HD), wide).reshape(1, 3072, HD)
    row_out, part, stat = call(
        rows_kernel,
        [((QUADS, POS, HD), bf16), ((16, POS, POS), f32), ((16, 8, POS), f32)],
        (queries, keys, values),
        flops=24 * 4 * 128 * 128 * 128,
        moved=5 * mib,
        exps=24 * 128 * 128,
    )
    items = lax.all_gather(items, "c", axis=0, tiled=True)
    core = lax.axis_index("c").astype(jnp.int32).reshape(1)
    column = call(
        column_kernel,
        [((1024, HD), bf16)],
        (core, items),
        scalars=1,
        scratch=[
            pltpu.VMEM((1024, HD), bf16),
            pltpu.VMEM((2, 1024, HD), bf16),
            pltpu.VMEM((2, 1024, HD), bf16),
        ],
        flops=4 * 1024 * 1280 * 128,
        moved=2 * mib,
        exps=1024 * 1280,
    )
    column = exchange(column.reshape(256, ROWS, HD), wide).reshape(1024, HD)

    seg = lax.axis_index(("z", "u", "w")).astype(jnp.int32).reshape(1)
    far = call(
        far_kernel,
        [((QUADS, PAY, POS), bf16)],
        (seg, quads, summary),
        scalars=1,
        flops=8 * 1024 * 2048 * 128,
        moved=3 * mib,
        exps=2 * 1024 * 2048,
    )
    far = exchange(far, near)
    return call(
        final_kernel,
        [((POS, QUADS * 4 * HD), bf16)],
        (far, column, row_out, part, stat),
        flops=2 * 8 * 128 * 128 * 128,
        moved=4 * mib,
    )


def solution(mesh):
    fine = Mesh(mesh.devices.reshape(4, 8, 4, 2, 2), ("x", "z", "u", "w", "c"))
    spec = P(("z", "u", "w", "c", "x"), None)
    return jax.shard_map(
        body, mesh=fine, in_specs=(spec, spec, spec), out_specs=spec, check_vma=False
    )
```

profile of v0, /device:TPU:1, one launch (start us, length us, event | category | flops | bytes accessed | tf_op | source)
XLA Modules:
  0.0 194.6 jit_solution(752807668017685490)
XLA Ops:
  6.5 1.2 copy-done
  7.8 1.2 copy-done.2
  9.0 1.2 copy-done.4
  10.2 1.0 shard_map.37
  11.2 46.3 %all_to_all.20 = bf16[768,4,128]{2,1,0:T(4,128)(2,1)} all-to-all(bf16[768,4,128]{2,1,0:T(4,128)(2,1)S(1)} %bitcast.11), channel_id=1, replica_groups=mesh['x'=4,'z'=8,'u'=4,'w'=2,'c'=2] {'z','u','w','x'}, dimensions={0} | all-to-all | bytes 1572864 | tf_op jit(solution)/shard_map/all_to_all | solution.py:261
  57.6 16.4 %all_to_all.21.q_ref = bf16[8,272,128]{2,1,0:T(8,128)(2,1)S(1)} all-to-all(bf16[8,272,128]{2,1,0:T(8,128)(2,1)S(1)} %get-tuple-element.10), channel_id=1, replica_groups=mesh['x'=4,'z'=8,'u'=4,'w'=2,'c'=2] {'c','x'}, dimensions={0} | all-to-all | bytes 1114112 | tf_op jit(solution)/shard_map/all_to_all | solution.py:261
  74.0 0.8 copy-done.8
  74.8 3.5 %all_gather.9 = bf16[2,128,128]{2,1,0:T(8,128)(2,1)} all-gather(bf16[1,128,128]{2,1,0:T(8,128)(2,1)S(1)} %bitcast.13), channel_id=1, replica_groups=mesh['x'=4,'z'=8,'u'=4,'w'=2,'c'=2] {'w'}, dimensions={0}, use_global_device_ids=true | all-gather | bytes 98304 | tf_op jit(solution)/shard_map/all_gather | solution.py:282
  78.4 1.4 copy-done.14
  79.8 12.3 %shard_map.39 = bf16[1024,128]{1,0:T(8,128)(2,1)} custom-call(s32[1]{0:T(128)} %bitcast.4.core_ref, bf16[2,3072,128]{2,1,0:T(8,128)(2,1)S(1)} %copy-done.14), custom_call_target="tpu_custom_call" | custom-call | flops 671088640 | bytes 2097152 | tf_op jit(solution)/shard_map/pallas_call | solution.py:249
  92.1 11.0 %all-to-all-start.3 = ((bf16[256,4,128]{2,1,0:T(4,128)(2,1)}), bf16[256,4,128]{2,1,0:T(4,128)(2,1)S(1)}, u32[]{:S(2)}, u32[]{:S(2)}) async-start(bf16[256,4,128]{2,1,0:T(4,128)(2,1)} %bitcast.7), calls=%async_computation.3 | async-start | bytes 524288 | tf_op jit(solution)/shard_map/all_to_all | solution.py:261
  103.2 58.4 %all-gather.3.cloned.1.call-done.kv_ref = bf16[64,128,128]{2,1,0:T(8,128)(2,1)} async-done(((bf16[2,128,128]{2,1,0:T(8,128)(2,1)}), bf16[64,128,128]{2,1,0:T(8,128)(2,1)}) %all-gather.3.cloned.1.call-update) | async-done | bytes 2097168 | tf_op jit(solution)/shard_map/all_gather | solution.py:283
  161.5 1.1 copy-done.9
  162.6 1.6 copy-done.13
  164.2 1.7 shard_map.38
  165.8 0.8 copy-done.10
  166.7 6.7 %all-to-all-start.1 = ((bf16[8,272,128]{2,1,0:T(8,128)(2,1)}), bf16[8,272,128]{2,1,0:T(8,128)(2,1)}, u32[]{:S(2)}, u32[]{:S(2)}) async-start(bf16[8,272,128]{2,1,0:T(8,128)(2,1)} %copy-done.10), calls=%async_computation.1 | async-start | bytes 1114112 | tf_op jit(solution)/shard_map/all_to_all | solution.py:261
  173.4 5.0 %shard_map.40 = (bf16[8,128,128]{2,1,0:T(8,128)(2,1)S(1)}, f32[16,128,128]{2,1,0:T(8,128)S(1)}, f32[16,8,128]{2,1,0:T(8,128)S(1)}) custom-call(bf16[128,4096]{1,0:T(8,128)(2,1)S(1)} %copy-done.1, bf16[128,4096]{1,0:T(8,128)(2,1)S(1)} %copy-done.3, bf16[128,4096]{1,0:T(8,128)(2,1)S(1)} %copy-done.5), custom_call_target="tpu_custom_call" | custom-call | flops 201326592 | bytes 5242880 | tf_op jit(solution)/shard_map/pallas_call | solution.py:249
  178.4 1.0 copy-done.6
  179.4 0.7 copy-done.11
  180.1 3.1 %all-to-all-done.1.far_ref = bf16[8,272,128]{2,1,0:T(8,128)(2,1)} async-done(((bf16[8,272,128]{2,1,0:T(8,128)(2,1)}), bf16[8,272,128]{2,1,0:T(8,128)(2,1)}, u32[]{:S(2)}, u32[]{:S(2)}) %all-to-all-start.1) | async-done | bytes 557088 | tf_op jit(solution)/shard_map/all_to_all | solution.py:261
  183.2 1.2 copy-done.7
  184.4 0.9 copy-done.12
  185.4 2.4 %shard_map.41 = bf16[128,4096]{1,0:T(8,128)(2,1)} custom-call(bf16[8,272,128]{2,1,0:T(8,128)(2,1)} %all-to-all-done.1.far_ref, bf16[1024,128]{1,0:T(8,128)(2,1)S(1)} %bitcast.10, bf16[8,128,128]{2,1,0:T(8,128)(2,1)S(1)} %copy-done.12, f32[16,128,128]{2,1,0:T(8,128)S(1)} %copy-done.7, f32[16,8,128]{2,1,0:T(8,128)S(1)} %get-tuple-element.14.stat_ref), custom_call_target="tpu_custom_call" | custom-call | flops 33554432 | bytes 4194304 | tf_op jit(solution)/shard_map/pallas_call | solution.py:249
  (26 shorter events, 0.2 us)
Async XLA Ops:
  6.5 71.9 %all-gather.5.cloned.1.call-start = ((), (), s32[]{:S(2)}) async-start(), calls=%async_computation.5 | async-start | bytes 2359296 | tf_op jit(solution)/shard_map/all_gather | solution.py:294
  6.5 1.2 copy-start
  7.8 1.2 copy-start.2
  9.0 1.2 copy-start.4
  57.6 104.0 %all-gather.3.cloned.1.call-start = ((), (), s32[]{:S(2)}) async-start(), calls=%async_computation.4 | async-start | bytes 2162688 | tf_op jit(solution)/shard_map/all_gather | solution.py:283
  74.0 0.8 copy-start.8
  78.4 1.4 copy-start.14
  92.1 74.6 %all-to-all-start.3 = ((bf16[256,4,128]{2,1,0:T(4,128)(2,1)}), bf16[256,4,128]{2,1,0:T(4,128)(2,1)S(1)}, u32[]{:S(2)}, u32[]{:S(2)}) async-start(bf16[256,4,128]{2,1,0:T(4,128)(2,1)} %bitcast.7), calls=%async_computation.3 | async-start | bytes 524288 | tf_op jit(solution)/shard_map/all_to_all | solution.py:261
  161.5 1.1 copy-start.9
  162.6 1.6 copy-start.13
  164.2 9.2 %copy-start.1 = (bf16[128,4096]{1,0:T(8,128)(2,1)S(1)}, bf16[128,4096]{1,0:T(8,128)(2,1)}, u32[]{:S(2)}) copy-start(bf16[128,4096]{1,0:T(8,128)(2,1)} %q_ref.3) | copy-start | bytes 3145732
  164.2 9.2 %copy-start.3 = (bf16[128,4096]{1,0:T(8,128)(2,1)S(1)}, bf16[128,4096]{1,0:T(8,128)(2,1)}, u32[]{:S(2)}) copy-start(bf16[128,4096]{1,0:T(8,128)(2,1)} %k_ref.3) | copy-start | bytes 3145732
  164.2 9.2 %copy-start.5 = (bf16[128,4096]{1,0:T(8,128)(2,1)S(1)}, bf16[128,4096]{1,0:T(8,128)(2,1)}, u32[]{:S(2)}) copy-start(bf16[128,4096]{1,0:T(8,128)(2,1)} %v_ref.3) | copy-start | bytes 3145732
  165.8 0.8 copy-start.10
  166.7 16.5 %all-to-all-start.1 = ((bf16[8,272,128]{2,1,0:T(8,128)(2,1)}), bf16[8,272,128]{2,1,0:T(8,128)(2,1)}, u32[]{:S(2)}, u32[]{:S(2)}) async-start(bf16[8,272,128]{2,1,0:T(8,128)(2,1)} %copy-done.10), calls=%async_computation.1 | async-start | bytes 1114112 | tf_op jit(solution)/shard_map/all_to_all | solution.py:261
  178.4 1.0 copy-start.6
  179.4 0.7 copy-start.11
  183.2 1.2 copy-start.7
  184.4 0.9 copy-start.12
Sparse Core Ops, SparseCore 0:
  57.7 13.6 all-gather.4
  78.5 82.9 all-gather.2
where the time goes:
time: 197 us; the launch traced here: 195 us
  blocking collectives  66.2 us (34%)
  waiting for transfers between devices  61.5 us (31%)
  Pallas kernels  22.4 us (11%)
  starting transfers between devices  17.8 us (9%)
  between operations  13.5 us (7%)
  local copies, waits for them, and re-layouts  13.2 us (7%)
    all_to_all x2, blocking collectives, exchange(): return lax.all_to_all(array, axes, split_axis=0, concat_axis=0, tiled=True)  62.7 us
    all_gather x1, waiting for transfers between devices, body(): summary = lax.all_gather(summary, ('z', 'u'), axis=0, tiled=True)  58.4 us
    pallas_call x5, Pallas kernels, call(): pl.pallas_call(kernel, out_shape=shapes if many else shapes[0], in_specs=...  22.4 us
    all_to_all x2, starting transfers between devices, exchange(): return lax.all_to_all(array, axes, split_axis=0, concat_axis=0, tiled=True)  17.8 us
    unnamed x30, local copies, waits for them, and re-layouts  13.2 us
  transfers between devices with their start and end apart: 4, of which 2 were waited for; matrix products, arithmetic and copies ran while one was open for 0% of the time, Pallas kernels for 10%

commit v1 on v0

v1 whole, which is shorter than its diff:
```python
import math

import jax
import jax.numpy as jnp
from jax import lax
from jax.experimental import pallas as pl
from jax.experimental.pallas import tpu as pltpu
from jax.sharding import Mesh
from jax.sharding import PartitionSpec as P

HD = 128
STRIDE = 32
QUADS = 8
POS = 128
ROWS = 4
LOW = -1e30
SCALE = math.log2(math.e) / math.sqrt(HD)
SUM_ROWS = 16
PAY = POS + SUM_ROWS
HEADS = 16
PAIR = HEADS * POS

f32 = jnp.float32
bf16 = jnp.bfloat16


def dot_t(a, b):
    return lax.dot_general(a, b, (((1,), (1,)), ((), ())), preferred_element_type=f32)


def dot_tl(a, b):
    return lax.dot_general(a, b, (((0,), (0,)), ((), ())), preferred_element_type=f32)


def dot(a, b):
    return lax.dot_general(a, b, (((1,), (0,)), ((), ())), preferred_element_type=f32)


def iota(shape, dim):
    return lax.broadcasted_iota(jnp.int32, shape, dim)


def one_hot(rows, cols, source):
    row = iota((rows, cols), 0)
    col = iota((rows, cols), 1)
    return jnp.where(source(row) == col, 1.0, 0.0).astype(bf16)


def div12(o):
    return (o * 5462) >> 16


def head(ref, quad, kind):
    start = (quad * 4 + kind) * HD
    return ref[:, start : start + HD]


def pack_far_kernel(q_ref, k_ref, v_ref, query_ref, sum_ref):
    pick = one_hot(
        8, 2 * POS, lambda o: (o >> 2) * POS + (o & 3) * STRIDE + STRIDE - 1
    )
    for g in range(HEADS):
        quad, kind = g // 2, 2 + g % 2
        query_ref[g] = head(q_ref, quad, kind)
        stack = jnp.concatenate([head(k_ref, quad, kind), head(v_ref, quad, kind)], axis=0)
        rows = dot(pick, stack).astype(bf16)
        for t in range(sum_ref.shape[0] // HEADS):
            sum_ref[t * HEADS + g] = rows


def pack_column_kernel(after_ref, q_ref, k_ref, v_ref, item_ref):
    def source(o):
        col = div12(o)
        rest = o - 12 * col
        return (rest >> 2) * POS + (rest & 3) * STRIDE + col

    perm = one_hot(384, 384, source)
    for quad in range(QUADS):
        stack = jnp.concatenate(
            [head(q_ref, quad, 1), head(k_ref, quad, 1), head(v_ref, quad, 1)], axis=0
        )
        item_ref[quad] = dot(perm, stack).astype(bf16)


def rows_kernel(q_ref, k_ref, v_ref, row_ref, part_ref, max_ref, sum_ref):
    pos = iota((POS, POS), 0)
    key = iota((POS, POS), 1)
    visible = jnp.logical_and((key >> 5) == (pos >> 5), key <= pos)
    tops = jnp.zeros((POS, POS), f32)
    sums = jnp.ones((POS, POS), f32)
    for quad in range(QUADS):
        for kind in (0, 2, 3):
            s = dot_t(head(q_ref, quad, kind), head(k_ref, quad, kind)) * SCALE
            s = jnp.where(visible, s, LOW)
            m = jnp.max(s, axis=1, keepdims=True)
            p = jnp.where(visible, jnp.exp2(s - m), 0.0)
            total = jnp.sum(p, axis=1, keepdims=True)
            acc = dot(p.astype(bf16), head(v_ref, quad, kind))
            if kind == 0:
                row_ref[quad] = (acc / total).astype(bf16)
            else:
                slot = quad * 2 + kind - 2
                part_ref[slot] = acc
                tops = jnp.where(key == slot, m, tops)
                sums = jnp.where(key == slot, total, sums)
    max_ref[...] = tops
    sum_ref[...] = sums


def column_kernel(core_ref, own_ref, other_ref, out_ref, q_scr, k_scr, v_scr):
    core = core_ref[0]

    def source(o):
        within = o & 31
        return (within >> 2) * 12 + (o >> 5) * 4 + (within & 3)

    split = one_hot(96, 96, source)
    split_kv = one_hot(64, 96, lambda o: source(o + 32))
    for g in range(32):
        at = slice(g * 32, (g + 1) * 32)
        y = dot(split, own_ref[g * 96 : (g + 1) * 96, :]).astype(bf16)
        q_scr[at, :] = y[0:32]
        k_scr[0, at, :] = y[32:64]
        v_scr[0, at, :] = y[64:96]
        y = dot(split_kv, other_ref[g * 96 : (g + 1) * 96, :]).astype(bf16)
        k_scr[1, at, :] = y[0:32]
        v_scr[1, at, :] = y[32:64]

    block = 256
    jq = iota((block, block), 0)
    jk = iota((block, block), 1)
    visible = (jk <= jq, (jk >> 4) < (jq >> 4) + core)
    for qb in range(1024 // block):
        q = q_scr[qb * block : (qb + 1) * block, :]
        pieces = []
        top = None
        for kb in range(qb + 1):
            for c in range(2):
                s = dot_t(q, k_scr[c, kb * block : (kb + 1) * block, :]) * SCALE
                if kb == qb:
                    s = jnp.where(visible[c], s, LOW)
                fold = jnp.maximum(s[:, :128], s[:, 128:])
                top = fold if top is None else jnp.maximum(top, fold)
                pieces.append((kb, c, s))
        m = jnp.max(top, axis=1, keepdims=True)
        total = jnp.zeros((block, 128), f32)
        acc = jnp.zeros((block, HD), f32)
        for kb, c, s in pieces:
            p = jnp.exp2(s - m)
            total = total + (p[:, :128] + p[:, 128:])
            acc = acc + dot(p.astype(bf16), v_scr[c, kb * block : (kb + 1) * block, :])
        total = jnp.sum(total, axis=1, keepdims=True)
        out_ref[qb * block : (qb + 1) * block, :] = (acc / total).astype(bf16)


FAR_Q = 512
FAR_K = 1024


def far_kernel(pair_ref, q_ref, kv_ref, out_ref, s_scr):
    pair = pair_ref[0]
    row_ids = PAIR // STRIDE
    last = (pair * row_ids) // FAR_K
    lane = iota((POS, 128), 1)
    eye = one_hot(SUM_ROWS, 128, lambda o: o)
    per = FAR_Q // POS
    planes = FAR_K // 256

    def piece(i, j):
        return jnp.concatenate([kv_ref[i * planes + t, j] for t in range(planes)], axis=0)

    def fold(x, op):
        r = x[:, :128]
        for t in range(1, FAR_K // 128):
            r = op(r, x[:, t * 128 : (t + 1) * 128])
        return r

    def block(b, unused):
        q = q_ref[pl.ds(b * per, per)].reshape(FAR_Q, HD)

        def score(i, top):
            s = dot_t(q, piece(i, 0)) * SCALE
            s_scr[i] = s
            return jnp.maximum(top, fold(s, jnp.maximum))

        top = lax.fori_loop(0, last, score, jnp.full((FAR_Q, 128), LOW, f32))
        s = dot_t(q, piece(last, 0)) * SCALE
        row_k = last * FAR_K + iota((FAR_Q, FAR_K), 1)
        row_q = pair * row_ids + ((b * FAR_Q + iota((FAR_Q, FAR_K), 0)) >> 5)
        s = jnp.where(row_k < row_q, s, LOW)
        s_scr[last] = s
        top = jnp.maximum(top, fold(s, jnp.maximum))
        m = jnp.max(top, axis=1, keepdims=True)

        def weigh(i, carried):
            total, acc = carried
            p = jnp.exp2(s_scr[i] - m)
            return (
                total + fold(p, jnp.add),
                acc + dot(p.astype(bf16), piece(i, 1)),
            )

        total, acc = lax.fori_loop(
            0,
            last + 1,
            weigh,
            (jnp.zeros((FAR_Q, 128), f32), jnp.zeros((FAR_Q, HD), f32)),
        )
        total = jnp.sum(total, axis=1, keepdims=True)
        out = (acc / total).astype(bf16)
        lse = jnp.where(m > 0.5 * LOW, m + jnp.log2(total), LOW)
        high = lse.astype(bf16).astype(f32)
        left = lse - high
        mid = left.astype(bf16).astype(f32)
        low = left - mid
        for e in range(per):
            at = slice(e * POS, (e + 1) * POS)
            terms = jnp.where(
                lane == 0,
                high[at],
                jnp.where(lane == 1, mid[at], jnp.where(lane == 2, low[at], 0.0)),
            ).astype(bf16)
            out_ref[b * per + e, :POS, :] = out[at]
            out_ref[b * per + e, POS:, :] = dot_t(eye, terms).astype(bf16)
        return unused

    lax.fori_loop(0, PAIR // FAR_Q, block, 0)


def final_kernel(far_ref, col_ref, row_ref, part_ref, max_ref, sum_ref, out_ref):
    back = one_hot(POS, POS, lambda o: (o & 31) * 4 + (o >> 5))
    row = iota((HEADS * SUM_ROWS, 128), 0)
    lane = iota((HEADS * SUM_ROWS, 128), 1)
    pick = jnp.where(
        jnp.logical_and((row >> 4) == lane, (row & 15) < 3), 1.0, 0.0
    ).astype(bf16)
    terms = jnp.concatenate([far_ref[g, POS:, :] for g in range(HEADS)], axis=0)
    lse = dot_tl(terms, pick)
    top = jnp.maximum(max_ref[...], lse)
    own = jnp.exp2(max_ref[...] - top)
    far = jnp.exp2(lse - top)
    scale = 1.0 / (sum_ref[...] * own + far)
    own = own * scale
    far = far * scale
    for quad in range(QUADS):
        base = quad * 4 * HD
        out_ref[:, base : base + HD] = row_ref[quad]
        out_ref[:, base + HD : base + 2 * HD] = dot(
            back, col_ref[quad * POS : (quad + 1) * POS, :]
        ).astype(bf16)
        for h in range(2):
            g = quad * 2 + h
            merged = (
                part_ref[g] * own[:, g : g + 1]
                + far_ref[g, :POS, :].astype(f32) * far[:, g : g + 1]
            )
            start = base + (2 + h) * HD
            out_ref[:, start : start + HD] = merged.astype(bf16)


def call(kernel, outs, args, scalars=0, scratch=(), flops=0, moved=0, exps=0, mib=16, unread=0):
    vmem = pl.BlockSpec(memory_space=pltpu.VMEM)
    smem = pl.BlockSpec(memory_space=pltpu.SMEM)
    hbm = pl.BlockSpec(memory_space=pl.ANY)
    shapes = [jax.ShapeDtypeStruct(s, d) for s, d in outs]
    many = len(shapes) > 1
    specs = [smem] * scalars + [hbm] * unread
    return pl.pallas_call(
        kernel,
        out_shape=shapes if many else shapes[0],
        in_specs=specs + [vmem] * (len(args) - len(specs)),
        out_specs=[vmem] * len(shapes) if many else vmem,
        scratch_shapes=list(scratch),
        compiler_params=pltpu.CompilerParams(vmem_limit_bytes=mib * 1024 * 1024),
        cost_estimate=pl.CostEstimate(flops=flops, bytes_accessed=moved, transcendentals=exps),
    )(*args)


def exchange(array, axes):
    return lax.all_to_all(array, axes, split_axis=0, concat_axis=0, tiled=True)


def body(queries, keys, values):
    heads_at = ("w", "c", "x")
    plane = ("u", "v", "w", "c", "x")
    wide = ("z", "u", "v", "w", "x")
    mib = 1 << 20
    heads, summary = call(
        pack_far_kernel,
        [((HEADS, POS, HD), bf16), ((64, 8, HD), bf16)],
        (queries, keys, values),
        flops=2 * 16 * 16 * 256 * 128,
        moved=4 * mib,
    )
    summary = exchange(summary, plane)
    summary = summary.reshape(64, 2, ROWS, HD).transpose(1, 0, 2, 3).reshape(1, 2, 256, HD)
    items = call(
        pack_column_kernel,
        [((QUADS, 384, HD), bf16)],
        (summary, queries, keys, values),
        unread=1,
        flops=2 * 8 * 384 * 384 * 128,
        moved=4 * mib,
    )
    summary = lax.all_gather(summary, "z", axis=0, tiled=True)
    items = exchange(items.reshape(768, ROWS, HD), wide).reshape(3072, HD)
    heads = exchange(heads, heads_at)
    other = lax.ppermute(items, "c", [(0, 1), (1, 0)])
    core = lax.axis_index("c").astype(jnp.int32).reshape(1)
    column = call(
        column_kernel,
        [((1024, HD), bf16)],
        (core, items, other),
        scalars=1,
        scratch=[
            pltpu.VMEM((1024, HD), bf16),
            pltpu.VMEM((2, 1024, HD), bf16),
            pltpu.VMEM((2, 1024, HD), bf16),
        ],
        flops=4 * 1024 * 1280 * 128,
        moved=2 * mib,
        exps=1024 * 1280,
    )
    column = exchange(column.reshape(256, ROWS, HD), wide).reshape(1024, HD)
    row_out, part, tops, sums = call(
        rows_kernel,
        [
            ((QUADS, POS, HD), bf16),
            ((HEADS, POS, HD), f32),
            ((POS, 128), f32),
            ((POS, 128), f32),
        ],
        (queries, keys, values),
        flops=24 * 4 * 128 * 128 * 128,
        moved=5 * mib,
        exps=24 * 128 * 128,
    )

    pair = lax.axis_index(("z", "u", "v")).astype(jnp.int32).reshape(1)
    far = call(
        far_kernel,
        [((HEADS, PAY, HD), bf16)],
        (pair, heads, summary),
        scalars=1,
        scratch=[pltpu.VMEM((2048 // FAR_K, FAR_Q, FAR_K), f32)],
        flops=8 * 1024 * 2048 * 128,
        moved=3 * mib,
        exps=2 * 1024 * 2048,
        mib=24,
    )
    far = exchange(far, heads_at)
    return call(
        final_kernel,
        [((POS, QUADS * 4 * HD), bf16)],
        (far, column, row_out, part, tops, sums),
        flops=2 * 8 * 128 * 128 * 128,
        moved=4 * mib,
    )


def solution(mesh):
    fine = Mesh(mesh.devices.reshape(4, 8, 2, 2, 2, 2), ("x", "z", "u", "v", "w", "c"))
    spec = P(("z", "u", "v", "w", "c", "x"), None)
    return jax.shard_map(
        body, mesh=fine, in_specs=(spec, spec, spec), out_specs=spec, check_vma=False
    )
```

time: 197 us -> 147 us (0.75)
  blocking collectives: 66.2 us -> 21.5 us
  waiting for transfers between devices: 61.5 us -> 33.2 us
  starting transfers between devices: 17.8 us -> 44.9 us
    all_gather x2 -> x1, waiting for transfers between devices: 58.4 us -> 0.02 us  [body(): summary = lax.all_gather(summary, 'z', axis=0, tiled=True)]
    all_to_all x2 -> x1, blocking collectives: 62.7 us -> 21.5 us  [exchange(): return lax.all_to_all(array, axes, split_axis=0, concat_axis=0, tiled=True)]
    all_to_all x2 -> x4, waiting for transfers between devices: 3.12 us -> 30 us  [exchange(): return lax.all_to_all(array, axes, split_axis=0, concat_axis=0, tiled=True)]
    all_to_all x2 -> x4, starting transfers between devices: 17.8 us -> 42.8 us  [exchange(): return lax.all_to_all(array, axes, split_axis=0, concat_axis=0, tiled=True)]
    all_gather x1 -> x0, blocking collectives: 3.55 us -> none  [body(): summary = lax.all_gather(summary, 'w', axis=0, tiled=True)]
    ppermute x0 -> x1, waiting for transfers between devices: none -> 2.44 us  [body(): other = lax.ppermute(items, 'c', [(0, 1), (1, 0)])]
    ppermute x0 -> x1, starting transfers between devices: none -> 2.06 us  [body(): other = lax.ppermute(items, 'c', [(0, 1), (1, 0)])]
    unnamed x30 -> x32, local copies, waits for them, and re-layouts: 13.2 us -> 12 us
  transfers between devices with their start and end apart: 4 -> 6, of which waited for: 2 -> 5; matrix products, arithmetic and copies ran while one was open for 0% -> 0% of each run, Pallas kernels for 10% -> 12%
where the time goes in v1:
time: 147 us; the launch traced here: 146 us
  starting transfers between devices  44.9 us (31%)
  waiting for transfers between devices  33.2 us (23%)
  blocking collectives  21.5 us (15%)
  Pallas kernels  21.3 us (14%)
  between operations  13.6 us (9%)
  local copies, waits for them, and re-layouts  12 us (8%)
    all_to_all x4, starting transfers between devices, exchange(): return lax.all_to_all(array, axes, split_axis=0, concat_axis=0, tiled=True)  42.8 us
    all_to_all x4, waiting for transfers between devices, exchange(): return lax.all_to_all(array, axes, split_axis=0, concat_axis=0, tiled=True)  30 us
    all_to_all x1, blocking collectives, exchange(): return lax.all_to_all(array, axes, split_axis=0, concat_axis=0, tiled=True)  21.5 us
    pallas_call x6, Pallas kernels, call(): pl.pallas_call(kernel, out_shape=shapes if many else shapes[0], in_specs=...  21.3 us
    unnamed x32, local copies, waits for them, and re-layouts  12 us
  transfers between devices with their start and end apart: 6, of which 5 were waited for; matrix products, arithmetic and copies ran while one was open for 0% of the time, Pallas kernels for 12%

profile of v1, /device:TPU:1, one launch (start us, length us, event | category | flops | bytes accessed | tf_op | source)
XLA Modules:
  0.0 146.4 jit_solution(11584439237287006571)
XLA Ops:
  6.5 1.2 copy-done
  7.8 1.2 copy-done.2
  9.0 1.2 copy-done.4
  10.5 0.8 copy-done.11
  11.3 21.5 %all_to_all.25 = bf16[64,8,128]{2,1,0:T(8,128)(2,1)S(1)} all-to-all(bf16[64,8,128]{2,1,0:T(8,128)(2,1)S(1)} %get-tuple-element.12), channel_id=1, replica_groups=mesh['x'=4,'z'=8,'u'=2,'v'=2,'w'=2,'c'=2] {'u','v','w','c','x'}, dimensions={0} | all-to-all | bytes 262144 | tf_op jit(solution)/shard_map/all_to_all | solution.py:280
  33.7 0.9 copy-done.6
  34.6 17.8 %all-to-all-start.3 = ((bf16[768,4,128]{2,1,0:T(4,128)(2,1)}), bf16[768,4,128]{2,1,0:T(4,128)(2,1)}, u32[]{:S(2)}, u32[]{:S(2)}) async-start(bf16[768,4,128]{2,1,0:T(4,128)(2,1)} %bitcast.10), calls=%async_computation.3 | async-start | bytes 1572864 | tf_op jit(solution)/shard_map/all_to_all | solution.py:280
  53.1 21.7 %all-to-all-done.3 = bf16[768,4,128]{2,1,0:T(4,128)(2,1)} async-done(((bf16[768,4,128]{2,1,0:T(4,128)(2,1)}), bf16[768,4,128]{2,1,0:T(4,128)(2,1)}, u32[]{:S(2)}, u32[]{:S(2)}) %all-to-all-start.3) | async-done | bytes 786464 | tf_op jit(solution)/shard_map/all_to_all | solution.py:280
  74.9 6.9 %all-to-all-start = ((bf16[16,128,128]{2,1,0:T(8,128)(2,1)}), bf16[16,128,128]{2,1,0:T(8,128)(2,1)}, u32[]{:S(2)}, u32[]{:S(2)}) async-start(bf16[16,128,128]{2,1,0:T(8,128)(2,1)} %copy-done.11), calls=%async_computation | async-start | bytes 1048576 | tf_op jit(solution)/shard_map/all_to_all | solution.py:280
  81.8 2.1 %collective-permute-start = (bf16[3072,128]{1,0:T(8,128)(2,1)}, bf16[3072,128]{1,0:T(8,128)(2,1)}, u32[]{:S(2)}, u32[]{:S(2)}) collective-permute-start(bf16[3072,128]{1,0:T(8,128)(2,1)} %bitcast.7.own_ref), channel_id=1, source_target_pairs={{0,1},{1,0},{2,3},{3,2},{4,5},{5,4},{6,7},{7,6},{8,9},{9,8},{10,11... | collective-permute-start | bytes 2359304 | tf_op jit(solution)/shard_map/ppermute | solution.py:308
  83.8 2.4 %collective-permute-done.other_ref = bf16[3072,128]{1,0:T(8,128)(2,1)} collective-permute-done((bf16[3072,128]{1,0:T(8,128)(2,1)}, bf16[3072,128]{1,0:T(8,128)(2,1)}, u32[]{:S(2)}, u32[]{:S(2)}) %collective-permute-start) | collective-permute-done | bytes 786464 | tf_op jit(solution)/shard_map/ppermute | solution.py:308
  86.3 4.4 %shard_map.40 = bf16[1024,128]{1,0:T(8,128)(2,1)S(1)} custom-call(s32[1]{0:T(128)} %bitcast.4.core_ref, bf16[3072,128]{1,0:T(8,128)(2,1)} %bitcast.7.own_ref, bf16[3072,128]{1,0:T(8,128)(2,1)} %collective-permute-done.other_ref), custom_call_target="tpu_custom_call" | custom-call | flops 671088640 | bytes 2097152 | tf_op jit(solution)/shard_map/pallas_call | solution.py:268
  92.1 11.4 %all-to-all-start.4 = ((bf16[256,4,128]{2,1,0:T(4,128)(2,1)}), bf16[256,4,128]{2,1,0:T(4,128)(2,1)S(1)}, u32[]{:S(2)}, u32[]{:S(2)}) async-start(bf16[256,4,128]{2,1,0:T(4,128)(2,1)} %bitcast.14), calls=%async_computation.4 | async-start | bytes 524288 | tf_op jit(solution)/shard_map/all_to_all | solution.py:280
  103.5 1.2 copy-done.15
  104.7 7.0 %shard_map.38 = bf16[16,144,128]{2,1,0:T(8,128)(2,1)S(1)} custom-call(s32[1]{0:T(128)} %bitcast.pair_ref, bf16[16,128,128]{2,1,0:T(8,128)(2,1)} %all-to-all-done.q_ref, bf16[8,2,256,128]{3,2,1,0:T(8,128)(2,1)S(1)} %copy-done.15), custom_call_target="tpu_custom_call" | custom-call | flops 2147483648 | bytes 3145728 | tf_op jit(solution)/shard_map/pallas_call | solution.py:268
  111.8 0.8 copy-done.10
  112.6 4.1 %all-to-all-done.4 = bf16[256,4,128]{2,1,0:T(4,128)(2,1)S(1)} async-done(((bf16[256,4,128]{2,1,0:T(4,128)(2,1)}), bf16[256,4,128]{2,1,0:T(4,128)(2,1)S(1)}, u32[]{:S(2)}, u32[]{:S(2)}) %all-to-all-start.4) | async-done | bytes 262176 | tf_op jit(solution)/shard_map/all_to_all | solution.py:280
  116.7 6.7 %all-to-all-start.2 = ((bf16[16,144,128]{2,1,0:T(8,128)(2,1)}), bf16[16,144,128]{2,1,0:T(8,128)(2,1)}, u32[]{:S(2)}, u32[]{:S(2)}) async-start(bf16[16,144,128]{2,1,0:T(8,128)(2,1)} %copy-done.10), calls=%async_computation.2 | async-start | bytes 1179648 | tf_op jit(solution)/shard_map/all_to_all | solution.py:280
  123.4 5.8 %shard_map.41 = (bf16[8,128,128]{2,1,0:T(8,128)(2,1)S(1)}, f32[16,128,128]{2,1,0:T(8,128)S(1)}, f32[128,128]{1,0:T(8,128)S(1)}, f32[128,128]{1,0:T(8,128)S(1)}) custom-call(bf16[128,4096]{1,0:T(8,128)(2,1)S(1)} %copy-done.1, bf16[128,4096]{1,0:T(8,128)(2,1)S(1)} %copy-done.3, bf16[128,4096]{1,0:T(8,128)(2,1)S(1)} %copy-done.5), custom_call_target="tpu_custom_call" | custom-call | flops 201326592 | bytes 5242880 | tf_op jit(solution)/shard_map/pallas_call | solution.py:268
  129.3 1.0 copy-done.8
  131.0 3.5 %all-to-all-done.2.far_ref = bf16[16,144,128]{2,1,0:T(8,128)(2,1)} async-done(((bf16[16,144,128]{2,1,0:T(8,128)(2,1)}), bf16[16,144,128]{2,1,0:T(8,128)(2,1)}, u32[]{:S(2)}, u32[]{:S(2)}) %all-to-all-start.2) | async-done | bytes 589856 | tf_op jit(solution)/shard_map/all_to_all | solution.py:280
  134.5 1.2 copy-done.9
  135.7 0.9 copy-done.13
  136.6 2.9 %shard_map.42 = bf16[128,4096]{1,0:T(8,128)(2,1)} custom-call(bf16[16,144,128]{2,1,0:T(8,128)(2,1)} %all-to-all-done.2.far_ref, bf16[1024,128]{1,0:T(8,128)(2,1)S(1)} %bitcast.13, bf16[8,128,128]{2,1,0:T(8,128)(2,1)S(1)} %copy-done.13, f32[16,128,128]{2,1,0:T(8,128)S(1)} %copy-done.9, f32[128,128]{1,0:T(8,128)S(1)} %get-tuple-element.15.max_ref, ...), custom_call_target="tpu_custom_call" | custom-call | flops 33554432 | bytes 4194304 | tf_op jit(solution)/shard_map/pallas_call | solution.py:268
  (29 shorter events, 4.0 us)
Async XLA Ops:
  6.5 1.2 copy-start
  7.8 1.2 copy-start.2
  9.0 1.2 copy-start.4
  10.2 22.7 %copy-start.1 = (bf16[128,4096]{1,0:T(8,128)(2,1)S(1)}, bf16[128,4096]{1,0:T(8,128)(2,1)}, u32[]{:S(2)}) copy-start(bf16[128,4096]{1,0:T(8,128)(2,1)} %q_ref.5) | copy-start | bytes 3145732
  10.2 22.7 %copy-start.3 = (bf16[128,4096]{1,0:T(8,128)(2,1)S(1)}, bf16[128,4096]{1,0:T(8,128)(2,1)}, u32[]{:S(2)}) copy-start(bf16[128,4096]{1,0:T(8,128)(2,1)} %k_ref.5) | copy-start | bytes 3145732
  10.2 22.7 %copy-start.5 = (bf16[128,4096]{1,0:T(8,128)(2,1)S(1)}, bf16[128,4096]{1,0:T(8,128)(2,1)}, u32[]{:S(2)}) copy-start(bf16[128,4096]{1,0:T(8,128)(2,1)} %v_ref.5) | copy-start | bytes 3145732
  10.5 0.8 copy-start.11
  32.9 0.9 copy-start.7
  33.7 0.9 copy-start.6
  34.6 40.3 %all-to-all-start.3 = ((bf16[768,4,128]{2,1,0:T(4,128)(2,1)}), bf16[768,4,128]{2,1,0:T(4,128)(2,1)}, u32[]{:S(2)}, u32[]{:S(2)}) async-start(bf16[768,4,128]{2,1,0:T(4,128)(2,1)} %bitcast.10), calls=%async_computation.3 | async-start | bytes 1572864 | tf_op jit(solution)/shard_map/all_to_all | solution.py:280
  52.4 51.1 %all-gather.2.cloned.1.call-start = ((), (), s32[]{:S(2)}) async-start(), calls=%async_computation.5 | async-start | bytes 1179648 | tf_op jit(solution)/shard_map/all_gather | solution.py:305
  74.9 17.2 %all-to-all-start = ((bf16[16,128,128]{2,1,0:T(8,128)(2,1)}), bf16[16,128,128]{2,1,0:T(8,128)(2,1)}, u32[]{:S(2)}, u32[]{:S(2)}) async-start(bf16[16,128,128]{2,1,0:T(8,128)(2,1)} %copy-done.11), calls=%async_computation | async-start | bytes 1048576 | tf_op jit(solution)/shard_map/all_to_all | solution.py:280
  81.8 4.5 %collective-permute-start = (bf16[3072,128]{1,0:T(8,128)(2,1)}, bf16[3072,128]{1,0:T(8,128)(2,1)}, u32[]{:S(2)}, u32[]{:S(2)}) collective-permute-start(bf16[3072,128]{1,0:T(8,128)(2,1)} %bitcast.7.own_ref), channel_id=1, source_target_pairs={{0,1},{1,0},{2,3},{3,2},{4,5},{5,4},{6,7},{7,6},{8,9},{9,8},{10,11... | collective-permute-start | bytes 2359304 | tf_op jit(solution)/shard_map/ppermute | solution.py:308
  90.7 0.7 copy-start.14
  92.1 24.6 %all-to-all-start.4 = ((bf16[256,4,128]{2,1,0:T(4,128)(2,1)}), bf16[256,4,128]{2,1,0:T(4,128)(2,1)S(1)}, u32[]{:S(2)}, u32[]{:S(2)}) async-start(bf16[256,4,128]{2,1,0:T(4,128)(2,1)} %bitcast.14), calls=%async_computation.4 | async-start | bytes 524288 | tf_op jit(solution)/shard_map/all_to_all | solution.py:280
  103.5 1.2 copy-start.15
  111.8 0.8 copy-start.10
  116.7 17.8 %all-to-all-start.2 = ((bf16[16,144,128]{2,1,0:T(8,128)(2,1)}), bf16[16,144,128]{2,1,0:T(8,128)(2,1)}, u32[]{:S(2)}, u32[]{:S(2)}) async-start(bf16[16,144,128]{2,1,0:T(8,128)(2,1)} %copy-done.10), calls=%async_computation.2 | async-start | bytes 1179648 | tf_op jit(solution)/shard_map/all_to_all | solution.py:280
  129.3 1.0 copy-start.8
  130.3 0.7 copy-start.12
  134.5 1.2 copy-start.9
  135.7 0.9 copy-start.13
Sparse Core Ops, SparseCore 0:
  55.3 37.8 all-gather.1

commit v2 on v1

--- a/solution.py
+++ b/solution.py
@@ -55,31 +55,49 @@
     return ref[:, start : start + HD]
 
 
-def pack_far_kernel(q_ref, k_ref, v_ref, query_ref, sum_ref):
-    pick = one_hot(
-        8, 2 * POS, lambda o: (o >> 2) * POS + (o & 3) * STRIDE + STRIDE - 1
-    )
+def pack_summary_kernel(k_ref, v_ref, sum_ref, buf, sems):
+    moves = []
+    for a, ref in enumerate((k_ref, v_ref)):
+        for r in range(ROWS):
+            move = pltpu.make_async_copy(
+                ref.at[pl.ds(r * STRIDE + 16, 16), :],
+                buf.at[pl.ds((a * ROWS + r) * 16, 16), :],
+                sems.at[a * ROWS + r],
+            )
+            move.start()
+            moves.append(move)
+    pick = one_hot(8, 128, lambda o: o * 16 + 15)
+    for move in moves:
+        move.wait()
     for g in range(HEADS):
-        quad, kind = g // 2, 2 + g % 2
-        query_ref[g] = head(q_ref, quad, kind)
-        stack = jnp.concatenate([head(k_ref, quad, kind), head(v_ref, quad, kind)], axis=0)
-        rows = dot(pick, stack).astype(bf16)
+        rows = dot(pick, head(buf, g // 2, 2 + g % 2)).astype(bf16)
         for t in range(sum_ref.shape[0] // HEADS):
             sum_ref[t * HEADS + g] = rows
 
 
-def pack_column_kernel(after_ref, q_ref, k_ref, v_ref, item_ref):
+def pack_kernel(after_ref, q_ref, k_ref, v_ref, item_ref, query_ref, items, heads, sems):
     def source(o):
         col = div12(o)
         rest = o - 12 * col
         return (rest >> 2) * POS + (rest & 3) * STRIDE + col
 
     perm = one_hot(384, 384, source)
+    moves = []
     for quad in range(QUADS):
         stack = jnp.concatenate(
             [head(q_ref, quad, 1), head(k_ref, quad, 1), head(v_ref, quad, 1)], axis=0
         )
-        item_ref[quad] = dot(perm, stack).astype(bf16)
+        items[quad] = dot(perm, stack).astype(bf16)
+        move = pltpu.make_async_copy(items.at[quad], item_ref.at[quad], sems.at[quad])
+        move.start()
+        moves.append(move)
+    for g in range(HEADS):
+        heads[g] = head(q_ref, g // 2, 2 + g % 2)
+    move = pltpu.make_async_copy(heads, query_ref, sems.at[QUADS])
+    move.start()
+    moves.append(move)
+    for move in moves:
+        move.wait()
 
 
 def rows_kernel(q_ref, k_ref, v_ref, row_ref, part_ref, max_ref, sum_ref):
@@ -107,8 +125,14 @@
     sum_ref[...] = sums
 
 
-def column_kernel(core_ref, own_ref, other_ref, out_ref, q_scr, k_scr, v_scr):
+def column_kernel(
+    core_ref, own_hbm, other_hbm, out_hbm, own_ref, other_ref, out_scr, q_scr, k_scr, v_scr, sems
+):
     core = core_ref[0]
+    own_in = pltpu.make_async_copy(own_hbm, own_ref, sems.at[0])
+    other_in = pltpu.make_async_copy(other_hbm, other_ref, sems.at[1])
+    own_in.start()
+    other_in.start()
 
     def source(o):
         within = o & 31
@@ -116,12 +140,17 @@
 
     split = one_hot(96, 96, source)
     split_kv = one_hot(64, 96, lambda o: source(o + 32))
+    by_x = one_hot(POS, POS, lambda o: ((o >> 2) & 7) * 16 + (o >> 5) * 4 + (o & 3))
+    own_in.wait()
     for g in range(32):
         at = slice(g * 32, (g + 1) * 32)
         y = dot(split, own_ref[g * 96 : (g + 1) * 96, :]).astype(bf16)
         q_scr[at, :] = y[0:32]
         k_scr[0, at, :] = y[32:64]
         v_scr[0, at, :] = y[64:96]
+    other_in.wait()
+    for g in range(32):
+        at = slice(g * 32, (g + 1) * 32)
         y = dot(split_kv, other_ref[g * 96 : (g + 1) * 96, :]).astype(bf16)
         k_scr[1, at, :] = y[0:32]
         v_scr[1, at, :] = y[32:64]
@@ -130,6 +159,7 @@
     jq = iota((block, block), 0)
     jk = iota((block, block), 1)
     visible = (jk <= jq, (jk >> 4) < (jq >> 4) + core)
+    moves = []
     for qb in range(1024 // block):
         q = q_scr[qb * block : (qb + 1) * block, :]
         pieces = []
@@ -150,21 +180,46 @@
             total = total + (p[:, :128] + p[:, 128:])
             acc = acc + dot(p.astype(bf16), v_scr[c, kb * block : (kb + 1) * block, :])
         total = jnp.sum(total, axis=1, keepdims=True)
-        out_ref[qb * block : (qb + 1) * block, :] = (acc / total).astype(bf16)
+        out = (acc / total).astype(bf16)
+        for t in range(block // POS):
+            y = dot(by_x, out[t * POS : (t + 1) * POS]).astype(bf16)
+            at = (qb * block // POS + t) * STRIDE
+            for x in range(4):
+                out_scr[x, at : at + STRIDE, :] = y[x * STRIDE : (x + 1) * STRIDE]
+        at = pl.ds(qb * block // 4, block // 4)
+        move = pltpu.make_async_copy(out_scr.at[:, at, :], out_hbm.at[:, at, :], sems.at[2 + qb])
+        move.start()
+        moves.append(move)
+    for move in moves:
+        move.wait()
 
 
 FAR_Q = 512
 FAR_K = 1024
-
-
-def far_kernel(pair_ref, q_ref, kv_ref, out_ref, s_scr):
+FAR_BLOCKS = PAIR // FAR_Q
+
+
+def far_kernel(pair_ref, q_hbm, kv_hbm, out_hbm, q_ref, kv_ref, out_ref, s_scr, sems):
     pair = pair_ref[0]
+    ins = [
+        pltpu.make_async_copy(q_hbm, q_ref, sems.at[0]),
+        pltpu.make_async_copy(kv_hbm, kv_ref, sems.at[1]),
+    ]
+    for move in ins:
+        move.start()
     row_ids = PAIR // STRIDE
     last = (pair * row_ids) // FAR_K
     lane = iota((POS, 128), 1)
     eye = one_hot(SUM_ROWS, 128, lambda o: o)
     per = FAR_Q // POS
     planes = FAR_K // 256
+
+    for move in ins:
+        move.wait()
+
+    def send(b):
+        at = pl.ds(b * per, per)
+        return pltpu.make_async_copy(out_ref.at[at], out_hbm.at[at], sems.at[2 + b])
 
     def piece(i, j):
         return jnp.concatenate([kv_ref[i * planes + t, j] for t in range(planes)], axis=0)
@@ -222,18 +277,35 @@
             ).astype(bf16)
             out_ref[b * per + e, :POS, :] = out[at]
             out_ref[b * per + e, POS:, :] = dot_t(eye, terms).astype(bf16)
+        send(b).start()
         return unused
 
-    lax.fori_loop(0, PAIR // FAR_Q, block, 0)
-
-
-def final_kernel(far_ref, col_ref, row_ref, part_ref, max_ref, sum_ref, out_ref):
-    back = one_hot(POS, POS, lambda o: (o & 31) * 4 + (o >> 5))
+    lax.fori_loop(0, FAR_BLOCKS, block, 0)
+    for b in range(FAR_BLOCKS):
+        send(b).wait()
+
+
+def final_kernel(
+    far_hbm, col_hbm, row_hbm, part_hbm, max_ref, sum_ref, out_hbm,
+    far_ref, col_ref, row_ref, part_ref, out_ref, sems,
+):
+    ins = [
+        pltpu.make_async_copy(far_hbm, far_ref, sems.at[0]),
+        pltpu.make_async_copy(part_hbm, part_ref, sems.at[1]),
+        pltpu.make_async_copy(col_hbm, col_ref, sems.at[2]),
+        pltpu.make_async_copy(row_hbm, row_ref, sems.at[3]),
+    ]
+    for move in ins:
+        move.start()
+    back = one_hot(
+        POS, POS, lambda o: (o & 3) * STRIDE + ((o >> 2) & 7) * 4 + (o >> 5)
+    )
     row = iota((HEADS * SUM_ROWS, 128), 0)
     lane = iota((HEADS * SUM_ROWS, 128), 1)
     pick = jnp.where(
         jnp.logical_and((row >> 4) == lane, (row & 15) < 3), 1.0, 0.0
     ).astype(bf16)
+    ins[0].wait()
     terms = jnp.concatenate([far_ref[g, POS:, :] for g in range(HEADS)], axis=0)
     lse = dot_tl(terms, pick)
     top = jnp.maximum(max_ref[...], lse)
@@ -242,12 +314,16 @@
     scale = 1.0 / (sum_ref[...] * own + far)
     own = own * scale
     far = far * scale
+    for move in ins[1:]:
+        move.wait()
+    moves = []
     for quad in range(QUADS):
         base = quad * 4 * HD
         out_ref[:, base : base + HD] = row_ref[quad]
-        out_ref[:, base + HD : base + 2 * HD] = dot(
-            back, col_ref[quad * POS : (quad + 1) * POS, :]
-        ).astype(bf16)
+        stack = jnp.concatenate(
+            [col_ref[x, quad * STRIDE : (quad + 1) * STRIDE, :] for x in range(4)], axis=0
+        )
+        out_ref[:, base + HD : base + 2 * HD] = dot(back, stack).astype(bf16)
         for h in range(2):
             g = quad * 2 + h
             merged = (
@@ -256,20 +332,28 @@
             )
             start = base + (2 + h) * HD
             out_ref[:, start : start + HD] = merged.astype(bf16)
-
-
-def call(kernel, outs, args, scalars=0, scratch=(), flops=0, moved=0, exps=0, mib=16, unread=0):
-    vmem = pl.BlockSpec(memory_space=pltpu.VMEM)
-    smem = pl.BlockSpec(memory_space=pltpu.SMEM)
-    hbm = pl.BlockSpec(memory_space=pl.ANY)
+        at = pl.ds(base, 4 * HD)
+        move = pltpu.make_async_copy(out_ref.at[:, at], out_hbm.at[:, at], sems.at[4 + quad])
+        move.start()
+        moves.append(move)
+    for move in moves:
+        move.wait()
+
+
+SPACES = {"v": pltpu.VMEM, "s": pltpu.SMEM, "h": pltpu.HBM, "a": pl.ANY}
+
+
+def call(kernel, outs, args, ins, to="v", scratch=(), flops=0, moved=0, exps=0, mib=16):
+    def spec(space):
+        return pl.BlockSpec(memory_space=SPACES[space])
+
     shapes = [jax.ShapeDtypeStruct(s, d) for s, d in outs]
     many = len(shapes) > 1
-    specs = [smem] * scalars + [hbm] * unread
     return pl.pallas_call(
         kernel,
         out_shape=shapes if many else shapes[0],
-        in_specs=specs + [vmem] * (len(args) - len(specs)),
-        out_specs=[vmem] * len(shapes) if many else vmem,
+        in_specs=[spec(space) for space in ins],
+        out_specs=[spec(to)] * len(shapes) if many else spec(to),
         scratch_shapes=list(scratch),
         compiler_params=pltpu.CompilerParams(vmem_limit_bytes=mib * 1024 * 1024),
         cost_estimate=pl.CostEstimate(flops=flops, bytes_accessed=moved, transcendentals=exps),
@@ -280,49 +364,40 @@
     return lax.all_to_all(array, axes, split_axis=0, concat_axis=0, tiled=True)
 
 
-def body(queries, keys, values):
-    heads_at = ("w", "c", "x")
-    plane = ("u", "v", "w", "c", "x")
-    wide = ("z", "u", "v", "w", "x")
-    mib = 1 << 20
-    heads, summary = call(
-        pack_far_kernel,
-        [((HEADS, POS, HD), bf16), ((64, 8, HD), bf16)],
-        (queries, keys, values),
-        flops=2 * 16 * 16 * 256 * 128,
-        moved=4 * mib,
-    )
-    summary = exchange(summary, plane)
-    summary = summary.reshape(64, 2, ROWS, HD).transpose(1, 0, 2, 3).reshape(1, 2, 256, HD)
-    items = call(
-        pack_column_kernel,
-        [((QUADS, 384, HD), bf16)],
-        (summary, queries, keys, values),
-        unread=1,
+def dma(n):
+    return pltpu.SemaphoreType.DMA((n,))
+
+
+mib = 1 << 20
+
+
+def pack_summary(keys, values):
+    return call(
+        pack_summary_kernel,
+        [((64, 8, HD), bf16)],
+        (keys, values),
+        "hh",
+        scratch=[pltpu.VMEM((128, QUADS * 4 * HD), bf16), dma(8)],
+        flops=2 * 16 * 16 * 128 * 128,
+        moved=mib,
+    )
+
+
+def pack(after, queries, keys, values):
+    return call(
+        pack_kernel,
+        [((QUADS, 384, HD), bf16), ((HEADS, POS, HD), bf16)],
+        (after, queries, keys, values),
+        "avvv",
+        to="h",
+        scratch=[pltpu.VMEM((QUADS, 384, HD), bf16), pltpu.VMEM((HEADS, POS, HD), bf16), dma(9)],
         flops=2 * 8 * 384 * 384 * 128,
         moved=4 * mib,
     )
-    summary = lax.all_gather(summary, "z", axis=0, tiled=True)
-    items = exchange(items.reshape(768, ROWS, HD), wide).reshape(3072, HD)
-    heads = exchange(heads, heads_at)
-    other = lax.ppermute(items, "c", [(0, 1), (1, 0)])
-    core = lax.axis_index("c").astype(jnp.int32).reshape(1)
-    column = call(
-        column_kernel,
-        [((1024, HD), bf16)],
-        (core, items, other),
-        scalars=1,
-        scratch=[
-            pltpu.VMEM((1024, HD), bf16),
-            pltpu.VMEM((2, 1024, HD), bf16),
-            pltpu.VMEM((2, 1024, HD), bf16),
-        ],
-        flops=4 * 1024 * 1280 * 128,
-        moved=2 * mib,
-        exps=1024 * 1280,
-    )
-    column = exchange(column.reshape(256, ROWS, HD), wide).reshape(1024, HD)
-    row_out, part, tops, sums = call(
+
+
+def rows(queries, keys, values):
+    return call(
         rows_kernel,
         [
             ((QUADS, POS, HD), bf16),
@@ -331,31 +406,95 @@
             ((POS, 128), f32),
         ],
         (queries, keys, values),
+        "vvv",
         flops=24 * 4 * 128 * 128 * 128,
         moved=5 * mib,
         exps=24 * 128 * 128,
     )
 
-    pair = lax.axis_index(("z", "u", "v")).astype(jnp.int32).reshape(1)
-    far = call(
+
+def columns(core, items, other):
+    return call(
+        column_kernel,
+        [((4, 256, HD), bf16)],
+        (core, items, other),
+        "shh",
+        to="h",
+        scratch=[
+            pltpu.VMEM((3072, HD), bf16),
+            pltpu.VMEM((3072, HD), bf16),
+            pltpu.VMEM((4, 256, HD), bf16),
+            pltpu.VMEM((1024, HD), bf16),
+            pltpu.VMEM((2, 1024, HD), bf16),
+            pltpu.VMEM((2, 1024, HD), bf16),
+            dma(6),
+        ],
+        flops=4 * 1024 * 1280 * 128,
+        moved=2 * mib,
+        exps=1024 * 1280,
+    )
+
+
+def far_part(pair, heads, summary):
+    return call(
         far_kernel,
         [((HEADS, PAY, HD), bf16)],
         (pair, heads, summary),
-        scalars=1,
-        scratch=[pltpu.VMEM((2048 // FAR_K, FAR_Q, FAR_K), f32)],
+        "shh",
+        to="h",
+        scratch=[
+            pltpu.VMEM((HEADS, POS, HD), bf16),
+            pltpu.VMEM((8, 2, 256, HD), bf16),
+            pltpu.VMEM((HEADS, PAY, HD), bf16),
+            pltpu.VMEM((2048 // FAR_K, FAR_Q, FAR_K), f32),
+            dma(2 + FAR_BLOCKS),
+        ],
         flops=8 * 1024 * 2048 * 128,
         moved=3 * mib,
         exps=2 * 1024 * 2048,
         mib=24,
     )
-    far = exchange(far, heads_at)
+
+
+def final(far, column, row_out, part, tops, sums):
     return call(
         final_kernel,
         [((POS, QUADS * 4 * HD), bf16)],
         (far, column, row_out, part, tops, sums),
+        "hhhhvv",
+        to="h",
+        scratch=[
+            pltpu.VMEM((HEADS, PAY, HD), bf16),
+            pltpu.VMEM((4, 256, HD), bf16),
+            pltpu.VMEM((QUADS, POS, HD), bf16),
+            pltpu.VMEM((HEADS, POS, HD), f32),
+            pltpu.VMEM((POS, QUADS * 4 * HD), bf16),
+            dma(12),
+        ],
         flops=2 * 8 * 128 * 128 * 128,
         moved=4 * mib,
     )
+
+
+def body(queries, keys, values):
+    heads_at = ("w", "c", "x")
+    plane = ("u", "v", "w", "c", "x")
+    wide = ("z", "u", "v", "w", "x")
+    back = ("x", "z", "u", "v", "w")
+    summary = exchange(pack_summary(keys, values), plane)
+    summary = summary.reshape(64, 2, ROWS, HD).transpose(1, 0, 2, 3).reshape(1, 2, 256, HD)
+    items, heads = pack(summary, queries, keys, values)
+    summary = lax.all_gather(summary, "z", axis=0, tiled=True)
+    items = exchange(items.reshape(768, ROWS, HD), wide).reshape(3072, HD)
+    heads = exchange(heads, heads_at)
+    other = lax.ppermute(items, "c", [(0, 1), (1, 0)])
+    core = lax.axis_index("c").astype(jnp.int32).reshape(1)
+    column = columns(core, items, other)
+    column = exchange(column.reshape(256, ROWS, HD), back).reshape(4, 256, HD)
+    row_out, part, tops, sums = rows(queries, keys, values)
+    pair = lax.axis_index(("z", "u", "v")).astype(jnp.int32).reshape(1)
+    far = exchange(far_part(pair, heads, summary), heads_at)
+    return final(far, column, row_out, part, tops, sums)
 
 
 def solution(mesh):

time: 147 us -> 151 us (1.027)
  Pallas kernels: 21.3 us -> 25.5 us
    pallas_call x6, Pallas kernels: 21.3 us -> 25.5 us  [call(): pl.pallas_call(kernel, out_shape=shapes if many else shapes[0], in_specs=...]
    unnamed x32 -> x36, local copies, waits for them, and re-layouts: 12 us -> 13.2 us
  transfers between devices with their start and end apart: 6 -> 6, of which waited for: 5 -> 4; matrix products, arithmetic and copies ran while one was open for 0% -> 0% of each run, Pallas kernels for 12% -> 12%
where the time goes in v2:
time: 151 us; the launch traced here: 150 us
  starting transfers between devices  43.9 us (29%)
  waiting for transfers between devices  32.5 us (22%)
  Pallas kernels  25.5 us (17%)
  blocking collectives  21.4 us (14%)
  between operations  13.6 us (9%)
  local copies, waits for them, and re-layouts  13.2 us (9%)
    all_to_all x4, starting transfers between devices, exchange(): return lax.all_to_all(array, axes, split_axis=0, concat_axis=0, tiled=True)  41.8 us
    all_to_all x4, waiting for transfers between devices, exchange(): return lax.all_to_all(array, axes, split_axis=0, concat_axis=0, tiled=True)  29.5 us
    pallas_call x6, Pallas kernels, call(): pl.pallas_call(kernel, out_shape=shapes if many else shapes[0], in_specs=...  25.5 us
    all_to_all x1, blocking collectives, exchange(): return lax.all_to_all(array, axes, split_axis=0, concat_axis=0, tiled=True)  21.4 us
    unnamed x36, local copies, waits for them, and re-layouts  13.2 us
  transfers between devices with their start and end apart: 6, of which 4 were waited for; matrix products, arithmetic and copies ran while one was open for 0% of the time, Pallas kernels for 12%

profile of v2, /device:TPU:1, one launch (start us, length us, event | category | flops | bytes accessed | tf_op | source)
XLA Modules:
  0.0 150.1 jit_solution(6370569128377560468)
XLA Ops:
  6.5 1.2 copy-done
  7.8 1.2 copy-done.2
  9.0 1.7 %shard_map.37 = bf16[64,8,128]{2,1,0:T(8,128)(2,1)S(1)} custom-call(bf16[128,4096]{1,0:T(8,128)(2,1)S(1)} %copy-done, bf16[128,4096]{1,0:T(8,128)(2,1)S(1)} %copy-done.2), custom_call_target="tpu_custom_call" | custom-call | flops 8388608 | bytes 1048576 | tf_op jit(solution)/shard_map/pallas_call | solution.py:352
  10.7 21.4 %all_to_all.25 = bf16[64,8,128]{2,1,0:T(8,128)(2,1)S(1)} all-to-all(bf16[64,8,128]{2,1,0:T(8,128)(2,1)S(1)} %shard_map.37), channel_id=1, replica_groups=mesh['x'=4,'z'=8,'u'=2,'v'=2,'w'=2,'c'=2] {'u','v','w','c','x'}, dimensions={0} | all-to-all | bytes 262144 | tf_op jit(solution)/shard_map/all_to_all | solution.py:364
  32.1 1.3 copy-done.4
  33.4 3.2 %shard_map.38 = (bf16[8,384,128]{2,1,0:T(8,128)(2,1)S(1)}, bf16[16,128,128]{2,1,0:T(8,128)(2,1)S(1)}) custom-call(bf16[1,2,256,128]{3,2,1,0:T(8,128)(2,1)S(1)} %bitcast.10, bf16[128,4096]{1,0:T(8,128)(2,1)S(1)} %copy-done.4, bf16[128,4096]{1,0:T(8,128)(2,1)S(1)} %copy-done.1, bf16[128,4096]{1,0:T(8,128)(2,1)S(1)} %copy-done.3), custom_call_target="tpu_custom_call" | custom-call | flops 301989888 | bytes 4194304 | tf_op jit(solution)/shard_map/pallas_call | solution.py:352
  37.7 16.9 %all-to-all-start.3 = ((bf16[768,4,128]{2,1,0:T(4,128)(2,1)}), bf16[768,4,128]{2,1,0:T(4,128)(2,1)S(1)}, u32[]{:S(2)}, u32[]{:S(2)}) async-start(bf16[768,4,128]{2,1,0:T(4,128)(2,1)} %bitcast.15), calls=%async_computation.3 | async-start | bytes 1572864 | tf_op jit(solution)/shard_map/all_to_all | solution.py:364
  55.3 22.6 %all-to-all-done.3 = bf16[768,4,128]{2,1,0:T(4,128)(2,1)S(1)} async-done(((bf16[768,4,128]{2,1,0:T(4,128)(2,1)}), bf16[768,4,128]{2,1,0:T(4,128)(2,1)S(1)}, u32[]{:S(2)}, u32[]{:S(2)}) %all-to-all-start.3) | async-done | bytes 786464 | tf_op jit(solution)/shard_map/all_to_all | solution.py:364
  77.9 6.9 %all-to-all-start.1 = ((bf16[16,128,128]{2,1,0:T(8,128)(2,1)}), bf16[16,128,128]{2,1,0:T(8,128)(2,1)S(1)}, u32[]{:S(2)}, u32[]{:S(2)}) async-start(bf16[16,128,128]{2,1,0:T(8,128)(2,1)} %copy-done.13), calls=%async_computation.1 | async-start | bytes 1048576 | tf_op jit(solution)/shard_map/all_to_all | solution.py:364
  84.8 2.0 %collective-permute-start = (bf16[3072,128]{1,0:T(8,128)(2,1)S(1)}, bf16[3072,128]{1,0:T(8,128)(2,1)}, u32[]{:S(2)}, u32[]{:S(2)}) collective-permute-start(bf16[3072,128]{1,0:T(8,128)(2,1)S(1)} %bitcast.13), channel_id=1, source_target_pairs={{0,1},{1,0},{2,3},{3,2},{4,5},{5,4},{6,7},{7,6},{8,9},{9,8},{10,11... | collective-permute-start | bytes 2359304 | tf_op jit(solution)/shard_map/ppermute | solution.py:490
  86.8 2.3 %collective-permute-done.other_hbm = bf16[3072,128]{1,0:T(8,128)(2,1)} collective-permute-done((bf16[3072,128]{1,0:T(8,128)(2,1)S(1)}, bf16[3072,128]{1,0:T(8,128)(2,1)}, u32[]{:S(2)}, u32[]{:S(2)}) %collective-permute-start) | collective-permute-done | bytes 786464 | tf_op jit(solution)/shard_map/ppermute | solution.py:490
  89.1 5.2 %shard_map.40 = bf16[4,256,128]{2,1,0:T(8,128)(2,1)S(1)} custom-call(s32[1]{0:T(128)} %bitcast.5.core_ref, bf16[3072,128]{1,0:T(8,128)(2,1)S(1)} %bitcast.14, bf16[3072,128]{1,0:T(8,128)(2,1)} %collective-permute-done.other_hbm), custom_call_target="tpu_custom_call" | custom-call | flops 671088640 | bytes 2097152 | tf_op jit(solution)/shard_map/pallas_call | solution.py:352
  95.8 11.6 %all-to-all-start.4 = ((bf16[256,4,128]{2,1,0:T(4,128)(2,1)}), bf16[256,4,128]{2,1,0:T(4,128)(2,1)S(1)}, u32[]{:S(2)}, u32[]{:S(2)}) async-start(bf16[256,4,128]{2,1,0:T(4,128)(2,1)} %bitcast.16), calls=%async_computation.4 | async-start | bytes 524288 | tf_op jit(solution)/shard_map/all_to_all | solution.py:364
  107.5 1.0 copy-done.12
  108.5 1.2 copy-done.17
  109.8 6.8 %shard_map.39 = bf16[16,144,128]{2,1,0:T(8,128)(2,1)S(1)} custom-call(s32[1]{0:T(128)} %bitcast.pair_ref, bf16[16,128,128]{2,1,0:T(8,128)(2,1)S(1)} %copy-done.12, bf16[8,2,256,128]{3,2,1,0:T(8,128)(2,1)S(1)} %copy-done.17), custom_call_target="tpu_custom_call" | custom-call | flops 2147483648 | bytes 3145728 | tf_op jit(solution)/shard_map/pallas_call | solution.py:352
  117.4 3.4 %all-to-all-done.4 = bf16[256,4,128]{2,1,0:T(4,128)(2,1)S(1)} async-done(((bf16[256,4,128]{2,1,0:T(4,128)(2,1)}), bf16[256,4,128]{2,1,0:T(4,128)(2,1)S(1)}, u32[]{:S(2)}, u32[]{:S(2)}) %all-to-all-start.4) | async-done | bytes 262176 | tf_op jit(solution)/shard_map/all_to_all | solution.py:364
  120.8 6.4 %all-to-all-start.2 = ((bf16[16,144,128]{2,1,0:T(8,128)(2,1)}), bf16[16,144,128]{2,1,0:T(8,128)(2,1)}, u32[]{:S(2)}, u32[]{:S(2)}) async-start(bf16[16,144,128]{2,1,0:T(8,128)(2,1)} %copy-done.10), calls=%async_computation.2 | async-start | bytes 1179648 | tf_op jit(solution)/shard_map/all_to_all | solution.py:364
  127.3 5.8 %shard_map.41 = (bf16[8,128,128]{2,1,0:T(8,128)(2,1)S(1)}, f32[16,128,128]{2,1,0:T(8,128)S(1)}, f32[128,128]{1,0:T(8,128)S(1)}, f32[128,128]{1,0:T(8,128)S(1)}) custom-call(bf16[128,4096]{1,0:T(8,128)(2,1)S(1)} %copy-done.5, bf16[128,4096]{1,0:T(8,128)(2,1)S(1)} %copy-done.1, bf16[128,4096]{1,0:T(8,128)(2,1)S(1)} %copy-done.3), custom_call_target="tpu_custom_call" | custom-call | flops 201326592 | bytes 5242880 | tf_op jit(solution)/shard_map/pallas_call | solution.py:352
  133.1 1.0 copy-done.7
  134.8 3.5 %all-to-all-done.2.far_hbm = bf16[16,144,128]{2,1,0:T(8,128)(2,1)} async-done(((bf16[16,144,128]{2,1,0:T(8,128)(2,1)}), bf16[16,144,128]{2,1,0:T(8,128)(2,1)}, u32[]{:S(2)}, u32[]{:S(2)}) %all-to-all-start.2) | async-done | bytes 589856 | tf_op jit(solution)/shard_map/all_to_all | solution.py:364
  138.3 1.2 copy-done.8
  139.5 0.9 copy-done.15
  140.5 2.7 %shard_map.42 = bf16[128,4096]{1,0:T(8,128)(2,1)} custom-call(bf16[16,144,128]{2,1,0:T(8,128)(2,1)} %all-to-all-done.2.far_hbm, bf16[4,256,128]{2,1,0:T(8,128)(2,1)S(1)} %bitcast.12, bf16[8,128,128]{2,1,0:T(8,128)(2,1)S(1)} %copy-done.15, f32[16,128,128]{2,1,0:T(8,128)S(1)} %copy-done.8, f32[128,128]{1,0:T(8,128)S(1)} %get-tuple-element.15.max_ref, ...), custom_call_target="tpu_custom_call" | custom-call | flops 33554432 | bytes 4194304 | tf_op jit(solution)/shard_map/pallas_call | solution.py:352
  (33 shorter events, 4.9 us)
Async XLA Ops:
  6.5 1.2 copy-start
  7.8 1.2 copy-start.2
  9.0 23.1 %copy-start.1 = (bf16[128,4096]{1,0:T(8,128)(2,1)S(1)}, bf16[128,4096]{1,0:T(8,128)(2,1)}, u32[]{:S(2)}) copy-start(bf16[128,4096]{1,0:T(8,128)(2,1)} %k_ref.5) | copy-start | bytes 3145732
  9.0 23.1 %copy-start.3 = (bf16[128,4096]{1,0:T(8,128)(2,1)S(1)}, bf16[128,4096]{1,0:T(8,128)(2,1)}, u32[]{:S(2)}) copy-start(bf16[128,4096]{1,0:T(8,128)(2,1)} %v_ref.5) | copy-start | bytes 3145732
  32.1 4.5 %copy-start.6 = (bf16[64,2,4,128]{3,2,0,1:T(4,128)(2,1)}, bf16[64,2,4,128]{3,2,0,1:T(4,128)(2,1)S(1)}, u32[]{:S(2)}) copy-start(bf16[64,2,4,128]{3,2,0,1:T(4,128)(2,1)S(1)} %copy.5) | copy-start | bytes 393220
  32.1 1.3 copy-start.4
  36.6 0.9 copy-start.9
  36.6 1.1 copy-start.13
  37.7 40.2 %all-to-all-start.3 = ((bf16[768,4,128]{2,1,0:T(4,128)(2,1)}), bf16[768,4,128]{2,1,0:T(4,128)(2,1)S(1)}, u32[]{:S(2)}, u32[]{:S(2)}) async-start(bf16[768,4,128]{2,1,0:T(4,128)(2,1)} %bitcast.15), calls=%async_computation.3 | async-start | bytes 1572864 | tf_op jit(solution)/shard_map/all_to_all | solution.py:364
  54.6 52.9 %all-gather.2.cloned.1.call-start = ((), (), s32[]{:S(2)}) async-start(), calls=%async_computation.5 | async-start | bytes 1179648 | tf_op jit(solution)/shard_map/all_gather | solution.py:487
  77.9 17.1 %all-to-all-start.1 = ((bf16[16,128,128]{2,1,0:T(8,128)(2,1)}), bf16[16,128,128]{2,1,0:T(8,128)(2,1)S(1)}, u32[]{:S(2)}, u32[]{:S(2)}) async-start(bf16[16,128,128]{2,1,0:T(8,128)(2,1)} %copy-done.13), calls=%async_computation.1 | async-start | bytes 1048576 | tf_op jit(solution)/shard_map/all_to_all | solution.py:364
  84.8 4.3 %collective-permute-start = (bf16[3072,128]{1,0:T(8,128)(2,1)S(1)}, bf16[3072,128]{1,0:T(8,128)(2,1)}, u32[]{:S(2)}, u32[]{:S(2)}) collective-permute-start(bf16[3072,128]{1,0:T(8,128)(2,1)S(1)} %bitcast.13), channel_id=1, source_target_pairs={{0,1},{1,0},{2,3},{3,2},{4,5},{5,4},{6,7},{7,6},{8,9},{9,8},{10,11... | collective-permute-start | bytes 2359304 | tf_op jit(solution)/shard_map/ppermute | solution.py:490
  94.3 0.7 copy-start.16
  95.0 0.8 copy-start.11
  95.8 25.0 %all-to-all-start.4 = ((bf16[256,4,128]{2,1,0:T(4,128)(2,1)}), bf16[256,4,128]{2,1,0:T(4,128)(2,1)S(1)}, u32[]{:S(2)}, u32[]{:S(2)}) async-start(bf16[256,4,128]{2,1,0:T(4,128)(2,1)} %bitcast.16), calls=%async_computation.4 | async-start | bytes 524288 | tf_op jit(solution)/shard_map/all_to_all | solution.py:364
  107.5 1.0 copy-start.12
  108.5 1.2 copy-start.17
  116.6 0.8 copy-start.10
  117.4 9.9 %copy-start.5 = (bf16[128,4096]{1,0:T(8,128)(2,1)S(1)}, bf16[128,4096]{1,0:T(8,128)(2,1)}, u32[]{:S(2)}) copy-start(bf16[128,4096]{1,0:T(8,128)(2,1)} %q_ref.3) | copy-start | bytes 3145732
  120.8 17.4 %all-to-all-start.2 = ((bf16[16,144,128]{2,1,0:T(8,128)(2,1)}), bf16[16,144,128]{2,1,0:T(8,128)(2,1)}, u32[]{:S(2)}, u32[]{:S(2)}) async-start(bf16[16,144,128]{2,1,0:T(8,128)(2,1)} %copy-done.10), calls=%async_computation.2 | async-start | bytes 1179648 | tf_op jit(solution)/shard_map/all_to_all | solution.py:364
  133.1 1.0 copy-start.7
  134.1 0.7 copy-start.14
  138.3 1.2 copy-start.8
  139.5 0.9 copy-start.15
Sparse Core Ops, SparseCore 0:
  57.5 38.0 all-gather.1

commit v3 on v2

--- a/solution.py
+++ b/solution.py
@@ -55,7 +55,7 @@
     return ref[:, start : start + HD]
 
 
-def pack_summary_kernel(k_ref, v_ref, sum_ref, buf, sems):
+def pack_summary_kernel(k_ref, v_ref, sum_hbm, buf, sum_ref, sems):
     moves = []
     for a, ref in enumerate((k_ref, v_ref)):
         for r in range(ROWS):
@@ -71,41 +71,75 @@
         move.wait()
     for g in range(HEADS):
         rows = dot(pick, head(buf, g // 2, 2 + g % 2)).astype(bf16)
-        for t in range(sum_ref.shape[0] // HEADS):
-            sum_ref[t * HEADS + g] = rows
-
-
-def pack_kernel(after_ref, q_ref, k_ref, v_ref, item_ref, query_ref, items, heads, sems):
+        sum_ref[g] = rows
+    moves = []
+    for t in range(sum_hbm.shape[0] // HEADS):
+        move = pltpu.make_async_copy(
+            sum_ref, sum_hbm.at[pl.ds(t * HEADS, HEADS)], sems.at[2 * ROWS + t]
+        )
+        move.start()
+        moves.append(move)
+    for move in moves:
+        move.wait()
+
+
+def pack_kernel(q_hbm, k_hbm, v_hbm, item_hbm, query_hbm, stack, items, sems, outs):
     def source(o):
         col = div12(o)
         rest = o - 12 * col
         return (rest >> 2) * POS + (rest & 3) * STRIDE + col
 
+    ins = []
+    for quad in range(QUADS):
+        at = pl.ds((quad * 4 + 1) * HD, HD)
+        for a, ref in enumerate((q_hbm, k_hbm, v_hbm)):
+            move = pltpu.make_async_copy(
+                ref.at[:, at], stack.at[quad, pl.ds(a * POS, POS), :], sems.at[quad * 3 + a]
+            )
+            move.start()
+            ins.append(move)
+    moves = []
+    for g in range(HEADS):
+        at = pl.ds(((g // 2) * 4 + 2 + g % 2) * HD, HD)
+        moves.append(
+            pltpu.make_async_copy(q_hbm.at[:, at], query_hbm.at[g], outs.at[QUADS + g])
+        )
     perm = one_hot(384, 384, source)
-    moves = []
     for quad in range(QUADS):
-        stack = jnp.concatenate(
-            [head(q_ref, quad, 1), head(k_ref, quad, 1), head(v_ref, quad, 1)], axis=0
-        )
-        items[quad] = dot(perm, stack).astype(bf16)
-        move = pltpu.make_async_copy(items.at[quad], item_ref.at[quad], sems.at[quad])
-        move.start()
+        for a in range(3):
+            ins[quad * 3 + a].wait()
+        items[quad] = dot(perm, stack[quad]).astype(bf16)
+        move = pltpu.make_async_copy(items.at[quad], item_hbm.at[quad], outs.at[quad])
+        move.start()
+        if quad == 0:
+            for copy in moves:
+                copy.start()
         moves.append(move)
-    for g in range(HEADS):
-        heads[g] = head(q_ref, g // 2, 2 + g % 2)
-    move = pltpu.make_async_copy(heads, query_ref, sems.at[QUADS])
-    move.start()
-    moves.append(move)
     for move in moves:
         move.wait()
 
 
-def rows_kernel(q_ref, k_ref, v_ref, row_ref, part_ref, max_ref, sum_ref):
+def order_kernel(after_ref, item_ref, out_ref):
+    pass
+
+
+def rows_kernel(
+    q_hbm, k_hbm, v_hbm, row_hbm, part_hbm, stat_hbm,
+    q_ref, k_ref, v_ref, row_ref, part_ref, stat_ref, sems,
+):
+    ins = []
+    for a, (hbm, ref) in enumerate(((q_hbm, q_ref), (k_hbm, k_ref), (v_hbm, v_ref))):
+        move = pltpu.make_async_copy(hbm, ref, sems.at[a])
+        move.start()
+        ins.append(move)
     pos = iota((POS, POS), 0)
     key = iota((POS, POS), 1)
     visible = jnp.logical_and((key >> 5) == (pos >> 5), key <= pos)
     tops = jnp.zeros((POS, POS), f32)
     sums = jnp.ones((POS, POS), f32)
+    for move in ins:
+        move.wait()
+    moves = []
     for quad in range(QUADS):
         for kind in (0, 2, 3):
             s = dot_t(head(q_ref, quad, kind), head(k_ref, quad, kind)) * SCALE
@@ -121,8 +155,17 @@
                 part_ref[slot] = acc
                 tops = jnp.where(key == slot, m, tops)
                 sums = jnp.where(key == slot, total, sums)
-    max_ref[...] = tops
-    sum_ref[...] = sums
+        two = pl.ds(quad * 2, 2)
+        moves.append(pltpu.make_async_copy(part_ref.at[two], part_hbm.at[two], sems.at[3 + quad]))
+        moves[-1].start()
+    stat_ref[0] = tops
+    stat_ref[1] = sums
+    moves.append(pltpu.make_async_copy(row_ref, row_hbm, sems.at[11]))
+    moves.append(pltpu.make_async_copy(stat_ref, stat_hbm, sems.at[12]))
+    moves[-1].start()
+    moves[-2].start()
+    for move in moves:
+        move.wait()
 
 
 def column_kernel(
@@ -286,11 +329,12 @@
 
 
 def final_kernel(
-    far_hbm, col_hbm, row_hbm, part_hbm, max_ref, sum_ref, out_hbm,
-    far_ref, col_ref, row_ref, part_ref, out_ref, sems,
+    far_hbm, col_hbm, row_hbm, part_hbm, stat_hbm, out_hbm,
+    far_ref, col_ref, row_ref, part_ref, stat_ref, out_ref, sems,
 ):
     ins = [
         pltpu.make_async_copy(far_hbm, far_ref, sems.at[0]),
+        pltpu.make_async_copy(stat_hbm, stat_ref, sems.at[12]),
         pltpu.make_async_copy(part_hbm, part_ref, sems.at[1]),
         pltpu.make_async_copy(col_hbm, col_ref, sems.at[2]),
         pltpu.make_async_copy(row_hbm, row_ref, sems.at[3]),
@@ -306,15 +350,16 @@
         jnp.logical_and((row >> 4) == lane, (row & 15) < 3), 1.0, 0.0
     ).astype(bf16)
     ins[0].wait()
+    ins[1].wait()
     terms = jnp.concatenate([far_ref[g, POS:, :] for g in range(HEADS)], axis=0)
     lse = dot_tl(terms, pick)
-    top = jnp.maximum(max_ref[...], lse)
-    own = jnp.exp2(max_ref[...] - top)
+    top = jnp.maximum(stat_ref[0], lse)
+    own = jnp.exp2(stat_ref[0] - top)
     far = jnp.exp2(lse - top)
-    scale = 1.0 / (sum_ref[...] * own + far)
+    scale = 1.0 / (stat_ref[1] * own + far)
     own = own * scale
     far = far * scale
-    for move in ins[1:]:
+    for move in ins[2:]:
         move.wait()
     moves = []
     for quad in range(QUADS):
@@ -343,7 +388,7 @@
 SPACES = {"v": pltpu.VMEM, "s": pltpu.SMEM, "h": pltpu.HBM, "a": pl.ANY}
 
 
-def call(kernel, outs, args, ins, to="v", scratch=(), flops=0, moved=0, exps=0, mib=16):
+def call(kernel, outs, args, ins, to="v", scratch=(), flops=0, moved=0, exps=0, alias=None):
     def spec(space):
         return pl.BlockSpec(memory_space=SPACES[space])
 
@@ -355,7 +400,8 @@
         in_specs=[spec(space) for space in ins],
         out_specs=[spec(to)] * len(shapes) if many else spec(to),
         scratch_shapes=list(scratch),
-        compiler_params=pltpu.CompilerParams(vmem_limit_bytes=mib * 1024 * 1024),
+        input_output_aliases=alias or {},
+        compiler_params=pltpu.CompilerParams(vmem_limit_bytes=60 * 1024 * 1024),
         cost_estimate=pl.CostEstimate(flops=flops, bytes_accessed=moved, transcendentals=exps),
     )(*args)
 
@@ -377,36 +423,52 @@
         [((64, 8, HD), bf16)],
         (keys, values),
         "hh",
-        scratch=[pltpu.VMEM((128, QUADS * 4 * HD), bf16), dma(8)],
+        to="h",
+        scratch=[
+            pltpu.VMEM((128, QUADS * 4 * HD), bf16),
+            pltpu.VMEM((HEADS, 8, HD), bf16),
+            dma(12),
+        ],
         flops=2 * 16 * 16 * 128 * 128,
         moved=mib,
     )
 
 
-def pack(after, queries, keys, values):
+def pack(queries, keys, values):
     return call(
         pack_kernel,
         [((QUADS, 384, HD), bf16), ((HEADS, POS, HD), bf16)],
-        (after, queries, keys, values),
-        "avvv",
+        (queries, keys, values),
+        "hhh",
         to="h",
-        scratch=[pltpu.VMEM((QUADS, 384, HD), bf16), pltpu.VMEM((HEADS, POS, HD), bf16), dma(9)],
+        scratch=[
+            pltpu.VMEM((QUADS, 384, HD), bf16),
+            pltpu.VMEM((QUADS, 384, HD), bf16),
+            dma(24),
+            dma(24),
+        ],
         flops=2 * 8 * 384 * 384 * 128,
         moved=4 * mib,
     )
 
 
+def ordered(after, items):
+    return call(
+        order_kernel, [((QUADS, 384, HD), bf16)], (after, items), "aa", to="a", alias={1: 0}
+    )
+
+
 def rows(queries, keys, values):
+    outs = [((QUADS, POS, HD), bf16), ((HEADS, POS, HD), f32), ((2, POS, 128), f32)]
     return call(
         rows_kernel,
-        [
-            ((QUADS, POS, HD), bf16),
-            ((HEADS, POS, HD), f32),
-            ((POS, 128), f32),
-            ((POS, 128), f32),
-        ],
+        outs,
         (queries, keys, values),
-        "vvv",
+        "hhh",
+        to="h",
+        scratch=[pltpu.VMEM((POS, QUADS * 4 * HD), bf16)] * 3
+        + [pltpu.VMEM(*out) for out in outs]
+        + [dma(13)],
         flops=24 * 4 * 128 * 128 * 128,
         moved=5 * mib,
         exps=24 * 128 * 128,
@@ -452,24 +514,24 @@
         flops=8 * 1024 * 2048 * 128,
         moved=3 * mib,
         exps=2 * 1024 * 2048,
-        mib=24,
-    )
-
-
-def final(far, column, row_out, part, tops, sums):
+    )
+
+
+def final(far, column, row_out, part, stat):
     return call(
         final_kernel,
         [((POS, QUADS * 4 * HD), bf16)],
-        (far, column, row_out, part, tops, sums),
-        "hhhhvv",
+        (far, column, row_out, part, stat),
+        "hhhhh",
         to="h",
         scratch=[
             pltpu.VMEM((HEADS, PAY, HD), bf16),
             pltpu.VMEM((4, 256, HD), bf16),
             pltpu.VMEM((QUADS, POS, HD), bf16),
             pltpu.VMEM((HEADS, POS, HD), f32),
+            pltpu.VMEM((2, POS, 128), f32),
             pltpu.VMEM((POS, QUADS * 4 * HD), bf16),
-            dma(12),
+            dma(13),
         ],
         flops=2 * 8 * 128 * 128 * 128,
         moved=4 * mib,
@@ -483,7 +545,8 @@
     back = ("x", "z", "u", "v", "w")
     summary = exchange(pack_summary(keys, values), plane)
     summary = summary.reshape(64, 2, ROWS, HD).transpose(1, 0, 2, 3).reshape(1, 2, 256, HD)
-    items, heads = pack(summary, queries, keys, values)
+    items, heads = pack(queries, keys, values)
+    items = ordered(summary, items)
     summary = lax.all_gather(summary, "z", axis=0, tiled=True)
     items = exchange(items.reshape(768, ROWS, HD), wide).reshape(3072, HD)
     heads = exchange(heads, heads_at)
@@ -491,10 +554,10 @@
     core = lax.axis_index("c").astype(jnp.int32).reshape(1)
     column = columns(core, items, other)
     column = exchange(column.reshape(256, ROWS, HD), back).reshape(4, 256, HD)
-    row_out, part, tops, sums = rows(queries, keys, values)
+    row_out, part, stat = rows(queries, keys, values)
     pair = lax.axis_index(("z", "u", "v")).astype(jnp.int32).reshape(1)
     far = exchange(far_part(pair, heads, summary), heads_at)
-    return final(far, column, row_out, part, tops, sums)
+    return final(far, column, row_out, part, stat)
 
 
 def solution(mesh):

time: 151 us -> 157 us (1.040)
  blocking collectives: 21.4 us -> 0 us
  Pallas kernels: 25.5 us -> 46.2 us
  starting transfers between devices: 43.9 us -> 60.1 us
  local copies, waits for them, and re-layouts: 13.2 us -> 3.13 us
    all_to_all x1 -> x0, blocking collectives: 21.4 us -> none  [exchange(): return lax.all_to_all(array, axes, split_axis=0, concat_axis=0, tiled=True)]
    pallas_call x6 -> x7, Pallas kernels: 25.5 us -> 46.2 us  [call(): pl.pallas_call(kernel, out_shape=shapes if many else shapes[0], in_specs=...]
    all_to_all x4 -> x5, starting transfers between devices: 41.8 us -> 58 us  [exchange(): return lax.all_to_all(array, axes, split_axis=0, concat_axis=0, tiled=True)]
    unnamed x36 -> x10, local copies, waits for them, and re-layouts: 13.2 us -> 2.43 us
    all_to_all x4 -> x5, waiting for transfers between devices: 29.5 us -> 30.3 us  [exchange(): return lax.all_to_all(array, axes, split_axis=0, concat_axis=0, tiled=True)]
  transfers between devices with their start and end apart: 6 -> 7, of which waited for: 4 -> 4; matrix products, arithmetic and copies ran while one was open for 0% -> 0% of each run, Pallas kernels for 12% -> 26%
where the time goes in v3:
time: 157 us; the launch traced here: 156 us
  starting transfers between devices  60.1 us (38%)
  Pallas kernels  46.2 us (29%)
  waiting for transfers between devices  33.1 us (21%)
  between operations  13.5 us (9%)
  local copies, waits for them, and re-layouts  3.13 us (2%)
    all_to_all x5, starting transfers between devices, exchange(): return lax.all_to_all(array, axes, split_axis=0, concat_axis=0, tiled=True)  58 us
    pallas_call x7, Pallas kernels, call(): pl.pallas_call(kernel, out_shape=shapes if many else shapes[0], in_specs=...  46.2 us
    all_to_all x5, waiting for transfers between devices, exchange(): return lax.all_to_all(array, axes, split_axis=0, concat_axis=0, tiled=True)  30.3 us
  transfers between devices with their start and end apart: 7, of which 4 were waited for; matrix products, arithmetic and copies ran while one was open for 0% of the time, Pallas kernels for 26%

profile of v3, /device:TPU:1, one launch (start us, length us, event | category | flops | bytes accessed | tf_op | source)
XLA Modules:
  0.0 156.1 jit_solution(12677197880872195156)
XLA Ops:
  6.5 2.3 %shard_map.38 = bf16[64,8,128]{2,1,0:T(8,128)(2,1)} custom-call(bf16[128,4096]{1,0:T(8,128)(2,1)} %k_hbm.3, bf16[128,4096]{1,0:T(8,128)(2,1)} %v_hbm.3), custom_call_target="tpu_custom_call" | custom-call | flops 8388608 | bytes 1048576 | tf_op jit(solution)/shard_map/pallas_call | solution.py:397
  8.8 11.6 %all-to-all-start.1 = ((bf16[64,8,128]{2,1,0:T(8,128)(2,1)}), bf16[64,8,128]{2,1,0:T(8,128)(2,1)S(1)}, u32[]{:S(2)}, u32[]{:S(2)}) async-start(bf16[64,8,128]{2,1,0:T(8,128)(2,1)} %shard_map.38), calls=%async_computation.1 | async-start | bytes 262144 | tf_op jit(solution)/shard_map/all_to_all | solution.py:410
  20.5 18.5 %shard_map.37 = (bf16[8,384,128]{2,1,0:T(8,128)(2,1)}, bf16[16,128,128]{2,1,0:T(8,128)(2,1)}) custom-call(bf16[128,4096]{1,0:T(8,128)(2,1)} %q_hbm.3, bf16[128,4096]{1,0:T(8,128)(2,1)} %k_hbm.3, bf16[128,4096]{1,0:T(8,128)(2,1)} %v_hbm.3), custom_call_target="tpu_custom_call" | custom-call | flops 301989888 | bytes 4194304 | tf_op jit(solution)/shard_map/pallas_call | solution.py:397
  39.0 0.7 copy.6
  39.7 22.2 %all-to-all-start.3 = ((bf16[768,4,128]{2,1,0:T(4,128)(2,1)}), bf16[768,4,128]{2,1,0:T(4,128)(2,1)S(1)}, u32[]{:S(2)}, u32[]{:S(2)}) async-start(bf16[768,4,128]{2,1,0:T(4,128)(2,1)} %bitcast.10), calls=%async_computation.3 | async-start | bytes 1572864 | tf_op jit(solution)/shard_map/all_to_all | solution.py:410
  61.9 0.0 all-gather.2.cloned.1.call-start
  61.9 0.7 all-gather.2.cloned.1.call-update
  62.6 22.7 %all-to-all-done.3 = bf16[768,4,128]{2,1,0:T(4,128)(2,1)S(1)} async-done(((bf16[768,4,128]{2,1,0:T(4,128)(2,1)}), bf16[768,4,128]{2,1,0:T(4,128)(2,1)S(1)}, u32[]{:S(2)}, u32[]{:S(2)}) %all-to-all-start.3) | async-done | bytes 786464 | tf_op jit(solution)/shard_map/all_to_all | solution.py:410
  85.3 6.8 %all-to-all-start = ((bf16[16,128,128]{2,1,0:T(8,128)(2,1)}), bf16[16,128,128]{2,1,0:T(8,128)(2,1)S(1)}, u32[]{:S(2)}, u32[]{:S(2)}) async-start(bf16[16,128,128]{2,1,0:T(8,128)(2,1)} %get-tuple-element.10), calls=%async_computation | async-start | bytes 1048576 | tf_op jit(solution)/shard_map/all_to_all | solution.py:410
  92.1 2.0 %collective-permute-start = (bf16[3072,128]{1,0:T(8,128)(2,1)S(1)}, bf16[3072,128]{1,0:T(8,128)(2,1)S(1)}, u32[]{:S(2)}, u32[]{:S(2)}) collective-permute-start(bf16[3072,128]{1,0:T(8,128)(2,1)S(1)} %bitcast.14), channel_id=1, source_target_pairs={{0,1},{1,0},{2,3},{3,2},{4,5},{5,4},{6,7},{7,6},{8,9},{9,8},{10,11... | collective-permute-start | bytes 2359304 | tf_op jit(solution)/shard_map/ppermute | solution.py:553
  94.1 2.1 %collective-permute-done.other_hbm = bf16[3072,128]{1,0:T(8,128)(2,1)S(1)} collective-permute-done((bf16[3072,128]{1,0:T(8,128)(2,1)S(1)}, bf16[3072,128]{1,0:T(8,128)(2,1)S(1)}, u32[]{:S(2)}, u32[]{:S(2)}) %collective-permute-start) | collective-permute-done | bytes 786464 | tf_op jit(solution)/shard_map/ppermute | solution.py:553
  96.2 0.9 copy-done.4
  97.1 5.7 %shard_map.41 = bf16[4,256,128]{2,1,0:T(8,128)(2,1)} custom-call(s32[1]{0:T(128)} %bitcast.4.core_ref, bf16[3072,128]{1,0:T(8,128)(2,1)} %bitcast.15, bf16[3072,128]{1,0:T(8,128)(2,1)} %copy-done.4), custom_call_target="tpu_custom_call" | custom-call | flops 671088640 | bytes 2097152 | tf_op jit(solution)/shard_map/pallas_call | solution.py:397
  102.8 0.0 all-to-all-done.q_hbm
  102.9 11.6 %all-to-all-start.4 = ((bf16[256,4,128]{2,1,0:T(4,128)(2,1)}), bf16[256,4,128]{2,1,0:T(4,128)(2,1)S(1)}, u32[]{:S(2)}, u32[]{:S(2)}) async-start(bf16[256,4,128]{2,1,0:T(4,128)(2,1)} %bitcast.17), calls=%async_computation.4 | async-start | bytes 524288 | tf_op jit(solution)/shard_map/all_to_all | solution.py:410
  114.5 0.0 all-gather.2.cloned.1.call-done.kv_hbm
  114.6 8.1 %shard_map.39 = bf16[16,144,128]{2,1,0:T(8,128)(2,1)} custom-call(s32[1]{0:T(128)} %bitcast.pair_ref, bf16[16,128,128]{2,1,0:T(8,128)(2,1)} %copy-done.3, bf16[8,2,256,128]{3,2,1,0:T(8,128)(2,1)} %all-gather.2.cloned.1.call-done.kv_hbm), custom_call_target="tpu_custom_call" | custom-call | flops 2147483648 | bytes 3145728 | tf_op jit(solution)/shard_map/pallas_call | solution.py:397
  122.6 5.3 %all-to-all-done.4 = bf16[256,4,128]{2,1,0:T(4,128)(2,1)S(1)} async-done(((bf16[256,4,128]{2,1,0:T(4,128)(2,1)}), bf16[256,4,128]{2,1,0:T(4,128)(2,1)S(1)}, u32[]{:S(2)}, u32[]{:S(2)}) %all-to-all-start.4) | async-done | bytes 262176 | tf_op jit(solution)/shard_map/all_to_all | solution.py:410
  127.9 0.7 copy-done.1
  128.6 5.8 %all-to-all-start.2 = ((bf16[16,144,128]{2,1,0:T(8,128)(2,1)}), bf16[16,144,128]{2,1,0:T(8,128)(2,1)S(1)}, u32[]{:S(2)}, u32[]{:S(2)}) async-start(bf16[16,144,128]{2,1,0:T(8,128)(2,1)} %shard_map.39), calls=%async_computation.2 | async-start | bytes 1179648 | tf_op jit(solution)/shard_map/all_to_all | solution.py:410
  134.4 8.6 %shard_map.42 = (bf16[8,128,128]{2,1,0:T(8,128)(2,1)}, f32[16,128,128]{2,1,0:T(8,128)}, f32[2,128,128]{2,1,0:T(8,128)}) custom-call(bf16[128,4096]{1,0:T(8,128)(2,1)} %q_hbm.3, bf16[128,4096]{1,0:T(8,128)(2,1)} %k_hbm.3, bf16[128,4096]{1,0:T(8,128)(2,1)} %v_hbm.3), custom_call_target="tpu_custom_call" | custom-call | flops 201326592 | bytes 5242880 | tf_op jit(solution)/shard_map/pallas_call | solution.py:397
  143.1 2.3 %all-to-all-done.2.far_hbm = bf16[16,144,128]{2,1,0:T(8,128)(2,1)S(1)} async-done(((bf16[16,144,128]{2,1,0:T(8,128)(2,1)}), bf16[16,144,128]{2,1,0:T(8,128)(2,1)S(1)}, u32[]{:S(2)}, u32[]{:S(2)}) %all-to-all-start.2) | async-done | bytes 589856 | tf_op jit(solution)/shard_map/all_to_all | solution.py:410
  145.4 0.8 copy-done
  146.2 3.0 %shard_map.43 = bf16[128,4096]{1,0:T(8,128)(2,1)} custom-call(bf16[16,144,128]{2,1,0:T(8,128)(2,1)} %copy-done, bf16[4,256,128]{2,1,0:T(8,128)(2,1)} %bitcast.13, bf16[8,128,128]{2,1,0:T(8,128)(2,1)} %get-tuple-element.12.row_hbm, f32[16,128,128]{2,1,0:T(8,128)} %get-tuple-element.13.part_hbm, f32[2,128,128]{2,1,0:T(8,128)} %get-tuple-element.14.stat_hbm), custom_call_target="tpu_custom_call" | custom-call | flops 33554432 | bytes 4194304 | tf_op jit(solution)/shard_map/pallas_call | solution.py:397
  (9 shorter events, 0.0 us)
Async XLA Ops:
  8.8 30.1 %all-to-all-start.1 = ((bf16[64,8,128]{2,1,0:T(8,128)(2,1)}), bf16[64,8,128]{2,1,0:T(8,128)(2,1)S(1)}, u32[]{:S(2)}, u32[]{:S(2)}) async-start(bf16[64,8,128]{2,1,0:T(8,128)(2,1)} %shard_map.38), calls=%async_computation.1 | async-start | bytes 262144 | tf_op jit(solution)/shard_map/all_to_all | solution.py:410
  39.7 45.6 %all-to-all-start.3 = ((bf16[768,4,128]{2,1,0:T(4,128)(2,1)}), bf16[768,4,128]{2,1,0:T(4,128)(2,1)S(1)}, u32[]{:S(2)}, u32[]{:S(2)}) async-start(bf16[768,4,128]{2,1,0:T(4,128)(2,1)} %bitcast.10), calls=%async_computation.3 | async-start | bytes 1572864 | tf_op jit(solution)/shard_map/all_to_all | solution.py:410
  61.9 52.7 %all-gather.2.cloned.1.call-start = ((), (), s32[]{:S(2)}) async-start(), calls=%async_computation.5 | async-start | bytes 1179648 | tf_op jit(solution)/shard_map/all_gather | solution.py:550
  85.3 10.9 %copy-start.2 = (bf16[768,4,128]{2,1,0:T(4,128)(2,1)}, bf16[768,4,128]{2,1,0:T(4,128)(2,1)S(1)}, u32[]{:S(2)}) copy-start(bf16[768,4,128]{2,1,0:T(4,128)(2,1)S(1)} %all-to-all-done.3) | copy-start | bytes 2359300
  85.3 17.5 %all-to-all-start = ((bf16[16,128,128]{2,1,0:T(8,128)(2,1)}), bf16[16,128,128]{2,1,0:T(8,128)(2,1)S(1)}, u32[]{:S(2)}, u32[]{:S(2)}) async-start(bf16[16,128,128]{2,1,0:T(8,128)(2,1)} %get-tuple-element.10), calls=%async_computation | async-start | bytes 1048576 | tf_op jit(solution)/shard_map/all_to_all | solution.py:410
  92.1 4.2 %collective-permute-start = (bf16[3072,128]{1,0:T(8,128)(2,1)S(1)}, bf16[3072,128]{1,0:T(8,128)(2,1)S(1)}, u32[]{:S(2)}, u32[]{:S(2)}) collective-permute-start(bf16[3072,128]{1,0:T(8,128)(2,1)S(1)} %bitcast.14), channel_id=1, source_target_pairs={{0,1},{1,0},{2,3},{3,2},{4,5},{5,4},{6,7},{7,6},{8,9},{9,8},{10,11... | collective-permute-start | bytes 2359304 | tf_op jit(solution)/shard_map/ppermute | solution.py:553
  96.2 0.9 copy-start.4
  102.9 11.7 %copy-start.3 = (bf16[16,128,128]{2,1,0:T(8,128)(2,1)}, bf16[16,128,128]{2,1,0:T(8,128)(2,1)S(1)}, u32[]{:S(2)}) copy-start(bf16[16,128,128]{2,1,0:T(8,128)(2,1)S(1)} %all-to-all-done.q_hbm) | copy-start | bytes 1572868
  102.9 25.0 %all-to-all-start.4 = ((bf16[256,4,128]{2,1,0:T(4,128)(2,1)}), bf16[256,4,128]{2,1,0:T(4,128)(2,1)S(1)}, u32[]{:S(2)}, u32[]{:S(2)}) async-start(bf16[256,4,128]{2,1,0:T(4,128)(2,1)} %bitcast.17), calls=%async_computation.4 | async-start | bytes 524288 | tf_op jit(solution)/shard_map/all_to_all | solution.py:410
  127.9 0.7 copy-start.1
  128.6 16.7 %all-to-all-start.2 = ((bf16[16,144,128]{2,1,0:T(8,128)(2,1)}), bf16[16,144,128]{2,1,0:T(8,128)(2,1)S(1)}, u32[]{:S(2)}, u32[]{:S(2)}) async-start(bf16[16,144,128]{2,1,0:T(8,128)(2,1)} %shard_map.39), calls=%async_computation.2 | async-start | bytes 1179648 | tf_op jit(solution)/shard_map/all_to_all | solution.py:410
  145.4 0.8 copy-start
Sparse Core Ops, SparseCore 0:
  64.8 37.8 all-gather.1

commit v4 on v3

--- a/solution.py
+++ b/solution.py
@@ -83,38 +83,45 @@
         move.wait()
 
 
-def pack_kernel(q_hbm, k_hbm, v_hbm, item_hbm, query_hbm, stack, items, sems, outs):
+def pack_kernel(q_hbm, k_hbm, v_hbm, item_hbm, query_hbm, qs, ks, vs, items, heads, ins, outs):
     def source(o):
         col = div12(o)
         rest = o - 12 * col
         return (rest >> 2) * POS + (rest & 3) * STRIDE + col
 
-    ins = []
+    def fetch(quad):
+        at = quad * 4 * HD
+        return [
+            pltpu.make_async_copy(
+                q_hbm.at[:, pl.ds(at + HD, 3 * HD)], qs.at[quad], ins.at[quad * 3]
+            ),
+            pltpu.make_async_copy(
+                k_hbm.at[:, pl.ds(at + HD, HD)], ks.at[quad], ins.at[quad * 3 + 1]
+            ),
+            pltpu.make_async_copy(
+                v_hbm.at[:, pl.ds(at + HD, HD)], vs.at[quad], ins.at[quad * 3 + 2]
+            ),
+        ]
+
     for quad in range(QUADS):
-        at = pl.ds((quad * 4 + 1) * HD, HD)
-        for a, ref in enumerate((q_hbm, k_hbm, v_hbm)):
-            move = pltpu.make_async_copy(
-                ref.at[:, at], stack.at[quad, pl.ds(a * POS, POS), :], sems.at[quad * 3 + a]
-            )
+        for move in fetch(quad):
             move.start()
-            ins.append(move)
+    perm = one_hot(384, 384, source)
     moves = []
-    for g in range(HEADS):
-        at = pl.ds(((g // 2) * 4 + 2 + g % 2) * HD, HD)
-        moves.append(
-            pltpu.make_async_copy(q_hbm.at[:, at], query_hbm.at[g], outs.at[QUADS + g])
-        )
-    perm = one_hot(384, 384, source)
     for quad in range(QUADS):
-        for a in range(3):
-            ins[quad * 3 + a].wait()
-        items[quad] = dot(perm, stack[quad]).astype(bf16)
-        move = pltpu.make_async_copy(items.at[quad], item_hbm.at[quad], outs.at[quad])
-        move.start()
-        if quad == 0:
-            for copy in moves:
-                copy.start()
-        moves.append(move)
+        for move in fetch(quad):
+            move.wait()
+        stack = jnp.concatenate([qs[quad, :, :HD], ks[quad], vs[quad]], axis=0)
+        items[quad] = dot(perm, stack).astype(bf16)
+        heads[quad * 2] = qs[quad, :, HD : 2 * HD]
+        heads[quad * 2 + 1] = qs[quad, :, 2 * HD :]
+        two = pl.ds(quad * 2, 2)
+        for move in (
+            pltpu.make_async_copy(items.at[quad], item_hbm.at[quad], outs.at[quad * 2]),
+            pltpu.make_async_copy(heads.at[two], query_hbm.at[two], outs.at[quad * 2 + 1]),
+        ):
+            move.start()
+            moves.append(move)
     for move in moves:
         move.wait()
 
@@ -237,8 +244,8 @@
         move.wait()
 
 
-FAR_Q = 512
-FAR_K = 1024
+FAR_Q = 1024
+FAR_K = 2048
 FAR_BLOCKS = PAIR // FAR_Q
 
 
@@ -385,7 +392,7 @@
         move.wait()
 
 
-SPACES = {"v": pltpu.VMEM, "s": pltpu.SMEM, "h": pltpu.HBM, "a": pl.ANY}
+SPACES = {"v": pltpu.VMEM, "s": pltpu.SMEM, "h": pl.ANY}
 
 
 def call(kernel, outs, args, ins, to="v", scratch=(), flops=0, moved=0, exps=0, alias=None):
@@ -442,10 +449,13 @@
         "hhh",
         to="h",
         scratch=[
+            pltpu.VMEM((QUADS, POS, 3 * HD), bf16),
+            pltpu.VMEM((QUADS, POS, HD), bf16),
+            pltpu.VMEM((QUADS, POS, HD), bf16),
             pltpu.VMEM((QUADS, 384, HD), bf16),
-            pltpu.VMEM((QUADS, 384, HD), bf16),
+            pltpu.VMEM((HEADS, POS, HD), bf16),
             dma(24),
-            dma(24),
+            dma(16),
         ],
         flops=2 * 8 * 384 * 384 * 128,
         moved=4 * mib,
@@ -454,7 +464,7 @@
 
 def ordered(after, items):
     return call(
-        order_kernel, [((QUADS, 384, HD), bf16)], (after, items), "aa", to="a", alias={1: 0}
+        order_kernel, [((QUADS, 384, HD), bf16)], (after, items), "hh", to="h", alias={1: 0}
     )
 
 

time: 157 us -> 143 us (0.911)
  Pallas kernels: 46.2 us -> 33.3 us
  starting transfers between devices: 60.1 us -> 54.9 us
  waiting for transfers between devices: 33.1 us -> 37.3 us
    pallas_call x7, Pallas kernels: 46.2 us -> 33.3 us  [call(): pl.pallas_call(kernel, out_shape=shapes if many else shapes[0], in_specs=...]
    all_to_all x5, starting transfers between devices: 58 us -> 52.8 us  [exchange(): return lax.all_to_all(array, axes, split_axis=0, concat_axis=0, tiled=True)]
    all_to_all x5, waiting for transfers between devices: 30.3 us -> 34.5 us  [exchange(): return lax.all_to_all(array, axes, split_axis=0, concat_axis=0, tiled=True)]
  transfers between devices with their start and end apart: 7 -> 7, of which waited for: 4 -> 5; matrix products, arithmetic and copies ran while one was open for 0% -> 0% of each run, Pallas kernels for 26% -> 20%
where the time goes in v4:
time: 143 us; the launch traced here: 142 us
  starting transfers between devices  54.9 us (38%)
  waiting for transfers between devices  37.3 us (26%)
  Pallas kernels  33.3 us (23%)
  between operations  13.5 us (9%)
  local copies, waits for them, and re-layouts  3.13 us (2%)
    all_to_all x5, starting transfers between devices, exchange(): return lax.all_to_all(array, axes, split_axis=0, concat_axis=0, tiled=True)  52.8 us
    all_to_all x5, waiting for transfers between devices, exchange(): return lax.all_to_all(array, axes, split_axis=0, concat_axis=0, tiled=True)  34.5 us
    pallas_call x7, Pallas kernels, call(): pl.pallas_call(kernel, out_shape=shapes if many else shapes[0], in_specs=...  33.3 us
  transfers between devices with their start and end apart: 7, of which 5 were waited for; matrix products, arithmetic and copies ran while one was open for 0% of the time, Pallas kernels for 20%

profile of v4, /device:TPU:1, one launch (start us, length us, event | category | flops | bytes accessed | tf_op | source)
XLA Modules:
  0.0 142.2 jit_solution(17073727737659674116)
XLA Ops:
  6.5 2.3 %shard_map.38 = bf16[64,8,128]{2,1,0:T(8,128)(2,1)} custom-call(bf16[128,4096]{1,0:T(8,128)(2,1)} %k_hbm.3, bf16[128,4096]{1,0:T(8,128)(2,1)} %v_hbm.3), custom_call_target="tpu_custom_call" | custom-call | flops 8388608 | bytes 1048576 | tf_op jit(solution)/shard_map/pallas_call | solution.py:404
  8.8 11.6 %all-to-all-start.1 = ((bf16[64,8,128]{2,1,0:T(8,128)(2,1)}), bf16[64,8,128]{2,1,0:T(8,128)(2,1)S(1)}, u32[]{:S(2)}, u32[]{:S(2)}) async-start(bf16[64,8,128]{2,1,0:T(8,128)(2,1)} %shard_map.38), calls=%async_computation.1 | async-start | bytes 262144 | tf_op jit(solution)/shard_map/all_to_all | solution.py:417
  20.5 4.0 %shard_map.37 = (bf16[8,384,128]{2,1,0:T(8,128)(2,1)}, bf16[16,128,128]{2,1,0:T(8,128)(2,1)}) custom-call(bf16[128,4096]{1,0:T(8,128)(2,1)} %q_hbm.3, bf16[128,4096]{1,0:T(8,128)(2,1)} %k_hbm.3, bf16[128,4096]{1,0:T(8,128)(2,1)} %v_hbm.3), custom_call_target="tpu_custom_call" | custom-call | flops 301989888 | bytes 4194304 | tf_op jit(solution)/shard_map/pallas_call | solution.py:404
  24.5 5.9 %all-to-all-done.1 = bf16[64,8,128]{2,1,0:T(8,128)(2,1)S(1)} async-done(((bf16[64,8,128]{2,1,0:T(8,128)(2,1)}), bf16[64,8,128]{2,1,0:T(8,128)(2,1)S(1)}, u32[]{:S(2)}, u32[]{:S(2)}) %all-to-all-start.1) | async-done | bytes 131104 | tf_op jit(solution)/shard_map/all_to_all | solution.py:417
  30.4 0.7 copy.6
  31.1 16.9 %all-to-all-start.3 = ((bf16[768,4,128]{2,1,0:T(4,128)(2,1)}), bf16[768,4,128]{2,1,0:T(4,128)(2,1)S(1)}, u32[]{:S(2)}, u32[]{:S(2)}) async-start(bf16[768,4,128]{2,1,0:T(4,128)(2,1)} %bitcast.10), calls=%async_computation.3 | async-start | bytes 1572864 | tf_op jit(solution)/shard_map/all_to_all | solution.py:417
  48.0 0.0 all-gather.2.cloned.1.call-start
  48.0 0.7 all-gather.2.cloned.1.call-update
  48.7 22.6 %all-to-all-done.3 = bf16[768,4,128]{2,1,0:T(4,128)(2,1)S(1)} async-done(((bf16[768,4,128]{2,1,0:T(4,128)(2,1)}), bf16[768,4,128]{2,1,0:T(4,128)(2,1)S(1)}, u32[]{:S(2)}, u32[]{:S(2)}) %all-to-all-start.3) | async-done | bytes 786464 | tf_op jit(solution)/shard_map/all_to_all | solution.py:417
  71.3 6.9 %all-to-all-start = ((bf16[16,128,128]{2,1,0:T(8,128)(2,1)}), bf16[16,128,128]{2,1,0:T(8,128)(2,1)S(1)}, u32[]{:S(2)}, u32[]{:S(2)}) async-start(bf16[16,128,128]{2,1,0:T(8,128)(2,1)} %get-tuple-element.10), calls=%async_computation | async-start | bytes 1048576 | tf_op jit(solution)/shard_map/all_to_all | solution.py:417
  78.2 2.0 %collective-permute-start = (bf16[3072,128]{1,0:T(8,128)(2,1)S(1)}, bf16[3072,128]{1,0:T(8,128)(2,1)S(1)}, u32[]{:S(2)}, u32[]{:S(2)}) collective-permute-start(bf16[3072,128]{1,0:T(8,128)(2,1)S(1)} %bitcast.14), channel_id=1, source_target_pairs={{0,1},{1,0},{2,3},{3,2},{4,5},{5,4},{6,7},{7,6},{8,9},{9,8},{10,11... | collective-permute-start | bytes 2359304 | tf_op jit(solution)/shard_map/ppermute | solution.py:563
  80.2 2.1 %collective-permute-done.other_hbm = bf16[3072,128]{1,0:T(8,128)(2,1)S(1)} collective-permute-done((bf16[3072,128]{1,0:T(8,128)(2,1)S(1)}, bf16[3072,128]{1,0:T(8,128)(2,1)S(1)}, u32[]{:S(2)}, u32[]{:S(2)}) %collective-permute-start) | collective-permute-done | bytes 786464 | tf_op jit(solution)/shard_map/ppermute | solution.py:563
  82.4 0.9 copy-done.4
  83.2 5.7 %shard_map.41 = bf16[4,256,128]{2,1,0:T(8,128)(2,1)} custom-call(s32[1]{0:T(128)} %bitcast.4.core_ref, bf16[3072,128]{1,0:T(8,128)(2,1)} %bitcast.15, bf16[3072,128]{1,0:T(8,128)(2,1)} %copy-done.4), custom_call_target="tpu_custom_call" | custom-call | flops 671088640 | bytes 2097152 | tf_op jit(solution)/shard_map/pallas_call | solution.py:404
  89.0 11.7 %all-to-all-start.4 = ((bf16[256,4,128]{2,1,0:T(4,128)(2,1)}), bf16[256,4,128]{2,1,0:T(4,128)(2,1)S(1)}, u32[]{:S(2)}, u32[]{:S(2)}) async-start(bf16[256,4,128]{2,1,0:T(4,128)(2,1)} %bitcast.17), calls=%async_computation.4 | async-start | bytes 524288 | tf_op jit(solution)/shard_map/all_to_all | solution.py:417
  100.6 0.0 all-gather.2.cloned.1.call-done.kv_hbm
  100.7 9.7 %shard_map.39 = bf16[16,144,128]{2,1,0:T(8,128)(2,1)} custom-call(s32[1]{0:T(128)} %bitcast.pair_ref, bf16[16,128,128]{2,1,0:T(8,128)(2,1)} %copy-done.3, bf16[8,2,256,128]{3,2,1,0:T(8,128)(2,1)} %all-gather.2.cloned.1.call-done.kv_hbm), custom_call_target="tpu_custom_call" | custom-call | flops 2147483648 | bytes 3145728 | tf_op jit(solution)/shard_map/pallas_call | solution.py:404
  110.4 3.7 %all-to-all-done.4 = bf16[256,4,128]{2,1,0:T(4,128)(2,1)S(1)} async-done(((bf16[256,4,128]{2,1,0:T(4,128)(2,1)}), bf16[256,4,128]{2,1,0:T(4,128)(2,1)S(1)}, u32[]{:S(2)}, u32[]{:S(2)}) %all-to-all-start.4) | async-done | bytes 262176 | tf_op jit(solution)/shard_map/all_to_all | solution.py:417
  114.1 0.7 copy-done.1
  114.8 5.8 %all-to-all-start.2 = ((bf16[16,144,128]{2,1,0:T(8,128)(2,1)}), bf16[16,144,128]{2,1,0:T(8,128)(2,1)S(1)}, u32[]{:S(2)}, u32[]{:S(2)}) async-start(bf16[16,144,128]{2,1,0:T(8,128)(2,1)} %shard_map.39), calls=%async_computation.2 | async-start | bytes 1179648 | tf_op jit(solution)/shard_map/all_to_all | solution.py:417
  120.6 8.6 %shard_map.42 = (bf16[8,128,128]{2,1,0:T(8,128)(2,1)}, f32[16,128,128]{2,1,0:T(8,128)}, f32[2,128,128]{2,1,0:T(8,128)}) custom-call(bf16[128,4096]{1,0:T(8,128)(2,1)} %q_hbm.3, bf16[128,4096]{1,0:T(8,128)(2,1)} %k_hbm.3, bf16[128,4096]{1,0:T(8,128)(2,1)} %v_hbm.3), custom_call_target="tpu_custom_call" | custom-call | flops 201326592 | bytes 5242880 | tf_op jit(solution)/shard_map/pallas_call | solution.py:404
  129.2 2.3 %all-to-all-done.2.far_hbm = bf16[16,144,128]{2,1,0:T(8,128)(2,1)S(1)} async-done(((bf16[16,144,128]{2,1,0:T(8,128)(2,1)}), bf16[16,144,128]{2,1,0:T(8,128)(2,1)S(1)}, u32[]{:S(2)}, u32[]{:S(2)}) %all-to-all-start.2) | async-done | bytes 589856 | tf_op jit(solution)/shard_map/all_to_all | solution.py:417
  131.5 0.8 copy-done
  132.3 3.0 %shard_map.43 = bf16[128,4096]{1,0:T(8,128)(2,1)} custom-call(bf16[16,144,128]{2,1,0:T(8,128)(2,1)} %copy-done, bf16[4,256,128]{2,1,0:T(8,128)(2,1)} %bitcast.13, bf16[8,128,128]{2,1,0:T(8,128)(2,1)} %get-tuple-element.12.row_hbm, f32[16,128,128]{2,1,0:T(8,128)} %get-tuple-element.13.part_hbm, f32[2,128,128]{2,1,0:T(8,128)} %get-tuple-element.14.stat_hbm), custom_call_target="tpu_custom_call" | custom-call | flops 33554432 | bytes 4194304 | tf_op jit(solution)/shard_map/pallas_call | solution.py:404
  (9 shorter events, 0.0 us)
Async XLA Ops:
  8.8 21.6 %all-to-all-start.1 = ((bf16[64,8,128]{2,1,0:T(8,128)(2,1)}), bf16[64,8,128]{2,1,0:T(8,128)(2,1)S(1)}, u32[]{:S(2)}, u32[]{:S(2)}) async-start(bf16[64,8,128]{2,1,0:T(8,128)(2,1)} %shard_map.38), calls=%async_computation.1 | async-start | bytes 262144 | tf_op jit(solution)/shard_map/all_to_all | solution.py:417
  31.1 40.2 %all-to-all-start.3 = ((bf16[768,4,128]{2,1,0:T(4,128)(2,1)}), bf16[768,4,128]{2,1,0:T(4,128)(2,1)S(1)}, u32[]{:S(2)}, u32[]{:S(2)}) async-start(bf16[768,4,128]{2,1,0:T(4,128)(2,1)} %bitcast.10), calls=%async_computation.3 | async-start | bytes 1572864 | tf_op jit(solution)/shard_map/all_to_all | solution.py:417
  48.0 52.7 %all-gather.2.cloned.1.call-start = ((), (), s32[]{:S(2)}) async-start(), calls=%async_computation.5 | async-start | bytes 1179648 | tf_op jit(solution)/shard_map/all_gather | solution.py:560
  71.3 11.1 %copy-start.2 = (bf16[768,4,128]{2,1,0:T(4,128)(2,1)}, bf16[768,4,128]{2,1,0:T(4,128)(2,1)S(1)}, u32[]{:S(2)}) copy-start(bf16[768,4,128]{2,1,0:T(4,128)(2,1)S(1)} %all-to-all-done.3) | copy-start | bytes 2359300
  71.3 17.7 %all-to-all-start = ((bf16[16,128,128]{2,1,0:T(8,128)(2,1)}), bf16[16,128,128]{2,1,0:T(8,128)(2,1)S(1)}, u32[]{:S(2)}, u32[]{:S(2)}) async-start(bf16[16,128,128]{2,1,0:T(8,128)(2,1)} %get-tuple-element.10), calls=%async_computation | async-start | bytes 1048576 | tf_op jit(solution)/shard_map/all_to_all | solution.py:417
  78.2 4.2 %collective-permute-start = (bf16[3072,128]{1,0:T(8,128)(2,1)S(1)}, bf16[3072,128]{1,0:T(8,128)(2,1)S(1)}, u32[]{:S(2)}, u32[]{:S(2)}) collective-permute-start(bf16[3072,128]{1,0:T(8,128)(2,1)S(1)} %bitcast.14), channel_id=1, source_target_pairs={{0,1},{1,0},{2,3},{3,2},{4,5},{5,4},{6,7},{7,6},{8,9},{9,8},{10,11... | collective-permute-start | bytes 2359304 | tf_op jit(solution)/shard_map/ppermute | solution.py:563
  82.3 0.9 copy-start.4
  89.0 11.7 %copy-start.3 = (bf16[16,128,128]{2,1,0:T(8,128)(2,1)}, bf16[16,128,128]{2,1,0:T(8,128)(2,1)S(1)}, u32[]{:S(2)}) copy-start(bf16[16,128,128]{2,1,0:T(8,128)(2,1)S(1)} %all-to-all-done.q_hbm) | copy-start | bytes 1572868
  89.0 25.1 %all-to-all-start.4 = ((bf16[256,4,128]{2,1,0:T(4,128)(2,1)}), bf16[256,4,128]{2,1,0:T(4,128)(2,1)S(1)}, u32[]{:S(2)}, u32[]{:S(2)}) async-start(bf16[256,4,128]{2,1,0:T(4,128)(2,1)} %bitcast.17), calls=%async_computation.4 | async-start | bytes 524288 | tf_op jit(solution)/shard_map/all_to_all | solution.py:417
  114.1 0.7 copy-start.1
  114.8 16.7 %all-to-all-start.2 = ((bf16[16,144,128]{2,1,0:T(8,128)(2,1)}), bf16[16,144,128]{2,1,0:T(8,128)(2,1)S(1)}, u32[]{:S(2)}, u32[]{:S(2)}) async-start(bf16[16,144,128]{2,1,0:T(8,128)(2,1)} %shard_map.39), calls=%async_computation.2 | async-start | bytes 1179648 | tf_op jit(solution)/shard_map/all_to_all | solution.py:417
  131.5 0.8 copy-start
Sparse Core Ops, SparseCore 0:
  50.9 38.0 all-gather.1

commit v5 on v4

--- a/solution.py
+++ b/solution.py
@@ -176,13 +176,9 @@
 
 
 def column_kernel(
-    core_ref, own_hbm, other_hbm, out_hbm, own_ref, other_ref, out_scr, q_scr, k_scr, v_scr, sems
+    core_ref, after_ref, own_ref, other_ref, out_hbm, out_scr, q_scr, k_scr, v_scr, sems
 ):
     core = core_ref[0]
-    own_in = pltpu.make_async_copy(own_hbm, own_ref, sems.at[0])
-    other_in = pltpu.make_async_copy(other_hbm, other_ref, sems.at[1])
-    own_in.start()
-    other_in.start()
 
     def source(o):
         within = o & 31
@@ -191,16 +187,12 @@
     split = one_hot(96, 96, source)
     split_kv = one_hot(64, 96, lambda o: source(o + 32))
     by_x = one_hot(POS, POS, lambda o: ((o >> 2) & 7) * 16 + (o >> 5) * 4 + (o & 3))
-    own_in.wait()
     for g in range(32):
         at = slice(g * 32, (g + 1) * 32)
         y = dot(split, own_ref[g * 96 : (g + 1) * 96, :]).astype(bf16)
         q_scr[at, :] = y[0:32]
         k_scr[0, at, :] = y[32:64]
         v_scr[0, at, :] = y[64:96]
-    other_in.wait()
-    for g in range(32):
-        at = slice(g * 32, (g + 1) * 32)
         y = dot(split_kv, other_ref[g * 96 : (g + 1) * 96, :]).astype(bf16)
         k_scr[1, at, :] = y[0:32]
         v_scr[1, at, :] = y[32:64]
@@ -237,7 +229,7 @@
             for x in range(4):
                 out_scr[x, at : at + STRIDE, :] = y[x * STRIDE : (x + 1) * STRIDE]
         at = pl.ds(qb * block // 4, block // 4)
-        move = pltpu.make_async_copy(out_scr.at[:, at, :], out_hbm.at[:, at, :], sems.at[2 + qb])
+        move = pltpu.make_async_copy(out_scr.at[:, at, :], out_hbm.at[:, at, :], sems.at[qb])
         move.start()
         moves.append(move)
     for move in moves:
@@ -336,15 +328,13 @@
 
 
 def final_kernel(
-    far_hbm, col_hbm, row_hbm, part_hbm, stat_hbm, out_hbm,
-    far_ref, col_ref, row_ref, part_ref, stat_ref, out_ref, sems,
+    far_ref, col_ref, row_hbm, part_hbm, stat_hbm, out_hbm,
+    row_ref, part_ref, stat_ref, out_ref, sems,
 ):
     ins = [
-        pltpu.make_async_copy(far_hbm, far_ref, sems.at[0]),
-        pltpu.make_async_copy(stat_hbm, stat_ref, sems.at[12]),
+        pltpu.make_async_copy(stat_hbm, stat_ref, sems.at[0]),
         pltpu.make_async_copy(part_hbm, part_ref, sems.at[1]),
-        pltpu.make_async_copy(col_hbm, col_ref, sems.at[2]),
-        pltpu.make_async_copy(row_hbm, row_ref, sems.at[3]),
+        pltpu.make_async_copy(row_hbm, row_ref, sems.at[2]),
     ]
     for move in ins:
         move.start()
@@ -357,7 +347,6 @@
         jnp.logical_and((row >> 4) == lane, (row & 15) < 3), 1.0, 0.0
     ).astype(bf16)
     ins[0].wait()
-    ins[1].wait()
     terms = jnp.concatenate([far_ref[g, POS:, :] for g in range(HEADS)], axis=0)
     lse = dot_tl(terms, pick)
     top = jnp.maximum(stat_ref[0], lse)
@@ -366,7 +355,7 @@
     scale = 1.0 / (stat_ref[1] * own + far)
     own = own * scale
     far = far * scale
-    for move in ins[2:]:
+    for move in ins[1:]:
         move.wait()
     moves = []
     for quad in range(QUADS):
@@ -385,17 +374,18 @@
             start = base + (2 + h) * HD
             out_ref[:, start : start + HD] = merged.astype(bf16)
         at = pl.ds(base, 4 * HD)
-        move = pltpu.make_async_copy(out_ref.at[:, at], out_hbm.at[:, at], sems.at[4 + quad])
+        move = pltpu.make_async_copy(out_ref.at[:, at], out_hbm.at[:, at], sems.at[3 + quad])
         move.start()
         moves.append(move)
     for move in moves:
         move.wait()
 
 
+VMEM_BYTES = 63_000_000
 SPACES = {"v": pltpu.VMEM, "s": pltpu.SMEM, "h": pl.ANY}
 
 
-def call(kernel, outs, args, ins, to="v", scratch=(), flops=0, moved=0, exps=0, alias=None):
+def call(kernel, outs, args, ins, to="v", scratch=(), flops=0, moved=0, exps=0, alias=None, room=0):
     def spec(space):
         return pl.BlockSpec(memory_space=SPACES[space])
 
@@ -408,7 +398,7 @@
         out_specs=[spec(to)] * len(shapes) if many else spec(to),
         scratch_shapes=list(scratch),
         input_output_aliases=alias or {},
-        compiler_params=pltpu.CompilerParams(vmem_limit_bytes=60 * 1024 * 1024),
+        compiler_params=pltpu.CompilerParams(vmem_limit_bytes=VMEM_BYTES - room),
         cost_estimate=pl.CostEstimate(flops=flops, bytes_accessed=moved, transcendentals=exps),
     )(*args)
 
@@ -479,28 +469,28 @@
         scratch=[pltpu.VMEM((POS, QUADS * 4 * HD), bf16)] * 3
         + [pltpu.VMEM(*out) for out in outs]
         + [dma(13)],
+        room=1_250_000,
         flops=24 * 4 * 128 * 128 * 128,
         moved=5 * mib,
         exps=24 * 128 * 128,
     )
 
 
-def columns(core, items, other):
+def columns(core, after, items, other):
     return call(
         column_kernel,
         [((4, 256, HD), bf16)],
-        (core, items, other),
-        "shh",
+        (core, after, items, other),
+        "shvv",
         to="h",
         scratch=[
-            pltpu.VMEM((3072, HD), bf16),
-            pltpu.VMEM((3072, HD), bf16),
             pltpu.VMEM((4, 256, HD), bf16),
             pltpu.VMEM((1024, HD), bf16),
             pltpu.VMEM((2, 1024, HD), bf16),
             pltpu.VMEM((2, 1024, HD), bf16),
-            dma(6),
+            dma(4),
         ],
+        room=1_250_000,
         flops=4 * 1024 * 1280 * 128,
         moved=2 * mib,
         exps=1024 * 1280,
@@ -532,17 +522,16 @@
         final_kernel,
         [((POS, QUADS * 4 * HD), bf16)],
         (far, column, row_out, part, stat),
-        "hhhhh",
+        "vvhhh",
         to="h",
         scratch=[
-            pltpu.VMEM((HEADS, PAY, HD), bf16),
-            pltpu.VMEM((4, 256, HD), bf16),
             pltpu.VMEM((QUADS, POS, HD), bf16),
             pltpu.VMEM((HEADS, POS, HD), f32),
             pltpu.VMEM((2, POS, 128), f32),
             pltpu.VMEM((POS, QUADS * 4 * HD), bf16),
-            dma(13),
+            dma(11),
         ],
+        room=500_000,
         flops=2 * 8 * 128 * 128 * 128,
         moved=4 * mib,
     )
@@ -562,9 +551,9 @@
     heads = exchange(heads, heads_at)
     other = lax.ppermute(items, "c", [(0, 1), (1, 0)])
     core = lax.axis_index("c").astype(jnp.int32).reshape(1)
-    column = columns(core, items, other)
+    row_out, part, stat = rows(queries, keys, values)
+    column = columns(core, stat, items, other)
     column = exchange(column.reshape(256, ROWS, HD), back).reshape(4, 256, HD)
-    row_out, part, stat = rows(queries, keys, values)
     pair = lax.axis_index(("z", "u", "v")).astype(jnp.int32).reshape(1)
     far = exchange(far_part(pair, heads, summary), heads_at)
     return final(far, column, row_out, part, stat)

time: 143 us -> 150 us (1.049)
  blocking collectives: 0 us -> 17.2 us
  starting transfers between devices: 54.9 us -> 49.5 us
  waiting for transfers between devices: 37.3 us -> 33.2 us
  local copies, waits for them, and re-layouts: 3.13 us -> 1.58 us
    all_to_all x0 -> x1, blocking collectives: none -> 17.2 us  [exchange(): return lax.all_to_all(array, axes, split_axis=0, concat_axis=0, tiled=True)]
    all_to_all x5 -> x4, starting transfers between devices: 52.8 us -> 47.3 us  [exchange(): return lax.all_to_all(array, axes, split_axis=0, concat_axis=0, tiled=True)]
    ppermute x1, waiting for transfers between devices: 2.15 us -> 0.01 us  [body(): other = lax.ppermute(items, 'c', [(0, 1), (1, 0)])]
    all_to_all x5 -> x4, waiting for transfers between devices: 34.5 us -> 32.5 us  [exchange(): return lax.all_to_all(array, axes, split_axis=0, concat_axis=0, tiled=True)]
    unnamed x10 -> x8, local copies, waits for them, and re-layouts: 2.43 us -> 0.89 us
  transfers between devices with their start and end apart: 7 -> 6, of which waited for: 5 -> 3; matrix products, arithmetic and copies ran while one was open for 0% -> 0% of each run, Pallas kernels for 20% -> 19%
where the time goes in v5:
time: 150 us; the launch traced here: 149 us
  starting transfers between devices  49.5 us (33%)
  Pallas kernels  34.2 us (23%)
  waiting for transfers between devices  33.2 us (22%)
  blocking collectives  17.2 us (11%)
  between operations  13.6 us (9%)
  local copies, waits for them, and re-layouts  1.58 us (1%)
    all_to_all x4, starting transfers between devices, exchange(): return lax.all_to_all(array, axes, split_axis=0, concat_axis=0, tiled=True)  47.3 us
    pallas_call x7, Pallas kernels, call(): pl.pallas_call(kernel, out_shape=shapes if many else shapes[0], in_specs=...  34.2 us
    all_to_all x4, waiting for transfers between devices, exchange(): return lax.all_to_all(array, axes, split_axis=0, concat_axis=0, tiled=True)  32.5 us
    all_to_all x1, blocking collectives, exchange(): return lax.all_to_all(array, axes, split_axis=0, concat_axis=0, tiled=True)  17.2 us
  transfers between devices with their start and end apart: 6, of which 3 were waited for; matrix products, arithmetic and copies ran while one was open for 0% of the time, Pallas kernels for 19%

profile of v5, /device:TPU:1, one launch (start us, length us, event | category | flops | bytes accessed | tf_op | source)
XLA Modules:
  0.0 149.3 jit_solution(10700294292635687923)
XLA Ops:
  6.5 2.3 %shard_map.38 = bf16[64,8,128]{2,1,0:T(8,128)(2,1)} custom-call(bf16[128,4096]{1,0:T(8,128)(2,1)} %k_hbm.3, bf16[128,4096]{1,0:T(8,128)(2,1)} %v_hbm.3), custom_call_target="tpu_custom_call" | custom-call | flops 8388608 | bytes 1048576 | tf_op jit(solution)/shard_map/pallas_call | solution.py:394
  8.8 11.6 %all-to-all-start.1 = ((bf16[64,8,128]{2,1,0:T(8,128)(2,1)}), bf16[64,8,128]{2,1,0:T(8,128)(2,1)S(1)}, u32[]{:S(2)}, u32[]{:S(2)}) async-start(bf16[64,8,128]{2,1,0:T(8,128)(2,1)} %shard_map.38), calls=%async_computation.1 | async-start | bytes 262144 | tf_op jit(solution)/shard_map/all_to_all | solution.py:407
  20.5 4.0 %shard_map.37 = (bf16[8,384,128]{2,1,0:T(8,128)(2,1)}, bf16[16,128,128]{2,1,0:T(8,128)(2,1)}) custom-call(bf16[128,4096]{1,0:T(8,128)(2,1)} %q_hbm.3, bf16[128,4096]{1,0:T(8,128)(2,1)} %k_hbm.3, bf16[128,4096]{1,0:T(8,128)(2,1)} %v_hbm.3), custom_call_target="tpu_custom_call" | custom-call | flops 301989888 | bytes 4194304 | tf_op jit(solution)/shard_map/pallas_call | solution.py:394
  24.5 5.9 %all-to-all-done.1 = bf16[64,8,128]{2,1,0:T(8,128)(2,1)S(1)} async-done(((bf16[64,8,128]{2,1,0:T(8,128)(2,1)}), bf16[64,8,128]{2,1,0:T(8,128)(2,1)S(1)}, u32[]{:S(2)}, u32[]{:S(2)}) %all-to-all-start.1) | async-done | bytes 131104 | tf_op jit(solution)/shard_map/all_to_all | solution.py:407
  30.4 0.7 copy.6
  31.1 16.9 %all-to-all-start.3 = ((bf16[768,4,128]{2,1,0:T(4,128)(2,1)}), bf16[768,4,128]{2,1,0:T(4,128)(2,1)S(1)}, u32[]{:S(2)}, u32[]{:S(2)}) async-start(bf16[768,4,128]{2,1,0:T(4,128)(2,1)} %bitcast.10), calls=%async_computation.3 | async-start | bytes 1572864 | tf_op jit(solution)/shard_map/all_to_all | solution.py:407
  48.0 0.0 all-gather.2.cloned.1.call-start
  48.0 0.7 all-gather.2.cloned.1.call-update
  48.7 22.6 %all-to-all-done.3 = bf16[768,4,128]{2,1,0:T(4,128)(2,1)S(1)} async-done(((bf16[768,4,128]{2,1,0:T(4,128)(2,1)}), bf16[768,4,128]{2,1,0:T(4,128)(2,1)S(1)}, u32[]{:S(2)}, u32[]{:S(2)}) %all-to-all-start.3) | async-done | bytes 786464 | tf_op jit(solution)/shard_map/all_to_all | solution.py:407
  71.3 6.9 %all-to-all-start = ((bf16[16,128,128]{2,1,0:T(8,128)(2,1)}), bf16[16,128,128]{2,1,0:T(8,128)(2,1)S(1)}, u32[]{:S(2)}, u32[]{:S(2)}) async-start(bf16[16,128,128]{2,1,0:T(8,128)(2,1)} %get-tuple-element.10), calls=%async_computation | async-start | bytes 1048576 | tf_op jit(solution)/shard_map/all_to_all | solution.py:407
  78.2 2.2 %collective-permute-start = (bf16[3072,128]{1,0:T(8,128)(2,1)S(1)}, bf16[3072,128]{1,0:T(8,128)(2,1)S(1)}, u32[]{:S(2)}, u32[]{:S(2)}) collective-permute-start(bf16[3072,128]{1,0:T(8,128)(2,1)S(1)} %bitcast.14), channel_id=1, source_target_pairs={{0,1},{1,0},{2,3},{3,2},{4,5},{5,4},{6,7},{7,6},{8,9},{9,8},{10,11... | collective-permute-start | bytes 2359304 | tf_op jit(solution)/shard_map/ppermute | solution.py:552
  80.4 8.6 %shard_map.40 = (bf16[8,128,128]{2,1,0:T(8,128)(2,1)}, f32[16,128,128]{2,1,0:T(8,128)}, f32[2,128,128]{2,1,0:T(8,128)}) custom-call(bf16[128,4096]{1,0:T(8,128)(2,1)} %q_hbm.3, bf16[128,4096]{1,0:T(8,128)(2,1)} %k_hbm.3, bf16[128,4096]{1,0:T(8,128)(2,1)} %v_hbm.3), custom_call_target="tpu_custom_call" | custom-call | flops 201326592 | bytes 5242880 | tf_op jit(solution)/shard_map/pallas_call | solution.py:394
  89.0 0.0 copy-done.1
  89.0 0.0 collective-permute-done.other_ref
  89.0 0.0 copy-start.3
  89.1 0.9 copy-done.3
  89.9 5.7 %shard_map.42 = bf16[4,256,128]{2,1,0:T(8,128)(2,1)} custom-call(s32[1]{0:T(128)} %bitcast.4.core_ref, f32[2,128,128]{2,1,0:T(8,128)} %get-tuple-element.11.after_ref.stat_hbm, bf16[3072,128]{1,0:T(8,128)(2,1)} %bitcast.15, bf16[3072,128]{1,0:T(8,128)(2,1)} %copy-done.3), custom_call_target="tpu_custom_call" | custom-call | flops 671088640 | bytes 2097152 | tf_op jit(solution)/shard_map/pallas_call | solution.py:394
  95.7 0.0 all-to-all-done.q_hbm
  95.7 11.9 %all-to-all-start.4 = ((bf16[256,4,128]{2,1,0:T(4,128)(2,1)}), bf16[256,4,128]{2,1,0:T(4,128)(2,1)S(1)}, u32[]{:S(2)}, u32[]{:S(2)}) async-start(bf16[256,4,128]{2,1,0:T(4,128)(2,1)} %bitcast.17), calls=%async_computation.4 | async-start | bytes 524288 | tf_op jit(solution)/shard_map/all_to_all | solution.py:407
  107.6 0.0 all-gather.2.cloned.1.call-done.kv_hbm
  107.7 9.7 %shard_map.39 = bf16[16,144,128]{2,1,0:T(8,128)(2,1)} custom-call(s32[1]{0:T(128)} %bitcast.pair_ref, bf16[16,128,128]{2,1,0:T(8,128)(2,1)} %copy-done.2, bf16[8,2,256,128]{3,2,1,0:T(8,128)(2,1)} %all-gather.2.cloned.1.call-done.kv_hbm), custom_call_target="tpu_custom_call" | custom-call | flops 2147483648 | bytes 3145728 | tf_op jit(solution)/shard_map/pallas_call | solution.py:394
  117.4 4.0 %all-to-all-done.4 = bf16[256,4,128]{2,1,0:T(4,128)(2,1)S(1)} async-done(((bf16[256,4,128]{2,1,0:T(4,128)(2,1)}), bf16[256,4,128]{2,1,0:T(4,128)(2,1)S(1)}, u32[]{:S(2)}, u32[]{:S(2)}) %all-to-all-start.4) | async-done | bytes 262176 | tf_op jit(solution)/shard_map/all_to_all | solution.py:407
  121.4 17.2 %all_to_all.25.far_ref = bf16[16,144,128]{2,1,0:T(8,128)(2,1)} all-to-all(bf16[16,144,128]{2,1,0:T(8,128)(2,1)} %shard_map.39), channel_id=1, replica_groups=mesh['x'=4,'z'=8,'u'=2,'v'=2,'w'=2,'c'=2] {'w','c','x'}, dimensions={0} | all-to-all | bytes 1179648 | tf_op jit(solution)/shard_map/all_to_all | solution.py:407
  138.6 3.9 %shard_map.43 = bf16[128,4096]{1,0:T(8,128)(2,1)} custom-call(bf16[16,144,128]{2,1,0:T(8,128)(2,1)} %all_to_all.25.far_ref, bf16[4,256,128]{2,1,0:T(8,128)(2,1)} %bitcast.13, bf16[8,128,128]{2,1,0:T(8,128)(2,1)} %get-tuple-element.13.row_hbm, f32[16,128,128]{2,1,0:T(8,128)} %get-tuple-element.14.part_hbm, f32[2,128,128]{2,1,0:T(8,128)} %get-tuple-element.11.after_ref.stat_hbm), custom_call_target="tpu_custom_call" | custom-call | flops 33554432 | bytes 4194304 | tf_op jit(solution)/shard_map/pallas_call | solution.py:394
  (6 shorter events, 0.0 us)
Async XLA Ops:
  8.8 21.6 %all-to-all-start.1 = ((bf16[64,8,128]{2,1,0:T(8,128)(2,1)}), bf16[64,8,128]{2,1,0:T(8,128)(2,1)S(1)}, u32[]{:S(2)}, u32[]{:S(2)}) async-start(bf16[64,8,128]{2,1,0:T(8,128)(2,1)} %shard_map.38), calls=%async_computation.1 | async-start | bytes 262144 | tf_op jit(solution)/shard_map/all_to_all | solution.py:407
  31.1 40.2 %all-to-all-start.3 = ((bf16[768,4,128]{2,1,0:T(4,128)(2,1)}), bf16[768,4,128]{2,1,0:T(4,128)(2,1)S(1)}, u32[]{:S(2)}, u32[]{:S(2)}) async-start(bf16[768,4,128]{2,1,0:T(4,128)(2,1)} %bitcast.10), calls=%async_computation.3 | async-start | bytes 1572864 | tf_op jit(solution)/shard_map/all_to_all | solution.py:407
  48.0 59.7 %all-gather.2.cloned.1.call-start = ((), (), s32[]{:S(2)}) async-start(), calls=%async_computation.5 | async-start | bytes 1179648 | tf_op jit(solution)/shard_map/all_gather | solution.py:549
  71.3 17.7 %copy-start.1 = (bf16[768,4,128]{2,1,0:T(4,128)(2,1)}, bf16[768,4,128]{2,1,0:T(4,128)(2,1)S(1)}, u32[]{:S(2)}) copy-start(bf16[768,4,128]{2,1,0:T(4,128)(2,1)S(1)} %all-to-all-done.3) | copy-start | bytes 2359300
  71.3 24.4 %all-to-all-start = ((bf16[16,128,128]{2,1,0:T(8,128)(2,1)}), bf16[16,128,128]{2,1,0:T(8,128)(2,1)S(1)}, u32[]{:S(2)}, u32[]{:S(2)}) async-start(bf16[16,128,128]{2,1,0:T(8,128)(2,1)} %get-tuple-element.10), calls=%async_computation | async-start | bytes 1048576 | tf_op jit(solution)/shard_map/all_to_all | solution.py:407
  78.2 10.9 %collective-permute-start = (bf16[3072,128]{1,0:T(8,128)(2,1)S(1)}, bf16[3072,128]{1,0:T(8,128)(2,1)S(1)}, u32[]{:S(2)}, u32[]{:S(2)}) collective-permute-start(bf16[3072,128]{1,0:T(8,128)(2,1)S(1)} %bitcast.14), channel_id=1, source_target_pairs={{0,1},{1,0},{2,3},{3,2},{4,5},{5,4},{6,7},{7,6},{8,9},{9,8},{10,11... | collective-permute-start | bytes 2359304 | tf_op jit(solution)/shard_map/ppermute | solution.py:552
  89.0 0.9 copy-start.3
  95.7 12.0 %copy-start.2 = (bf16[16,128,128]{2,1,0:T(8,128)(2,1)}, bf16[16,128,128]{2,1,0:T(8,128)(2,1)S(1)}, u32[]{:S(2)}) copy-start(bf16[16,128,128]{2,1,0:T(8,128)(2,1)S(1)} %all-to-all-done.q_hbm) | copy-start | bytes 1572868
  95.7 25.7 %all-to-all-start.4 = ((bf16[256,4,128]{2,1,0:T(4,128)(2,1)}), bf16[256,4,128]{2,1,0:T(4,128)(2,1)S(1)}, u32[]{:S(2)}, u32[]{:S(2)}) async-start(bf16[256,4,128]{2,1,0:T(4,128)(2,1)} %bitcast.17), calls=%async_computation.4 | async-start | bytes 524288 | tf_op jit(solution)/shard_map/all_to_all | solution.py:407
  121.4 17.2 %copy-start = (bf16[256,4,128]{2,1,0:T(4,128)(2,1)}, bf16[256,4,128]{2,1,0:T(4,128)(2,1)S(1)}, u32[]{:S(2)}) copy-start(bf16[256,4,128]{2,1,0:T(4,128)(2,1)S(1)} %all-to-all-done.4) | copy-start | bytes 786436
Sparse Core Ops, SparseCore 0:
  50.9 38.0 all-gather.1

commit v6 on v5

--- a/solution.py
+++ b/solution.py
@@ -176,7 +176,7 @@
 
 
 def column_kernel(
-    core_ref, after_ref, own_ref, other_ref, out_hbm, out_scr, q_scr, k_scr, v_scr, sems
+    core_ref, own_ref, other_ref, out_hbm, out_scr, q_scr, k_scr, v_scr, sems
 ):
     core = core_ref[0]
 
@@ -476,12 +476,12 @@
     )
 
 
-def columns(core, after, items, other):
+def columns(core, items, other):
     return call(
         column_kernel,
         [((4, 256, HD), bf16)],
-        (core, after, items, other),
-        "shvv",
+        (core, items, other),
+        "svv",
         to="h",
         scratch=[
             pltpu.VMEM((4, 256, HD), bf16),
@@ -490,7 +490,7 @@
             pltpu.VMEM((2, 1024, HD), bf16),
             dma(4),
         ],
-        room=1_250_000,
+        room=2_600_000,
         flops=4 * 1024 * 1280 * 128,
         moved=2 * mib,
         exps=1024 * 1280,
@@ -551,11 +551,11 @@
     heads = exchange(heads, heads_at)
     other = lax.ppermute(items, "c", [(0, 1), (1, 0)])
     core = lax.axis_index("c").astype(jnp.int32).reshape(1)
-    row_out, part, stat = rows(queries, keys, values)
-    column = columns(core, stat, items, other)
+    column = columns(core, items, other)
     column = exchange(column.reshape(256, ROWS, HD), back).reshape(4, 256, HD)
     pair = lax.axis_index(("z", "u", "v")).astype(jnp.int32).reshape(1)
     far = exchange(far_part(pair, heads, summary), heads_at)
+    row_out, part, stat = rows(queries, keys, values)
     return final(far, column, row_out, part, stat)
 
 

time: 150 us -> 144 us (0.960)
  blocking collectives: 17.2 us -> 0 us
  starting transfers between devices: 49.5 us -> 54.9 us
  waiting for transfers between devices: 33.2 us -> 37.4 us
  local copies, waits for them, and re-layouts: 1.58 us -> 3.13 us
    all_to_all x1 -> x0, blocking collectives: 17.2 us -> none  [exchange(): return lax.all_to_all(array, axes, split_axis=0, concat_axis=0, tiled=True)]
    all_to_all x4 -> x5, starting transfers between devices: 47.3 us -> 52.8 us  [exchange(): return lax.all_to_all(array, axes, split_axis=0, concat_axis=0, tiled=True)]
    ppermute x1, waiting for transfers between devices: 0.01 us -> 2.15 us  [body(): other = lax.ppermute(items, 'c', [(0, 1), (1, 0)])]
    all_to_all x4 -> x5, waiting for transfers between devices: 32.5 us -> 34.5 us  [exchange(): return lax.all_to_all(array, axes, split_axis=0, concat_axis=0, tiled=True)]
    unnamed x8 -> x10, local copies, waits for them, and re-layouts: 0.89 us -> 2.43 us
  transfers between devices with their start and end apart: 6 -> 7, of which waited for: 3 -> 5; matrix products, arithmetic and copies ran while one was open for 0% -> 0% of each run, Pallas kernels for 19% -> 20%
where the time goes in v6:
time: 144 us; the launch traced here: 143 us
  starting transfers between devices  54.9 us (38%)
  waiting for transfers between devices  37.4 us (26%)
  Pallas kernels  34.2 us (24%)
  between operations  13.5 us (9%)
  local copies, waits for them, and re-layouts  3.13 us (2%)
    all_to_all x5, starting transfers between devices, exchange(): return lax.all_to_all(array, axes, split_axis=0, concat_axis=0, tiled=True)  52.8 us
    all_to_all x5, waiting for transfers between devices, exchange(): return lax.all_to_all(array, axes, split_axis=0, concat_axis=0, tiled=True)  34.5 us
    pallas_call x7, Pallas kernels, call(): pl.pallas_call(kernel, out_shape=shapes if many else shapes[0], in_specs=...  34.2 us
  transfers between devices with their start and end apart: 7, of which 5 were waited for; matrix products, arithmetic and copies ran while one was open for 0% of the time, Pallas kernels for 20%

profile of v6, /device:TPU:1, one launch (start us, length us, event | category | flops | bytes accessed | tf_op | source)
XLA Modules:
  0.0 143.1 jit_solution(12927146054212138338)
XLA Ops:
  6.5 2.3 %shard_map.38 = bf16[64,8,128]{2,1,0:T(8,128)(2,1)} custom-call(bf16[128,4096]{1,0:T(8,128)(2,1)} %k_hbm.3, bf16[128,4096]{1,0:T(8,128)(2,1)} %v_hbm.3), custom_call_target="tpu_custom_call" | custom-call | flops 8388608 | bytes 1048576 | tf_op jit(solution)/shard_map/pallas_call | solution.py:394
  8.8 11.6 %all-to-all-start.1 = ((bf16[64,8,128]{2,1,0:T(8,128)(2,1)}), bf16[64,8,128]{2,1,0:T(8,128)(2,1)S(1)}, u32[]{:S(2)}, u32[]{:S(2)}) async-start(bf16[64,8,128]{2,1,0:T(8,128)(2,1)} %shard_map.38), calls=%async_computation.1 | async-start | bytes 262144 | tf_op jit(solution)/shard_map/all_to_all | solution.py:407
  20.5 4.0 %shard_map.37 = (bf16[8,384,128]{2,1,0:T(8,128)(2,1)}, bf16[16,128,128]{2,1,0:T(8,128)(2,1)}) custom-call(bf16[128,4096]{1,0:T(8,128)(2,1)} %q_hbm.3, bf16[128,4096]{1,0:T(8,128)(2,1)} %k_hbm.3, bf16[128,4096]{1,0:T(8,128)(2,1)} %v_hbm.3), custom_call_target="tpu_custom_call" | custom-call | flops 301989888 | bytes 4194304 | tf_op jit(solution)/shard_map/pallas_call | solution.py:394
  24.5 5.9 %all-to-all-done.1 = bf16[64,8,128]{2,1,0:T(8,128)(2,1)S(1)} async-done(((bf16[64,8,128]{2,1,0:T(8,128)(2,1)}), bf16[64,8,128]{2,1,0:T(8,128)(2,1)S(1)}, u32[]{:S(2)}, u32[]{:S(2)}) %all-to-all-start.1) | async-done | bytes 131104 | tf_op jit(solution)/shard_map/all_to_all | solution.py:407
  30.4 0.7 copy.6
  31.1 16.9 %all-to-all-start.3 = ((bf16[768,4,128]{2,1,0:T(4,128)(2,1)}), bf16[768,4,128]{2,1,0:T(4,128)(2,1)S(1)}, u32[]{:S(2)}, u32[]{:S(2)}) async-start(bf16[768,4,128]{2,1,0:T(4,128)(2,1)} %bitcast.10), calls=%async_computation.3 | async-start | bytes 1572864 | tf_op jit(solution)/shard_map/all_to_all | solution.py:407
  48.0 0.0 all-gather.2.cloned.1.call-start
  48.0 0.7 all-gather.2.cloned.1.call-update
  48.7 22.6 %all-to-all-done.3 = bf16[768,4,128]{2,1,0:T(4,128)(2,1)S(1)} async-done(((bf16[768,4,128]{2,1,0:T(4,128)(2,1)}), bf16[768,4,128]{2,1,0:T(4,128)(2,1)S(1)}, u32[]{:S(2)}, u32[]{:S(2)}) %all-to-all-start.3) | async-done | bytes 786464 | tf_op jit(solution)/shard_map/all_to_all | solution.py:407
  71.3 6.9 %all-to-all-start = ((bf16[16,128,128]{2,1,0:T(8,128)(2,1)}), bf16[16,128,128]{2,1,0:T(8,128)(2,1)S(1)}, u32[]{:S(2)}, u32[]{:S(2)}) async-start(bf16[16,128,128]{2,1,0:T(8,128)(2,1)} %get-tuple-element.10), calls=%async_computation | async-start | bytes 1048576 | tf_op jit(solution)/shard_map/all_to_all | solution.py:407
  78.2 2.0 %collective-permute-start = (bf16[3072,128]{1,0:T(8,128)(2,1)S(1)}, bf16[3072,128]{1,0:T(8,128)(2,1)S(1)}, u32[]{:S(2)}, u32[]{:S(2)}) collective-permute-start(bf16[3072,128]{1,0:T(8,128)(2,1)S(1)} %bitcast.14), channel_id=1, source_target_pairs={{0,1},{1,0},{2,3},{3,2},{4,5},{5,4},{6,7},{7,6},{8,9},{9,8},{10,11... | collective-permute-start | bytes 2359304 | tf_op jit(solution)/shard_map/ppermute | solution.py:552
  80.2 2.1 %collective-permute-done.other_ref = bf16[3072,128]{1,0:T(8,128)(2,1)S(1)} collective-permute-done((bf16[3072,128]{1,0:T(8,128)(2,1)S(1)}, bf16[3072,128]{1,0:T(8,128)(2,1)S(1)}, u32[]{:S(2)}, u32[]{:S(2)}) %collective-permute-start) | collective-permute-done | bytes 786464 | tf_op jit(solution)/shard_map/ppermute | solution.py:552
  82.4 0.9 copy-done.4
  83.2 5.7 %shard_map.41 = bf16[4,256,128]{2,1,0:T(8,128)(2,1)} custom-call(s32[1]{0:T(128)} %bitcast.4.core_ref, bf16[3072,128]{1,0:T(8,128)(2,1)} %bitcast.15, bf16[3072,128]{1,0:T(8,128)(2,1)} %copy-done.4), custom_call_target="tpu_custom_call" | custom-call | flops 671088640 | bytes 2097152 | tf_op jit(solution)/shard_map/pallas_call | solution.py:394
  89.0 11.7 %all-to-all-start.4 = ((bf16[256,4,128]{2,1,0:T(4,128)(2,1)}), bf16[256,4,128]{2,1,0:T(4,128)(2,1)S(1)}, u32[]{:S(2)}, u32[]{:S(2)}) async-start(bf16[256,4,128]{2,1,0:T(4,128)(2,1)} %bitcast.17), calls=%async_computation.4 | async-start | bytes 524288 | tf_op jit(solution)/shard_map/all_to_all | solution.py:407
  100.7 0.0 all-gather.2.cloned.1.call-done.kv_hbm
  100.7 9.7 %shard_map.39 = bf16[16,144,128]{2,1,0:T(8,128)(2,1)} custom-call(s32[1]{0:T(128)} %bitcast.pair_ref, bf16[16,128,128]{2,1,0:T(8,128)(2,1)} %copy-done.3, bf16[8,2,256,128]{3,2,1,0:T(8,128)(2,1)} %all-gather.2.cloned.1.call-done.kv_hbm), custom_call_target="tpu_custom_call" | custom-call | flops 2147483648 | bytes 3145728 | tf_op jit(solution)/shard_map/pallas_call | solution.py:394
  110.4 3.7 %all-to-all-done.4 = bf16[256,4,128]{2,1,0:T(4,128)(2,1)S(1)} async-done(((bf16[256,4,128]{2,1,0:T(4,128)(2,1)}), bf16[256,4,128]{2,1,0:T(4,128)(2,1)S(1)}, u32[]{:S(2)}, u32[]{:S(2)}) %all-to-all-start.4) | async-done | bytes 262176 | tf_op jit(solution)/shard_map/all_to_all | solution.py:407
  114.1 0.7 copy-done.1
  114.8 5.8 %all-to-all-start.2 = ((bf16[16,144,128]{2,1,0:T(8,128)(2,1)}), bf16[16,144,128]{2,1,0:T(8,128)(2,1)S(1)}, u32[]{:S(2)}, u32[]{:S(2)}) async-start(bf16[16,144,128]{2,1,0:T(8,128)(2,1)} %shard_map.39), calls=%async_computation.2 | async-start | bytes 1179648 | tf_op jit(solution)/shard_map/all_to_all | solution.py:407
  120.6 8.6 %shard_map.42 = (bf16[8,128,128]{2,1,0:T(8,128)(2,1)}, f32[16,128,128]{2,1,0:T(8,128)}, f32[2,128,128]{2,1,0:T(8,128)}) custom-call(bf16[128,4096]{1,0:T(8,128)(2,1)} %q_hbm.3, bf16[128,4096]{1,0:T(8,128)(2,1)} %k_hbm.3, bf16[128,4096]{1,0:T(8,128)(2,1)} %v_hbm.3), custom_call_target="tpu_custom_call" | custom-call | flops 201326592 | bytes 5242880 | tf_op jit(solution)/shard_map/pallas_call | solution.py:394
  129.2 2.3 %all-to-all-done.2.far_ref = bf16[16,144,128]{2,1,0:T(8,128)(2,1)S(1)} async-done(((bf16[16,144,128]{2,1,0:T(8,128)(2,1)}), bf16[16,144,128]{2,1,0:T(8,128)(2,1)S(1)}, u32[]{:S(2)}, u32[]{:S(2)}) %all-to-all-start.2) | async-done | bytes 589856 | tf_op jit(solution)/shard_map/all_to_all | solution.py:407
  131.5 0.8 copy-done
  132.3 3.9 %shard_map.43 = bf16[128,4096]{1,0:T(8,128)(2,1)} custom-call(bf16[16,144,128]{2,1,0:T(8,128)(2,1)} %copy-done, bf16[4,256,128]{2,1,0:T(8,128)(2,1)} %bitcast.13, bf16[8,128,128]{2,1,0:T(8,128)(2,1)} %get-tuple-element.12.row_hbm, f32[16,128,128]{2,1,0:T(8,128)} %get-tuple-element.13.part_hbm, f32[2,128,128]{2,1,0:T(8,128)} %get-tuple-element.14.stat_hbm), custom_call_target="tpu_custom_call" | custom-call | flops 33554432 | bytes 4194304 | tf_op jit(solution)/shard_map/pallas_call | solution.py:394
  (9 shorter events, 0.0 us)
Async XLA Ops:
  8.8 21.6 %all-to-all-start.1 = ((bf16[64,8,128]{2,1,0:T(8,128)(2,1)}), bf16[64,8,128]{2,1,0:T(8,128)(2,1)S(1)}, u32[]{:S(2)}, u32[]{:S(2)}) async-start(bf16[64,8,128]{2,1,0:T(8,128)(2,1)} %shard_map.38), calls=%async_computation.1 | async-start | bytes 262144 | tf_op jit(solution)/shard_map/all_to_all | solution.py:407
  31.1 40.2 %all-to-all-start.3 = ((bf16[768,4,128]{2,1,0:T(4,128)(2,1)}), bf16[768,4,128]{2,1,0:T(4,128)(2,1)S(1)}, u32[]{:S(2)}, u32[]{:S(2)}) async-start(bf16[768,4,128]{2,1,0:T(4,128)(2,1)} %bitcast.10), calls=%async_computation.3 | async-start | bytes 1572864 | tf_op jit(solution)/shard_map/all_to_all | solution.py:407
  48.0 52.7 %all-gather.2.cloned.1.call-start = ((), (), s32[]{:S(2)}) async-start(), calls=%async_computation.5 | async-start | bytes 1179648 | tf_op jit(solution)/shard_map/all_gather | solution.py:549
  71.3 11.1 %copy-start.2 = (bf16[768,4,128]{2,1,0:T(4,128)(2,1)}, bf16[768,4,128]{2,1,0:T(4,128)(2,1)S(1)}, u32[]{:S(2)}) copy-start(bf16[768,4,128]{2,1,0:T(4,128)(2,1)S(1)} %all-to-all-done.3) | copy-start | bytes 2359300
  71.3 17.7 %all-to-all-start = ((bf16[16,128,128]{2,1,0:T(8,128)(2,1)}), bf16[16,128,128]{2,1,0:T(8,128)(2,1)S(1)}, u32[]{:S(2)}, u32[]{:S(2)}) async-start(bf16[16,128,128]{2,1,0:T(8,128)(2,1)} %get-tuple-element.10), calls=%async_computation | async-start | bytes 1048576 | tf_op jit(solution)/shard_map/all_to_all | solution.py:407
  78.2 4.2 %collective-permute-start = (bf16[3072,128]{1,0:T(8,128)(2,1)S(1)}, bf16[3072,128]{1,0:T(8,128)(2,1)S(1)}, u32[]{:S(2)}, u32[]{:S(2)}) collective-permute-start(bf16[3072,128]{1,0:T(8,128)(2,1)S(1)} %bitcast.14), channel_id=1, source_target_pairs={{0,1},{1,0},{2,3},{3,2},{4,5},{5,4},{6,7},{7,6},{8,9},{9,8},{10,11... | collective-permute-start | bytes 2359304 | tf_op jit(solution)/shard_map/ppermute | solution.py:552
  82.3 0.9 copy-start.4
  89.0 11.7 %copy-start.3 = (bf16[16,128,128]{2,1,0:T(8,128)(2,1)}, bf16[16,128,128]{2,1,0:T(8,128)(2,1)S(1)}, u32[]{:S(2)}) copy-start(bf16[16,128,128]{2,1,0:T(8,128)(2,1)S(1)} %all-to-all-done.q_hbm) | copy-start | bytes 1572868
  89.0 25.1 %all-to-all-start.4 = ((bf16[256,4,128]{2,1,0:T(4,128)(2,1)}), bf16[256,4,128]{2,1,0:T(4,128)(2,1)S(1)}, u32[]{:S(2)}, u32[]{:S(2)}) async-start(bf16[256,4,128]{2,1,0:T(4,128)(2,1)} %bitcast.17), calls=%async_computation.4 | async-start | bytes 524288 | tf_op jit(solution)/shard_map/all_to_all | solution.py:407
  114.1 0.7 copy-start.1
  114.8 16.7 %all-to-all-start.2 = ((bf16[16,144,128]{2,1,0:T(8,128)(2,1)}), bf16[16,144,128]{2,1,0:T(8,128)(2,1)S(1)}, u32[]{:S(2)}, u32[]{:S(2)}) async-start(bf16[16,144,128]{2,1,0:T(8,128)(2,1)} %shard_map.39), calls=%async_computation.2 | async-start | bytes 1179648 | tf_op jit(solution)/shard_map/all_to_all | solution.py:407
  131.5 0.8 copy-start
Sparse Core Ops, SparseCore 0:
  50.9 38.0 all-gather.1

commit v7 on v6

--- a/solution.py
+++ b/solution.py
@@ -126,7 +126,7 @@
         move.wait()
 
 
-def order_kernel(after_ref, item_ref, out_ref):
+def order_kernel(after_ref, array_ref, out_ref):
     pass
 
 
@@ -327,26 +327,55 @@
         send(b).wait()
 
 
-def final_kernel(
-    far_ref, col_ref, row_hbm, part_hbm, stat_hbm, out_hbm,
-    row_ref, part_ref, stat_ref, out_ref, sems,
-):
+def place_kernel(col_hbm, row_hbm, out_hbm, col_ref, row_ref, out_ref, sems):
     ins = [
-        pltpu.make_async_copy(stat_hbm, stat_ref, sems.at[0]),
-        pltpu.make_async_copy(part_hbm, part_ref, sems.at[1]),
-        pltpu.make_async_copy(row_hbm, row_ref, sems.at[2]),
+        pltpu.make_async_copy(col_hbm, col_ref, sems.at[0]),
+        pltpu.make_async_copy(row_hbm, row_ref, sems.at[1]),
     ]
     for move in ins:
         move.start()
     back = one_hot(
         POS, POS, lambda o: (o & 3) * STRIDE + ((o >> 2) & 7) * 4 + (o >> 5)
     )
+    for move in ins:
+        move.wait()
+    moves = []
+    for quad in range(QUADS):
+        out_ref[quad, :, :HD] = row_ref[quad]
+        stack = jnp.concatenate(
+            [col_ref[x, quad * STRIDE : (quad + 1) * STRIDE, :] for x in range(4)], axis=0
+        )
+        out_ref[quad, :, HD:] = dot(back, stack).astype(bf16)
+        move = pltpu.make_async_copy(
+            out_ref.at[quad], out_hbm.at[:, pl.ds(quad * 4 * HD, 2 * HD)], sems.at[2 + quad]
+        )
+        move.start()
+        moves.append(move)
+    for move in moves:
+        move.wait()
+
+
+def merge_kernel(
+    placed_hbm, far_hbm, part_hbm, stat_hbm, out_hbm, far_ref, part_ref, stat_ref, out_ref, sems
+):
+    ins = [
+        pltpu.make_async_copy(far_hbm, far_ref, sems.at[0]),
+        pltpu.make_async_copy(stat_hbm, stat_ref, sems.at[1]),
+    ]
+    for g in range(0, HEADS, 4):
+        some = pl.ds(g, 4)
+        ins.append(
+            pltpu.make_async_copy(part_hbm.at[some], part_ref.at[some], sems.at[2 + g // 4])
+        )
+    for move in ins:
+        move.start()
     row = iota((HEADS * SUM_ROWS, 128), 0)
     lane = iota((HEADS * SUM_ROWS, 128), 1)
     pick = jnp.where(
         jnp.logical_and((row >> 4) == lane, (row & 15) < 3), 1.0, 0.0
     ).astype(bf16)
     ins[0].wait()
+    ins[1].wait()
     terms = jnp.concatenate([far_ref[g, POS:, :] for g in range(HEADS)], axis=0)
     lse = dot_tl(terms, pick)
     top = jnp.maximum(stat_ref[0], lse)
@@ -355,28 +384,24 @@
     scale = 1.0 / (stat_ref[1] * own + far)
     own = own * scale
     far = far * scale
-    for move in ins[1:]:
-        move.wait()
     moves = []
-    for quad in range(QUADS):
-        base = quad * 4 * HD
-        out_ref[:, base : base + HD] = row_ref[quad]
-        stack = jnp.concatenate(
-            [col_ref[x, quad * STRIDE : (quad + 1) * STRIDE, :] for x in range(4)], axis=0
+    for g in range(HEADS):
+        if g % 4 == 0:
+            ins[2 + g // 4].wait()
+        merged = (
+            part_ref[g] * own[:, g : g + 1]
+            + far_ref[g, :POS, :].astype(f32) * far[:, g : g + 1]
         )
-        out_ref[:, base + HD : base + 2 * HD] = dot(back, stack).astype(bf16)
-        for h in range(2):
-            g = quad * 2 + h
-            merged = (
-                part_ref[g] * own[:, g : g + 1]
-                + far_ref[g, :POS, :].astype(f32) * far[:, g : g + 1]
+        quad, h = g // 2, g % 2
+        out_ref[quad, :, h * HD : (h + 1) * HD] = merged.astype(bf16)
+        if h == 1:
+            move = pltpu.make_async_copy(
+                out_ref.at[quad],
+                out_hbm.at[:, pl.ds((quad * 4 + 2) * HD, 2 * HD)],
+                sems.at[6 + quad],
             )
-            start = base + (2 + h) * HD
-            out_ref[:, start : start + HD] = merged.astype(bf16)
-        at = pl.ds(base, 4 * HD)
-        move = pltpu.make_async_copy(out_ref.at[:, at], out_hbm.at[:, at], sems.at[3 + quad])
-        move.start()
-        moves.append(move)
+            move.start()
+            moves.append(move)
     for move in moves:
         move.wait()
 
@@ -452,9 +477,15 @@
     )
 
 
-def ordered(after, items):
-    return call(
-        order_kernel, [((QUADS, 384, HD), bf16)], (after, items), "hh", to="h", alias={1: 0}
+def ordered(after, array):
+    return call(
+        order_kernel,
+        [(array.shape, array.dtype)],
+        (after, array),
+        "hh",
+        to="h",
+        alias={1: 0},
+        room=46_000_000,
     )
 
 
@@ -469,7 +500,6 @@
         scratch=[pltpu.VMEM((POS, QUADS * 4 * HD), bf16)] * 3
         + [pltpu.VMEM(*out) for out in outs]
         + [dma(13)],
-        room=1_250_000,
         flops=24 * 4 * 128 * 128 * 128,
         moved=5 * mib,
         exps=24 * 128 * 128,
@@ -490,7 +520,7 @@
             pltpu.VMEM((2, 1024, HD), bf16),
             dma(4),
         ],
-        room=2_600_000,
+        room=46_000_000,
         flops=4 * 1024 * 1280 * 128,
         moved=2 * mib,
         exps=1024 * 1280,
@@ -517,23 +547,41 @@
     )
 
 
-def final(far, column, row_out, part, stat):
-    return call(
-        final_kernel,
+def place(column, row_out):
+    return call(
+        place_kernel,
         [((POS, QUADS * 4 * HD), bf16)],
-        (far, column, row_out, part, stat),
-        "vvhhh",
+        (column, row_out),
+        "hh",
         to="h",
         scratch=[
+            pltpu.VMEM((4, 256, HD), bf16),
             pltpu.VMEM((QUADS, POS, HD), bf16),
+            pltpu.VMEM((QUADS, POS, 2 * HD), bf16),
+            dma(10),
+        ],
+        flops=2 * 8 * 128 * 128 * 128,
+        moved=mib,
+    )
+
+
+def merge(placed, far, part, stat):
+    return call(
+        merge_kernel,
+        [((POS, QUADS * 4 * HD), bf16)],
+        (placed, far, part, stat),
+        "hhhh",
+        to="h",
+        scratch=[
+            pltpu.VMEM((HEADS, PAY, HD), bf16),
             pltpu.VMEM((HEADS, POS, HD), f32),
             pltpu.VMEM((2, POS, 128), f32),
-            pltpu.VMEM((POS, QUADS * 4 * HD), bf16),
-            dma(11),
+            pltpu.VMEM((QUADS, POS, 2 * HD), bf16),
+            dma(14),
         ],
-        room=500_000,
+        alias={0: 0},
         flops=2 * 8 * 128 * 128 * 128,
-        moved=4 * mib,
+        moved=3 * mib,
     )
 
 
@@ -548,15 +596,16 @@
     items = ordered(summary, items)
     summary = lax.all_gather(summary, "z", axis=0, tiled=True)
     items = exchange(items.reshape(768, ROWS, HD), wide).reshape(3072, HD)
-    heads = exchange(heads, heads_at)
+    row_out, part, stat = rows(queries, keys, values)
+    items = ordered(stat, items)
+    heads = exchange(ordered(stat, heads), heads_at)
     other = lax.ppermute(items, "c", [(0, 1), (1, 0)])
     core = lax.axis_index("c").astype(jnp.int32).reshape(1)
     column = columns(core, items, other)
     column = exchange(column.reshape(256, ROWS, HD), back).reshape(4, 256, HD)
     pair = lax.axis_index(("z", "u", "v")).astype(jnp.int32).reshape(1)
     far = exchange(far_part(pair, heads, summary), heads_at)
-    row_out, part, stat = rows(queries, keys, values)
-    return final(far, column, row_out, part, stat)
+    return merge(place(column, row_out), far, part, stat)
 
 
 def solution(mesh):

time: 144 us -> 142 us (0.986)
  waiting for transfers between devices: 37.4 us -> 35.6 us
    unnamed x10 -> x16, local copies, waits for them, and re-layouts: 2.43 us -> 4.48 us
    all_to_all x5, waiting for transfers between devices: 34.5 us -> 32.9 us  [exchange(): return lax.all_to_all(array, axes, split_axis=0, concat_axis=0, tiled=True)]
    all_to_all x5, starting transfers between devices: 52.8 us -> 51.3 us  [exchange(): return lax.all_to_all(array, axes, split_axis=0, concat_axis=0, tiled=True)]
    pallas_call x7 -> x10, Pallas kernels: 34.2 us -> 33.9 us  [call(): pl.pallas_call(kernel, out_shape=shapes if many else shapes[0], in_specs=...]
  transfers between devices with their start and end apart: 7 -> 7, of which waited for: 5 -> 6; matrix products, arithmetic and copies ran while one was open for 0% -> 0% of each run, Pallas kernels for 20% -> 20%
where the time goes in v7:
time: 142 us; the launch traced here: 141 us
  starting transfers between devices  53.5 us (38%)
  waiting for transfers between devices  35.6 us (25%)
  Pallas kernels  33.9 us (24%)
  between operations  13.6 us (10%)
  local copies, waits for them, and re-layouts  4.53 us (3%)
    all_to_all x5, starting transfers between devices, exchange(): return lax.all_to_all(array, axes, split_axis=0, concat_axis=0, tiled=True)  51.3 us
    pallas_call x10, Pallas kernels, call(): pl.pallas_call(kernel, out_shape=shapes if many else shapes[0], in_specs=...  33.9 us
    all_to_all x5, waiting for transfers between devices, exchange(): return lax.all_to_all(array, axes, split_axis=0, concat_axis=0, tiled=True)  32.9 us
    unnamed x16, local copies, waits for them, and re-layouts  4.48 us
  transfers between devices with their start and end apart: 7, of which 6 were waited for; matrix products, arithmetic and copies ran while one was open for 0% of the time, Pallas kernels for 20%

profile of v7, /device:TPU:1, one launch (start us, length us, event | category | flops | bytes accessed | tf_op | source)
XLA Modules:
  0.0 141.1 jit_solution(731444014669262436)
XLA Ops:
  6.5 2.3 %shard_map.38 = bf16[64,8,128]{2,1,0:T(8,128)(2,1)} custom-call(bf16[128,4096]{1,0:T(8,128)(2,1)} %k_hbm.3, bf16[128,4096]{1,0:T(8,128)(2,1)} %v_hbm.3), custom_call_target="tpu_custom_call" | custom-call | flops 8388608 | bytes 1048576 | tf_op jit(solution)/shard_map/pallas_call | solution.py:419
  8.8 11.6 %all-to-all-start = ((bf16[64,8,128]{2,1,0:T(8,128)(2,1)}), bf16[64,8,128]{2,1,0:T(8,128)(2,1)S(1)}, u32[]{:S(2)}, u32[]{:S(2)}) async-start(bf16[64,8,128]{2,1,0:T(8,128)(2,1)} %shard_map.38), calls=%async_computation | async-start | bytes 262144 | tf_op jit(solution)/shard_map/all_to_all | solution.py:432
  20.5 4.0 %shard_map.39 = (bf16[8,384,128]{2,1,0:T(8,128)(2,1)}, bf16[16,128,128]{2,1,0:T(8,128)(2,1)}) custom-call(bf16[128,4096]{1,0:T(8,128)(2,1)} %q_hbm.3, bf16[128,4096]{1,0:T(8,128)(2,1)} %k_hbm.3, bf16[128,4096]{1,0:T(8,128)(2,1)} %v_hbm.3), custom_call_target="tpu_custom_call" | custom-call | flops 301989888 | bytes 4194304 | tf_op jit(solution)/shard_map/pallas_call | solution.py:419
  24.5 5.9 %all-to-all-done = bf16[64,8,128]{2,1,0:T(8,128)(2,1)S(1)} async-done(((bf16[64,8,128]{2,1,0:T(8,128)(2,1)}), bf16[64,8,128]{2,1,0:T(8,128)(2,1)S(1)}, u32[]{:S(2)}, u32[]{:S(2)}) %all-to-all-start) | async-done | bytes 131104 | tf_op jit(solution)/shard_map/all_to_all | solution.py:432
  30.5 1.2 copy-done
  31.7 0.9 copy-done.1
  32.5 16.9 %all-to-all-start.1 = ((bf16[768,4,128]{2,1,0:T(4,128)(2,1)}), bf16[768,4,128]{2,1,0:T(4,128)(2,1)S(1)}, u32[]{:S(2)}, u32[]{:S(2)}) async-start(bf16[768,4,128]{2,1,0:T(4,128)(2,1)} %bitcast.11), calls=%async_computation.1 | async-start | bytes 1572864 | tf_op jit(solution)/shard_map/all_to_all | solution.py:432
  50.1 8.6 %shard_map.37 = (bf16[8,128,128]{2,1,0:T(8,128)(2,1)}, f32[16,128,128]{2,1,0:T(8,128)}, f32[2,128,128]{2,1,0:T(8,128)}) custom-call(bf16[128,4096]{1,0:T(8,128)(2,1)} %q_hbm.3, bf16[128,4096]{1,0:T(8,128)(2,1)} %k_hbm.3, bf16[128,4096]{1,0:T(8,128)(2,1)} %v_hbm.3), custom_call_target="tpu_custom_call" | custom-call | flops 201326592 | bytes 5242880 | tf_op jit(solution)/shard_map/pallas_call | solution.py:419
  58.8 0.9 copy-done.3
  59.7 13.0 %all-to-all-done.1 = bf16[768,4,128]{2,1,0:T(4,128)(2,1)S(1)} async-done(((bf16[768,4,128]{2,1,0:T(4,128)(2,1)}), bf16[768,4,128]{2,1,0:T(4,128)(2,1)S(1)}, u32[]{:S(2)}, u32[]{:S(2)}) %all-to-all-start.1) | async-done | bytes 786464 | tf_op jit(solution)/shard_map/all_to_all | solution.py:432
  72.7 6.9 %all-to-all-start.3 = ((bf16[16,128,128]{2,1,0:T(8,128)(2,1)}), bf16[16,128,128]{2,1,0:T(8,128)(2,1)S(1)}, u32[]{:S(2)}, u32[]{:S(2)}) async-start(bf16[16,128,128]{2,1,0:T(8,128)(2,1)} %shard_map.44), calls=%async_computation.3 | async-start | bytes 1048576 | tf_op jit(solution)/shard_map/all_to_all | solution.py:432
  79.6 2.2 %collective-permute-start = (bf16[3072,128]{1,0:T(8,128)(2,1)S(1)}, bf16[3072,128]{1,0:T(8,128)(2,1)S(1)}, u32[]{:S(2)}, u32[]{:S(2)}) collective-permute-start(bf16[3072,128]{1,0:T(8,128)(2,1)S(1)} %shard_map.41.own_ref), channel_id=1, source_target_pairs={{0,1},{1,0},{2,3},{3,2},{4,5},{5,4},{6,7},{7,6},{8,9},{9,8},{10,11... | collective-permute-start | bytes 2359304 | tf_op jit(solution)/shard_map/ppermute | solution.py:602
  81.8 2.0 %collective-permute-done.other_ref = bf16[3072,128]{1,0:T(8,128)(2,1)S(1)} collective-permute-done((bf16[3072,128]{1,0:T(8,128)(2,1)S(1)}, bf16[3072,128]{1,0:T(8,128)(2,1)S(1)}, u32[]{:S(2)}, u32[]{:S(2)}) %collective-permute-start) | collective-permute-done | bytes 786464 | tf_op jit(solution)/shard_map/ppermute | solution.py:602
  83.8 4.4 %shard_map.42 = bf16[4,256,128]{2,1,0:T(8,128)(2,1)} custom-call(s32[1]{0:T(128)} %bitcast.core_ref, bf16[3072,128]{1,0:T(8,128)(2,1)S(1)} %shard_map.41.own_ref, bf16[3072,128]{1,0:T(8,128)(2,1)S(1)} %collective-permute-done.other_ref), custom_call_target="tpu_custom_call" | custom-call | flops 671088640 | bytes 2097152 | tf_op jit(solution)/shard_map/pallas_call | solution.py:419
  88.2 1.6 %all-to-all-done.3.q_hbm = bf16[16,128,128]{2,1,0:T(8,128)(2,1)S(1)} async-done(((bf16[16,128,128]{2,1,0:T(8,128)(2,1)}), bf16[16,128,128]{2,1,0:T(8,128)(2,1)S(1)}, u32[]{:S(2)}, u32[]{:S(2)}) %all-to-all-start.3) | async-done | bytes 524320 | tf_op jit(solution)/shard_map/all_to_all | solution.py:432
  89.8 10.1 %all-to-all-start.2 = ((bf16[256,4,128]{2,1,0:T(4,128)(2,1)}), bf16[256,4,128]{2,1,0:T(4,128)(2,1)S(1)}, u32[]{:S(2)}, u32[]{:S(2)}) async-start(bf16[256,4,128]{2,1,0:T(4,128)(2,1)} %bitcast.6), calls=%async_computation.2 | async-start | bytes 524288 | tf_op jit(solution)/shard_map/all_to_all | solution.py:432
  99.9 9.7 %shard_map.45 = bf16[16,144,128]{2,1,0:T(8,128)(2,1)} custom-call(s32[1]{0:T(128)} %bitcast.8.pair_ref, bf16[16,128,128]{2,1,0:T(8,128)(2,1)} %copy-done.7, bf16[8,2,256,128]{3,2,1,0:T(8,128)(2,1)} %all-gather.2.cloned.1.call-done.kv_hbm), custom_call_target="tpu_custom_call" | custom-call | flops 2147483648 | bytes 3145728 | tf_op jit(solution)/shard_map/pallas_call | solution.py:419
  109.6 3.4 %all-to-all-done.2 = bf16[256,4,128]{2,1,0:T(4,128)(2,1)S(1)} async-done(((bf16[256,4,128]{2,1,0:T(4,128)(2,1)}), bf16[256,4,128]{2,1,0:T(4,128)(2,1)S(1)}, u32[]{:S(2)}, u32[]{:S(2)}) %all-to-all-start.2) | async-done | bytes 262176 | tf_op jit(solution)/shard_map/all_to_all | solution.py:432
  113.1 0.7 copy-done.6
  113.8 5.8 %all-to-all-start.4 = ((bf16[16,144,128]{2,1,0:T(8,128)(2,1)}), bf16[16,144,128]{2,1,0:T(8,128)(2,1)S(1)}, u32[]{:S(2)}, u32[]{:S(2)}) async-start(bf16[16,144,128]{2,1,0:T(8,128)(2,1)} %shard_map.45), calls=%async_computation.4 | async-start | bytes 1179648 | tf_op jit(solution)/shard_map/all_to_all | solution.py:432
  119.6 2.0 %shard_map.43.placed_hbm = bf16[128,4096]{1,0:T(8,128)(2,1)} custom-call(bf16[4,256,128]{2,1,0:T(8,128)(2,1)} %bitcast.14, bf16[8,128,128]{2,1,0:T(8,128)(2,1)} %get-tuple-element.12.row_hbm), custom_call_target="tpu_custom_call" | custom-call | flops 33554432 | bytes 1048576 | tf_op jit(solution)/shard_map/pallas_call | solution.py:419
  121.6 8.9 %all-to-all-done.4.far_hbm = bf16[16,144,128]{2,1,0:T(8,128)(2,1)S(1)} async-done(((bf16[16,144,128]{2,1,0:T(8,128)(2,1)}), bf16[16,144,128]{2,1,0:T(8,128)(2,1)S(1)}, u32[]{:S(2)}, u32[]{:S(2)}) %all-to-all-start.4) | async-done | bytes 589856 | tf_op jit(solution)/shard_map/all_to_all | solution.py:432
  130.5 0.8 copy-done.5
  131.3 2.9 %shard_map.46 = bf16[128,4096]{1,0:T(8,128)(2,1)} custom-call(bf16[128,4096]{1,0:T(8,128)(2,1)} %shard_map.43.placed_hbm, bf16[16,144,128]{2,1,0:T(8,128)(2,1)} %copy-done.5, f32[16,128,128]{2,1,0:T(8,128)} %get-tuple-element.14.part_hbm, f32[2,128,128]{2,1,0:T(8,128)} %get-tuple-element.10.after_ref.stat_hbm), custom_call_target="tpu_custom_call", output_to_operand_aliasing={{}: (0, {})} | custom-call | flops 33554432 | bytes 3145728 | tf_op jit(solution)/shard_map/pallas_call | solution.py:419
  (18 shorter events, 0.8 us)
Async XLA Ops:
  8.8 21.6 %all-to-all-start = ((bf16[64,8,128]{2,1,0:T(8,128)(2,1)}), bf16[64,8,128]{2,1,0:T(8,128)(2,1)S(1)}, u32[]{:S(2)}, u32[]{:S(2)}) async-start(bf16[64,8,128]{2,1,0:T(8,128)(2,1)} %shard_map.38), calls=%async_computation | async-start | bytes 262144 | tf_op jit(solution)/shard_map/all_to_all | solution.py:432
  30.5 1.2 copy-start.2
  30.5 1.2 copy-start
  31.6 0.9 copy-start.1
  32.5 40.2 %all-to-all-start.1 = ((bf16[768,4,128]{2,1,0:T(4,128)(2,1)}), bf16[768,4,128]{2,1,0:T(4,128)(2,1)S(1)}, u32[]{:S(2)}, u32[]{:S(2)}) async-start(bf16[768,4,128]{2,1,0:T(4,128)(2,1)} %bitcast.11), calls=%async_computation.1 | async-start | bytes 1572864 | tf_op jit(solution)/shard_map/all_to_all | solution.py:432
  49.4 50.5 %all-gather.2.cloned.1.call-start = ((), (), s32[]{:S(2)}) async-start(), calls=%async_computation.5 | async-start | bytes 1179648 | tf_op jit(solution)/shard_map/all_gather | solution.py:597
  58.8 0.9 copy-start.3
  59.7 19.9 %copy-start.4 = (f32[2,128,128]{2,1,0:T(8,128)S(1)}, f32[2,128,128]{2,1,0:T(8,128)}, u32[]{:S(2)}) copy-start(f32[2,128,128]{2,1,0:T(8,128)} %get-tuple-element.10.after_ref.stat_hbm) | copy-start | bytes 393220
  72.7 17.1 %all-to-all-start.3 = ((bf16[16,128,128]{2,1,0:T(8,128)(2,1)}), bf16[16,128,128]{2,1,0:T(8,128)(2,1)S(1)}, u32[]{:S(2)}, u32[]{:S(2)}) async-start(bf16[16,128,128]{2,1,0:T(8,128)(2,1)} %shard_map.44), calls=%async_computation.3 | async-start | bytes 1048576 | tf_op jit(solution)/shard_map/all_to_all | solution.py:432
  79.6 4.2 %collective-permute-start = (bf16[3072,128]{1,0:T(8,128)(2,1)S(1)}, bf16[3072,128]{1,0:T(8,128)(2,1)S(1)}, u32[]{:S(2)}, u32[]{:S(2)}) collective-permute-start(bf16[3072,128]{1,0:T(8,128)(2,1)S(1)} %shard_map.41.own_ref), channel_id=1, source_target_pairs={{0,1},{1,0},{2,3},{3,2},{4,5},{5,4},{6,7},{7,6},{8,9},{9,8},{10,11... | collective-permute-start | bytes 2359304 | tf_op jit(solution)/shard_map/ppermute | solution.py:602
  89.8 10.1 %copy-start.7 = (bf16[16,128,128]{2,1,0:T(8,128)(2,1)}, bf16[16,128,128]{2,1,0:T(8,128)(2,1)S(1)}, u32[]{:S(2)}) copy-start(bf16[16,128,128]{2,1,0:T(8,128)(2,1)S(1)} %all-to-all-done.3.q_hbm) | copy-start | bytes 1572868
  89.8 23.2 %all-to-all-start.2 = ((bf16[256,4,128]{2,1,0:T(4,128)(2,1)}), bf16[256,4,128]{2,1,0:T(4,128)(2,1)S(1)}, u32[]{:S(2)}, u32[]{:S(2)}) async-start(bf16[256,4,128]{2,1,0:T(4,128)(2,1)} %bitcast.6), calls=%async_computation.2 | async-start | bytes 524288 | tf_op jit(solution)/shard_map/all_to_all | solution.py:432
  113.1 0.7 copy-start.6
  113.8 16.7 %all-to-all-start.4 = ((bf16[16,144,128]{2,1,0:T(8,128)(2,1)}), bf16[16,144,128]{2,1,0:T(8,128)(2,1)S(1)}, u32[]{:S(2)}, u32[]{:S(2)}) async-start(bf16[16,144,128]{2,1,0:T(8,128)(2,1)} %shard_map.45), calls=%async_computation.4 | async-start | bytes 1179648 | tf_op jit(solution)/shard_map/all_to_all | solution.py:432
  130.5 0.8 copy-start.5
Sparse Core Ops, SparseCore 0:
  52.3 38.0 all-gather.1

commit v8 on v7

--- a/solution.py
+++ b/solution.py
@@ -477,7 +477,7 @@
     )
 
 
-def ordered(after, array):
+def ordered(after, array, room=46_000_000):
     return call(
         order_kernel,
         [(array.shape, array.dtype)],
@@ -485,7 +485,7 @@
         "hh",
         to="h",
         alias={1: 0},
-        room=46_000_000,
+        room=room,
     )
 
 
@@ -560,6 +560,7 @@
             pltpu.VMEM((QUADS, POS, 2 * HD), bf16),
             dma(10),
         ],
+        room=46_000_000,
         flops=2 * 8 * 128 * 128 * 128,
         moved=mib,
     )
@@ -580,6 +581,7 @@
             dma(14),
         ],
         alias={0: 0},
+        room=500_000,
         flops=2 * 8 * 128 * 128 * 128,
         moved=3 * mib,
     )
@@ -593,7 +595,7 @@
     summary = exchange(pack_summary(keys, values), plane)
     summary = summary.reshape(64, 2, ROWS, HD).transpose(1, 0, 2, 3).reshape(1, 2, 256, HD)
     items, heads = pack(queries, keys, values)
-    items = ordered(summary, items)
+    items = ordered(summary, items, room=0)
     summary = lax.all_gather(summary, "z", axis=0, tiled=True)
     items = exchange(items.reshape(768, ROWS, HD), wide).reshape(3072, HD)
     row_out, part, stat = rows(queries, keys, values)

time: 142 us -> 140 us (0.986)
  local copies, waits for them, and re-layouts: 4.53 us -> 2.43 us
    unnamed x16 -> x10, local copies, waits for them, and re-layouts: 4.48 us -> 1.74 us
where the time goes in v8:
time: 140 us; the launch traced here: 139 us
  starting transfers between devices  53.5 us (38%)
  waiting for transfers between devices  36.5 us (26%)
  Pallas kernels  33 us (24%)
  between operations  13.6 us (10%)
  local copies, waits for them, and re-layouts  2.43 us (2%)
    all_to_all x5, starting transfers between devices, exchange(): return lax.all_to_all(array, axes, split_axis=0, concat_axis=0, tiled=True)  51.3 us
    all_to_all x5, waiting for transfers between devices, exchange(): return lax.all_to_all(array, axes, split_axis=0, concat_axis=0, tiled=True)  33.8 us
    pallas_call x10, Pallas kernels, call(): pl.pallas_call(kernel, out_shape=shapes if many else shapes[0], in_specs=...  33 us
  transfers between devices with their start and end apart: 7, of which 6 were waited for; matrix products, arithmetic and copies ran while one was open for 0% of the time, Pallas kernels for 20%

profile of v8, /device:TPU:1, one launch (start us, length us, event | category | flops | bytes accessed | tf_op | source)
XLA Modules:
  0.0 138.9 jit_solution(6053187354088734645)
XLA Ops:
  6.5 2.3 %shard_map.38 = bf16[64,8,128]{2,1,0:T(8,128)(2,1)} custom-call(bf16[128,4096]{1,0:T(8,128)(2,1)} %k_hbm.3, bf16[128,4096]{1,0:T(8,128)(2,1)} %v_hbm.3), custom_call_target="tpu_custom_call" | custom-call | flops 8388608 | bytes 1048576 | tf_op jit(solution)/shard_map/pallas_call | solution.py:419
  8.8 11.6 %all-to-all-start = ((bf16[64,8,128]{2,1,0:T(8,128)(2,1)}), bf16[64,8,128]{2,1,0:T(8,128)(2,1)S(1)}, u32[]{:S(2)}, u32[]{:S(2)}) async-start(bf16[64,8,128]{2,1,0:T(8,128)(2,1)} %shard_map.38), calls=%async_computation | async-start | bytes 262144 | tf_op jit(solution)/shard_map/all_to_all | solution.py:432
  20.5 4.0 %shard_map.39 = (bf16[8,384,128]{2,1,0:T(8,128)(2,1)}, bf16[16,128,128]{2,1,0:T(8,128)(2,1)}) custom-call(bf16[128,4096]{1,0:T(8,128)(2,1)} %q_hbm.3, bf16[128,4096]{1,0:T(8,128)(2,1)} %k_hbm.3, bf16[128,4096]{1,0:T(8,128)(2,1)} %v_hbm.3), custom_call_target="tpu_custom_call" | custom-call | flops 301989888 | bytes 4194304 | tf_op jit(solution)/shard_map/pallas_call | solution.py:419
  24.5 5.9 %all-to-all-done = bf16[64,8,128]{2,1,0:T(8,128)(2,1)S(1)} async-done(((bf16[64,8,128]{2,1,0:T(8,128)(2,1)}), bf16[64,8,128]{2,1,0:T(8,128)(2,1)S(1)}, u32[]{:S(2)}, u32[]{:S(2)}) %all-to-all-start) | async-done | bytes 131104 | tf_op jit(solution)/shard_map/all_to_all | solution.py:432
  30.4 0.7 copy.9
  31.1 16.9 %all-to-all-start.1 = ((bf16[768,4,128]{2,1,0:T(4,128)(2,1)}), bf16[768,4,128]{2,1,0:T(4,128)(2,1)S(1)}, u32[]{:S(2)}, u32[]{:S(2)}) async-start(bf16[768,4,128]{2,1,0:T(4,128)(2,1)} %bitcast.12), calls=%async_computation.1 | async-start | bytes 1572864 | tf_op jit(solution)/shard_map/all_to_all | solution.py:432
  48.0 0.0 all-gather.2.cloned.1.call-start
  48.0 0.7 all-gather.2.cloned.1.call-update
  48.7 8.6 %shard_map.37 = (bf16[8,128,128]{2,1,0:T(8,128)(2,1)}, f32[16,128,128]{2,1,0:T(8,128)}, f32[2,128,128]{2,1,0:T(8,128)}) custom-call(bf16[128,4096]{1,0:T(8,128)(2,1)} %q_hbm.3, bf16[128,4096]{1,0:T(8,128)(2,1)} %k_hbm.3, bf16[128,4096]{1,0:T(8,128)(2,1)} %v_hbm.3), custom_call_target="tpu_custom_call" | custom-call | flops 201326592 | bytes 5242880 | tf_op jit(solution)/shard_map/pallas_call | solution.py:419
  57.4 0.9 copy-done
  58.3 13.0 %all-to-all-done.1 = bf16[768,4,128]{2,1,0:T(4,128)(2,1)S(1)} async-done(((bf16[768,4,128]{2,1,0:T(4,128)(2,1)}), bf16[768,4,128]{2,1,0:T(4,128)(2,1)S(1)}, u32[]{:S(2)}, u32[]{:S(2)}) %all-to-all-start.1) | async-done | bytes 786464 | tf_op jit(solution)/shard_map/all_to_all | solution.py:432
  71.3 6.9 %all-to-all-start.3 = ((bf16[16,128,128]{2,1,0:T(8,128)(2,1)}), bf16[16,128,128]{2,1,0:T(8,128)(2,1)S(1)}, u32[]{:S(2)}, u32[]{:S(2)}) async-start(bf16[16,128,128]{2,1,0:T(8,128)(2,1)} %shard_map.44), calls=%async_computation.3 | async-start | bytes 1048576 | tf_op jit(solution)/shard_map/all_to_all | solution.py:432
  78.2 2.2 %collective-permute-start = (bf16[3072,128]{1,0:T(8,128)(2,1)S(1)}, bf16[3072,128]{1,0:T(8,128)(2,1)S(1)}, u32[]{:S(2)}, u32[]{:S(2)}) collective-permute-start(bf16[3072,128]{1,0:T(8,128)(2,1)S(1)} %shard_map.41.own_ref), channel_id=1, source_target_pairs={{0,1},{1,0},{2,3},{3,2},{4,5},{5,4},{6,7},{7,6},{8,9},{9,8},{10,11... | collective-permute-start | bytes 2359304 | tf_op jit(solution)/shard_map/ppermute | solution.py:604
  80.4 2.0 %collective-permute-done.other_ref = bf16[3072,128]{1,0:T(8,128)(2,1)S(1)} collective-permute-done((bf16[3072,128]{1,0:T(8,128)(2,1)S(1)}, bf16[3072,128]{1,0:T(8,128)(2,1)S(1)}, u32[]{:S(2)}, u32[]{:S(2)}) %collective-permute-start) | collective-permute-done | bytes 786464 | tf_op jit(solution)/shard_map/ppermute | solution.py:604
  82.4 4.4 %shard_map.42 = bf16[4,256,128]{2,1,0:T(8,128)(2,1)} custom-call(s32[1]{0:T(128)} %bitcast.core_ref, bf16[3072,128]{1,0:T(8,128)(2,1)S(1)} %shard_map.41.own_ref, bf16[3072,128]{1,0:T(8,128)(2,1)S(1)} %collective-permute-done.other_ref), custom_call_target="tpu_custom_call" | custom-call | flops 671088640 | bytes 2097152 | tf_op jit(solution)/shard_map/pallas_call | solution.py:419
  86.8 1.6 %all-to-all-done.3.q_hbm = bf16[16,128,128]{2,1,0:T(8,128)(2,1)S(1)} async-done(((bf16[16,128,128]{2,1,0:T(8,128)(2,1)}), bf16[16,128,128]{2,1,0:T(8,128)(2,1)S(1)}, u32[]{:S(2)}, u32[]{:S(2)}) %all-to-all-start.3) | async-done | bytes 524320 | tf_op jit(solution)/shard_map/all_to_all | solution.py:432
  88.4 10.1 %all-to-all-start.2 = ((bf16[256,4,128]{2,1,0:T(4,128)(2,1)}), bf16[256,4,128]{2,1,0:T(4,128)(2,1)S(1)}, u32[]{:S(2)}, u32[]{:S(2)}) async-start(bf16[256,4,128]{2,1,0:T(4,128)(2,1)} %bitcast.6), calls=%async_computation.2 | async-start | bytes 524288 | tf_op jit(solution)/shard_map/all_to_all | solution.py:432
  98.5 9.7 %shard_map.45 = bf16[16,144,128]{2,1,0:T(8,128)(2,1)} custom-call(s32[1]{0:T(128)} %bitcast.8.pair_ref, bf16[16,128,128]{2,1,0:T(8,128)(2,1)} %copy-done.4, bf16[8,2,256,128]{3,2,1,0:T(8,128)(2,1)} %all-gather.2.cloned.1.call-done.kv_hbm), custom_call_target="tpu_custom_call" | custom-call | flops 2147483648 | bytes 3145728 | tf_op jit(solution)/shard_map/pallas_call | solution.py:419
  108.2 3.4 %all-to-all-done.2 = bf16[256,4,128]{2,1,0:T(4,128)(2,1)S(1)} async-done(((bf16[256,4,128]{2,1,0:T(4,128)(2,1)}), bf16[256,4,128]{2,1,0:T(4,128)(2,1)S(1)}, u32[]{:S(2)}, u32[]{:S(2)}) %all-to-all-start.2) | async-done | bytes 262176 | tf_op jit(solution)/shard_map/all_to_all | solution.py:432
  111.6 5.8 %all-to-all-start.4 = ((bf16[16,144,128]{2,1,0:T(8,128)(2,1)}), bf16[16,144,128]{2,1,0:T(8,128)(2,1)S(1)}, u32[]{:S(2)}, u32[]{:S(2)}) async-start(bf16[16,144,128]{2,1,0:T(8,128)(2,1)} %shard_map.45), calls=%async_computation.4 | async-start | bytes 1179648 | tf_op jit(solution)/shard_map/all_to_all | solution.py:432
  117.4 1.1 shard_map.43.placed_hbm
  118.5 9.8 %all-to-all-done.4.far_hbm = bf16[16,144,128]{2,1,0:T(8,128)(2,1)S(1)} async-done(((bf16[16,144,128]{2,1,0:T(8,128)(2,1)}), bf16[16,144,128]{2,1,0:T(8,128)(2,1)S(1)}, u32[]{:S(2)}, u32[]{:S(2)}) %all-to-all-start.4) | async-done | bytes 589856 | tf_op jit(solution)/shard_map/all_to_all | solution.py:432
  128.4 0.8 copy-done.3
  129.2 2.9 %shard_map.46 = bf16[128,4096]{1,0:T(8,128)(2,1)} custom-call(bf16[128,4096]{1,0:T(8,128)(2,1)} %shard_map.43.placed_hbm, bf16[16,144,128]{2,1,0:T(8,128)(2,1)} %copy-done.3, f32[16,128,128]{2,1,0:T(8,128)} %get-tuple-element.14.part_hbm, f32[2,128,128]{2,1,0:T(8,128)} %get-tuple-element.10.after_ref.stat_hbm), custom_call_target="tpu_custom_call", output_to_operand_aliasing={{}: (0, {})} | custom-call | flops 33554432 | bytes 3145728 | tf_op jit(solution)/shard_map/pallas_call | solution.py:419
  (12 shorter events, 0.0 us)
Async XLA Ops:
  8.8 21.6 %all-to-all-start = ((bf16[64,8,128]{2,1,0:T(8,128)(2,1)}), bf16[64,8,128]{2,1,0:T(8,128)(2,1)S(1)}, u32[]{:S(2)}, u32[]{:S(2)}) async-start(bf16[64,8,128]{2,1,0:T(8,128)(2,1)} %shard_map.38), calls=%async_computation | async-start | bytes 262144 | tf_op jit(solution)/shard_map/all_to_all | solution.py:432
  31.1 40.2 %all-to-all-start.1 = ((bf16[768,4,128]{2,1,0:T(4,128)(2,1)}), bf16[768,4,128]{2,1,0:T(4,128)(2,1)S(1)}, u32[]{:S(2)}, u32[]{:S(2)}) async-start(bf16[768,4,128]{2,1,0:T(4,128)(2,1)} %bitcast.12), calls=%async_computation.1 | async-start | bytes 1572864 | tf_op jit(solution)/shard_map/all_to_all | solution.py:432
  48.0 50.5 %all-gather.2.cloned.1.call-start = ((), (), s32[]{:S(2)}) async-start(), calls=%async_computation.5 | async-start | bytes 1179648 | tf_op jit(solution)/shard_map/all_gather | solution.py:599
  57.3 0.9 copy-start
  58.3 19.9 %copy-start.1 = (f32[2,128,128]{2,1,0:T(8,128)S(1)}, f32[2,128,128]{2,1,0:T(8,128)}, u32[]{:S(2)}) copy-start(f32[2,128,128]{2,1,0:T(8,128)} %get-tuple-element.10.after_ref.stat_hbm) | copy-start | bytes 393220
  71.3 17.1 %all-to-all-start.3 = ((bf16[16,128,128]{2,1,0:T(8,128)(2,1)}), bf16[16,128,128]{2,1,0:T(8,128)(2,1)S(1)}, u32[]{:S(2)}, u32[]{:S(2)}) async-start(bf16[16,128,128]{2,1,0:T(8,128)(2,1)} %shard_map.44), calls=%async_computation.3 | async-start | bytes 1048576 | tf_op jit(solution)/shard_map/all_to_all | solution.py:432
  78.2 4.2 %collective-permute-start = (bf16[3072,128]{1,0:T(8,128)(2,1)S(1)}, bf16[3072,128]{1,0:T(8,128)(2,1)S(1)}, u32[]{:S(2)}, u32[]{:S(2)}) collective-permute-start(bf16[3072,128]{1,0:T(8,128)(2,1)S(1)} %shard_map.41.own_ref), channel_id=1, source_target_pairs={{0,1},{1,0},{2,3},{3,2},{4,5},{5,4},{6,7},{7,6},{8,9},{9,8},{10,11... | collective-permute-start | bytes 2359304 | tf_op jit(solution)/shard_map/ppermute | solution.py:604
  88.4 10.1 %copy-start.4 = (bf16[16,128,128]{2,1,0:T(8,128)(2,1)}, bf16[16,128,128]{2,1,0:T(8,128)(2,1)S(1)}, u32[]{:S(2)}) copy-start(bf16[16,128,128]{2,1,0:T(8,128)(2,1)S(1)} %all-to-all-done.3.q_hbm) | copy-start | bytes 1572868
  88.4 23.2 %all-to-all-start.2 = ((bf16[256,4,128]{2,1,0:T(4,128)(2,1)}), bf16[256,4,128]{2,1,0:T(4,128)(2,1)S(1)}, u32[]{:S(2)}, u32[]{:S(2)}) async-start(bf16[256,4,128]{2,1,0:T(4,128)(2,1)} %bitcast.6), calls=%async_computation.2 | async-start | bytes 524288 | tf_op jit(solution)/shard_map/all_to_all | solution.py:432
  108.2 9.2 %copy-start.2 = (bf16[8,128,128]{2,1,0:T(8,128)(2,1)S(1)}, bf16[8,128,128]{2,1,0:T(8,128)(2,1)}, u32[]{:S(2)}) copy-start(bf16[8,128,128]{2,1,0:T(8,128)(2,1)} %get-tuple-element.12.row_hbm) | copy-start | bytes 786436
  111.6 16.7 %all-to-all-start.4 = ((bf16[16,144,128]{2,1,0:T(8,128)(2,1)}), bf16[16,144,128]{2,1,0:T(8,128)(2,1)S(1)}, u32[]{:S(2)}, u32[]{:S(2)}) async-start(bf16[16,144,128]{2,1,0:T(8,128)(2,1)} %shard_map.45), calls=%async_computation.4 | async-start | bytes 1179648 | tf_op jit(solution)/shard_map/all_to_all | solution.py:432
  128.4 0.8 copy-start.3
Sparse Core Ops, SparseCore 0:
  50.9 38.0 all-gather.1

commit v9 on v8

--- a/solution.py
+++ b/solution.py
@@ -581,7 +581,7 @@
             dma(14),
         ],
         alias={0: 0},
-        room=500_000,
+        room=900_000,
         flops=2 * 8 * 128 * 128 * 128,
         moved=3 * mib,
     )
@@ -593,9 +593,9 @@
     wide = ("z", "u", "v", "w", "x")
     back = ("x", "z", "u", "v", "w")
     summary = exchange(pack_summary(keys, values), plane)
-    summary = summary.reshape(64, 2, ROWS, HD).transpose(1, 0, 2, 3).reshape(1, 2, 256, HD)
     items, heads = pack(queries, keys, values)
     items = ordered(summary, items, room=0)
+    summary = summary.reshape(64, 2, ROWS, HD).transpose(1, 0, 2, 3).reshape(1, 2, 256, HD)
     summary = lax.all_gather(summary, "z", axis=0, tiled=True)
     items = exchange(items.reshape(768, ROWS, HD), wide).reshape(3072, HD)
     row_out, part, stat = rows(queries, keys, values)

time: 140 us -> 140 us (level)
  transfers between devices with their start and end apart: 7 -> 7, of which waited for: 6 -> 6; matrix products, arithmetic and copies ran while one was open for 0% -> 1% of each run, Pallas kernels for 20% -> 20%
where the time goes in v9:
time: 140 us; the launch traced here: 139 us
  starting transfers between devices  53.6 us (38%)
  waiting for transfers between devices  35.8 us (26%)
  Pallas kernels  32.9 us (24%)
  between operations  13.6 us (10%)
  local copies, waits for them, and re-layouts  3.1 us (2%)
    all_to_all x5, starting transfers between devices, exchange(): return lax.all_to_all(array, axes, split_axis=0, concat_axis=0, tiled=True)  51.4 us
    all_to_all x5, waiting for transfers between devices, exchange(): return lax.all_to_all(array, axes, split_axis=0, concat_axis=0, tiled=True)  33.8 us
    pallas_call x10, Pallas kernels, call(): pl.pallas_call(kernel, out_shape=shapes if many else shapes[0], in_specs=...  32.9 us
  transfers between devices with their start and end apart: 7, of which 6 were waited for; matrix products, arithmetic and copies ran while one was open for 1% of the time, Pallas kernels for 20%

profile of v9, /device:TPU:1, one launch (start us, length us, event | category | flops | bytes accessed | tf_op | source)
XLA Modules:
  0.0 139.0 jit_solution(4723751671206141819)
XLA Ops:
  6.5 2.3 %shard_map.38 = bf16[64,8,128]{2,1,0:T(8,128)(2,1)} custom-call(bf16[128,4096]{1,0:T(8,128)(2,1)} %k_hbm.3, bf16[128,4096]{1,0:T(8,128)(2,1)} %v_hbm.3), custom_call_target="tpu_custom_call" | custom-call | flops 8388608 | bytes 1048576 | tf_op jit(solution)/shard_map/pallas_call | solution.py:419
  8.8 11.6 %all-to-all-start = ((bf16[64,8,128]{2,1,0:T(8,128)(2,1)}), bf16[64,8,128]{2,1,0:T(8,128)(2,1)S(1)}, u32[]{:S(2)}, u32[]{:S(2)}) async-start(bf16[64,8,128]{2,1,0:T(8,128)(2,1)} %shard_map.38), calls=%async_computation | async-start | bytes 262144 | tf_op jit(solution)/shard_map/all_to_all | solution.py:432
  20.5 4.0 %shard_map.39 = (bf16[8,384,128]{2,1,0:T(8,128)(2,1)}, bf16[16,128,128]{2,1,0:T(8,128)(2,1)}) custom-call(bf16[128,4096]{1,0:T(8,128)(2,1)} %q_hbm.3, bf16[128,4096]{1,0:T(8,128)(2,1)} %k_hbm.3, bf16[128,4096]{1,0:T(8,128)(2,1)} %v_hbm.3), custom_call_target="tpu_custom_call" | custom-call | flops 301989888 | bytes 4194304 | tf_op jit(solution)/shard_map/pallas_call | solution.py:419
  24.5 5.9 %all-to-all-done.after_ref = bf16[64,8,128]{2,1,0:T(8,128)(2,1)S(1)} async-done(((bf16[64,8,128]{2,1,0:T(8,128)(2,1)}), bf16[64,8,128]{2,1,0:T(8,128)(2,1)S(1)}, u32[]{:S(2)}, u32[]{:S(2)}) %all-to-all-start) | async-done | bytes 131104 | tf_op jit(solution)/shard_map/all_to_all | solution.py:432
  30.4 0.6 copy-done.4
  31.1 17.0 %all-to-all-start.1 = ((bf16[768,4,128]{2,1,0:T(4,128)(2,1)}), bf16[768,4,128]{2,1,0:T(4,128)(2,1)S(1)}, u32[]{:S(2)}, u32[]{:S(2)}) async-start(bf16[768,4,128]{2,1,0:T(4,128)(2,1)} %bitcast.12), calls=%async_computation.1 | async-start | bytes 1572864 | tf_op jit(solution)/shard_map/all_to_all | solution.py:432
  48.1 0.0 all-gather.2.cloned.1.call-start
  48.1 0.7 copy.9
  48.8 8.6 %shard_map.37 = (bf16[8,128,128]{2,1,0:T(8,128)(2,1)}, f32[16,128,128]{2,1,0:T(8,128)}, f32[2,128,128]{2,1,0:T(8,128)}) custom-call(bf16[128,4096]{1,0:T(8,128)(2,1)} %q_hbm.3, bf16[128,4096]{1,0:T(8,128)(2,1)} %k_hbm.3, bf16[128,4096]{1,0:T(8,128)(2,1)} %v_hbm.3), custom_call_target="tpu_custom_call" | custom-call | flops 201326592 | bytes 5242880 | tf_op jit(solution)/shard_map/pallas_call | solution.py:419
  57.5 0.9 copy-done
  58.4 13.0 %all-to-all-done.1 = bf16[768,4,128]{2,1,0:T(4,128)(2,1)S(1)} async-done(((bf16[768,4,128]{2,1,0:T(4,128)(2,1)}), bf16[768,4,128]{2,1,0:T(4,128)(2,1)S(1)}, u32[]{:S(2)}, u32[]{:S(2)}) %all-to-all-start.1) | async-done | bytes 786464 | tf_op jit(solution)/shard_map/all_to_all | solution.py:432
  71.4 6.9 %all-to-all-start.3 = ((bf16[16,128,128]{2,1,0:T(8,128)(2,1)}), bf16[16,128,128]{2,1,0:T(8,128)(2,1)S(1)}, u32[]{:S(2)}, u32[]{:S(2)}) async-start(bf16[16,128,128]{2,1,0:T(8,128)(2,1)} %shard_map.44), calls=%async_computation.3 | async-start | bytes 1048576 | tf_op jit(solution)/shard_map/all_to_all | solution.py:432
  78.3 2.2 %collective-permute-start = (bf16[3072,128]{1,0:T(8,128)(2,1)S(1)}, bf16[3072,128]{1,0:T(8,128)(2,1)S(1)}, u32[]{:S(2)}, u32[]{:S(2)}) collective-permute-start(bf16[3072,128]{1,0:T(8,128)(2,1)S(1)} %shard_map.41.own_ref), channel_id=1, source_target_pairs={{0,1},{1,0},{2,3},{3,2},{4,5},{5,4},{6,7},{7,6},{8,9},{9,8},{10,11... | collective-permute-start | bytes 2359304 | tf_op jit(solution)/shard_map/ppermute | solution.py:604
  80.5 2.0 %collective-permute-done.other_ref = bf16[3072,128]{1,0:T(8,128)(2,1)S(1)} collective-permute-done((bf16[3072,128]{1,0:T(8,128)(2,1)S(1)}, bf16[3072,128]{1,0:T(8,128)(2,1)S(1)}, u32[]{:S(2)}, u32[]{:S(2)}) %collective-permute-start) | collective-permute-done | bytes 786464 | tf_op jit(solution)/shard_map/ppermute | solution.py:604
  82.5 4.4 %shard_map.42 = bf16[4,256,128]{2,1,0:T(8,128)(2,1)} custom-call(s32[1]{0:T(128)} %bitcast.core_ref, bf16[3072,128]{1,0:T(8,128)(2,1)S(1)} %shard_map.41.own_ref, bf16[3072,128]{1,0:T(8,128)(2,1)S(1)} %collective-permute-done.other_ref), custom_call_target="tpu_custom_call" | custom-call | flops 671088640 | bytes 2097152 | tf_op jit(solution)/shard_map/pallas_call | solution.py:419
  86.8 1.6 %all-to-all-done.3.q_hbm = bf16[16,128,128]{2,1,0:T(8,128)(2,1)S(1)} async-done(((bf16[16,128,128]{2,1,0:T(8,128)(2,1)}), bf16[16,128,128]{2,1,0:T(8,128)(2,1)S(1)}, u32[]{:S(2)}, u32[]{:S(2)}) %all-to-all-start.3) | async-done | bytes 524320 | tf_op jit(solution)/shard_map/all_to_all | solution.py:432
  88.5 10.1 %all-to-all-start.2 = ((bf16[256,4,128]{2,1,0:T(4,128)(2,1)}), bf16[256,4,128]{2,1,0:T(4,128)(2,1)S(1)}, u32[]{:S(2)}, u32[]{:S(2)}) async-start(bf16[256,4,128]{2,1,0:T(4,128)(2,1)} %bitcast.3), calls=%async_computation.2 | async-start | bytes 524288 | tf_op jit(solution)/shard_map/all_to_all | solution.py:432
  98.6 9.7 %shard_map.45 = bf16[16,144,128]{2,1,0:T(8,128)(2,1)} custom-call(s32[1]{0:T(128)} %bitcast.5.pair_ref, bf16[16,128,128]{2,1,0:T(8,128)(2,1)} %copy-done.6, bf16[8,2,256,128]{3,2,1,0:T(8,128)(2,1)} %all-gather.2.cloned.1.call-done.kv_hbm), custom_call_target="tpu_custom_call" | custom-call | flops 2147483648 | bytes 3145728 | tf_op jit(solution)/shard_map/pallas_call | solution.py:419
  108.3 3.4 %all-to-all-done.2 = bf16[256,4,128]{2,1,0:T(4,128)(2,1)S(1)} async-done(((bf16[256,4,128]{2,1,0:T(4,128)(2,1)}), bf16[256,4,128]{2,1,0:T(4,128)(2,1)S(1)}, u32[]{:S(2)}, u32[]{:S(2)}) %all-to-all-start.2) | async-done | bytes 262176 | tf_op jit(solution)/shard_map/all_to_all | solution.py:432
  111.7 5.8 %all-to-all-start.4 = ((bf16[16,144,128]{2,1,0:T(8,128)(2,1)}), bf16[16,144,128]{2,1,0:T(8,128)(2,1)S(1)}, u32[]{:S(2)}, u32[]{:S(2)}) async-start(bf16[16,144,128]{2,1,0:T(8,128)(2,1)} %shard_map.45), calls=%async_computation.4 | async-start | bytes 1179648 | tf_op jit(solution)/shard_map/all_to_all | solution.py:432
  117.5 1.1 shard_map.43.placed_hbm
  118.6 9.8 %all-to-all-done.4.far_hbm = bf16[16,144,128]{2,1,0:T(8,128)(2,1)S(1)} async-done(((bf16[16,144,128]{2,1,0:T(8,128)(2,1)}), bf16[16,144,128]{2,1,0:T(8,128)(2,1)S(1)}, u32[]{:S(2)}, u32[]{:S(2)}) %all-to-all-start.4) | async-done | bytes 589856 | tf_op jit(solution)/shard_map/all_to_all | solution.py:432
  128.5 0.8 copy-done.3
  129.3 2.9 %shard_map.46 = bf16[128,4096]{1,0:T(8,128)(2,1)} custom-call(bf16[128,4096]{1,0:T(8,128)(2,1)} %shard_map.43.placed_hbm, bf16[16,144,128]{2,1,0:T(8,128)(2,1)} %copy-done.3, f32[16,128,128]{2,1,0:T(8,128)} %get-tuple-element.14.part_hbm, f32[2,128,128]{2,1,0:T(8,128)} %get-tuple-element.10.after_ref.stat_hbm), custom_call_target="tpu_custom_call", output_to_operand_aliasing={{}: (0, {})} | custom-call | flops 33554432 | bytes 3145728 | tf_op jit(solution)/shard_map/pallas_call | solution.py:419
  (16 shorter events, 0.1 us)
Async XLA Ops:
  8.8 21.6 %all-to-all-start = ((bf16[64,8,128]{2,1,0:T(8,128)(2,1)}), bf16[64,8,128]{2,1,0:T(8,128)(2,1)S(1)}, u32[]{:S(2)}, u32[]{:S(2)}) async-start(bf16[64,8,128]{2,1,0:T(8,128)(2,1)} %shard_map.38), calls=%async_computation | async-start | bytes 262144 | tf_op jit(solution)/shard_map/all_to_all | solution.py:432
  30.4 0.6 copy-start.4
  31.1 17.1 %copy-start.5 = (bf16[64,8,128]{2,1,0:T(8,128)(2,1)S(1)}, bf16[64,8,128]{2,1,0:T(8,128)(2,1)}, u32[]{:S(2)}) copy-start(bf16[64,8,128]{2,1,0:T(8,128)(2,1)} %copy-done.4) | copy-start | bytes 393220
  31.1 40.3 %all-to-all-start.1 = ((bf16[768,4,128]{2,1,0:T(4,128)(2,1)}), bf16[768,4,128]{2,1,0:T(4,128)(2,1)S(1)}, u32[]{:S(2)}, u32[]{:S(2)}) async-start(bf16[768,4,128]{2,1,0:T(4,128)(2,1)} %bitcast.12), calls=%async_computation.1 | async-start | bytes 1572864 | tf_op jit(solution)/shard_map/all_to_all | solution.py:432
  48.1 50.5 %all-gather.2.cloned.1.call-start = ((), (), s32[]{:S(2)}) async-start(), calls=%async_computation.5 | async-start | bytes 1179648 | tf_op jit(solution)/shard_map/all_gather | solution.py:599
  57.5 0.9 copy-start
  58.4 19.9 %copy-start.1 = (f32[2,128,128]{2,1,0:T(8,128)S(1)}, f32[2,128,128]{2,1,0:T(8,128)}, u32[]{:S(2)}) copy-start(f32[2,128,128]{2,1,0:T(8,128)} %get-tuple-element.10.after_ref.stat_hbm) | copy-start | bytes 393220
  71.4 17.1 %all-to-all-start.3 = ((bf16[16,128,128]{2,1,0:T(8,128)(2,1)}), bf16[16,128,128]{2,1,0:T(8,128)(2,1)S(1)}, u32[]{:S(2)}, u32[]{:S(2)}) async-start(bf16[16,128,128]{2,1,0:T(8,128)(2,1)} %shard_map.44), calls=%async_computation.3 | async-start | bytes 1048576 | tf_op jit(solution)/shard_map/all_to_all | solution.py:432
  78.3 4.2 %collective-permute-start = (bf16[3072,128]{1,0:T(8,128)(2,1)S(1)}, bf16[3072,128]{1,0:T(8,128)(2,1)S(1)}, u32[]{:S(2)}, u32[]{:S(2)}) collective-permute-start(bf16[3072,128]{1,0:T(8,128)(2,1)S(1)} %shard_map.41.own_ref), channel_id=1, source_target_pairs={{0,1},{1,0},{2,3},{3,2},{4,5},{5,4},{6,7},{7,6},{8,9},{9,8},{10,11... | collective-permute-start | bytes 2359304 | tf_op jit(solution)/shard_map/ppermute | solution.py:604
  88.5 10.1 %copy-start.6 = (bf16[16,128,128]{2,1,0:T(8,128)(2,1)}, bf16[16,128,128]{2,1,0:T(8,128)(2,1)S(1)}, u32[]{:S(2)}) copy-start(bf16[16,128,128]{2,1,0:T(8,128)(2,1)S(1)} %all-to-all-done.3.q_hbm) | copy-start | bytes 1572868
  88.5 23.3 %all-to-all-start.2 = ((bf16[256,4,128]{2,1,0:T(4,128)(2,1)}), bf16[256,4,128]{2,1,0:T(4,128)(2,1)S(1)}, u32[]{:S(2)}, u32[]{:S(2)}) async-start(bf16[256,4,128]{2,1,0:T(4,128)(2,1)} %bitcast.3), calls=%async_computation.2 | async-start | bytes 524288 | tf_op jit(solution)/shard_map/all_to_all | solution.py:432
  108.3 9.2 %copy-start.2 = (bf16[8,128,128]{2,1,0:T(8,128)(2,1)S(1)}, bf16[8,128,128]{2,1,0:T(8,128)(2,1)}, u32[]{:S(2)}) copy-start(bf16[8,128,128]{2,1,0:T(8,128)(2,1)} %get-tuple-element.12.row_hbm) | copy-start | bytes 786436
  111.7 16.7 %all-to-all-start.4 = ((bf16[16,144,128]{2,1,0:T(8,128)(2,1)}), bf16[16,144,128]{2,1,0:T(8,128)(2,1)S(1)}, u32[]{:S(2)}, u32[]{:S(2)}) async-start(bf16[16,144,128]{2,1,0:T(8,128)(2,1)} %shard_map.45), calls=%async_computation.4 | async-start | bytes 1179648 | tf_op jit(solution)/shard_map/all_to_all | solution.py:432
  128.4 0.8 copy-start.3
Sparse Core Ops, SparseCore 0:
  51.0 38.0 all-gather.1

commit v10 on v9

--- a/solution.py
+++ b/solution.py
@@ -581,7 +581,7 @@
             dma(14),
         ],
         alias={0: 0},
-        room=900_000,
+        room=2_300_000,
         flops=2 * 8 * 128 * 128 * 128,
         moved=3 * mib,
     )
@@ -594,7 +594,7 @@
     back = ("x", "z", "u", "v", "w")
     summary = exchange(pack_summary(keys, values), plane)
     items, heads = pack(queries, keys, values)
-    items = ordered(summary, items, room=0)
+    items = ordered(summary, items, room=1_700_000)
     summary = summary.reshape(64, 2, ROWS, HD).transpose(1, 0, 2, 3).reshape(1, 2, 256, HD)
     summary = lax.all_gather(summary, "z", axis=0, tiled=True)
     items = exchange(items.reshape(768, ROWS, HD), wide).reshape(3072, HD)

time: 140 us -> 140 us (level)
  no operation moved by 1% of the time
where the time goes in v10:
time: 140 us; the launch traced here: 139 us
  starting transfers between devices  53.6 us (38%)
  waiting for transfers between devices  35.8 us (26%)
  Pallas kernels  32.9 us (24%)
  between operations  13.6 us (10%)
  local copies, waits for them, and re-layouts  3.1 us (2%)
    all_to_all x5, starting transfers between devices, exchange(): return lax.all_to_all(array, axes, split_axis=0, concat_axis=0, tiled=True)  51.4 us
    all_to_all x5, waiting for transfers between devices, exchange(): return lax.all_to_all(array, axes, split_axis=0, concat_axis=0, tiled=True)  33.8 us
    pallas_call x10, Pallas kernels, call(): pl.pallas_call(kernel, out_shape=shapes if many else shapes[0], in_specs=...  32.9 us
  transfers between devices with their start and end apart: 7, of which 6 were waited for; matrix products, arithmetic and copies ran while one was open for 1% of the time, Pallas kernels for 20%

profile of v10, /device:TPU:1, one launch (start us, length us, event | category | flops | bytes accessed | tf_op | source)
XLA Modules:
  0.0 139.0 jit_solution(4723751671206141819)
XLA Ops:
  6.5 2.3 %shard_map.38 = bf16[64,8,128]{2,1,0:T(8,128)(2,1)} custom-call(bf16[128,4096]{1,0:T(8,128)(2,1)} %k_hbm.3, bf16[128,4096]{1,0:T(8,128)(2,1)} %v_hbm.3), custom_call_target="tpu_custom_call" | custom-call | flops 8388608 | bytes 1048576 | tf_op jit(solution)/shard_map/pallas_call | solution.py:419
  8.8 11.6 %all-to-all-start = ((bf16[64,8,128]{2,1,0:T(8,128)(2,1)}), bf16[64,8,128]{2,1,0:T(8,128)(2,1)S(1)}, u32[]{:S(2)}, u32[]{:S(2)}) async-start(bf16[64,8,128]{2,1,0:T(8,128)(2,1)} %shard_map.38), calls=%async_computation | async-start | bytes 262144 | tf_op jit(solution)/shard_map/all_to_all | solution.py:432
  20.5 4.0 %shard_map.39 = (bf16[8,384,128]{2,1,0:T(8,128)(2,1)}, bf16[16,128,128]{2,1,0:T(8,128)(2,1)}) custom-call(bf16[128,4096]{1,0:T(8,128)(2,1)} %q_hbm.3, bf16[128,4096]{1,0:T(8,128)(2,1)} %k_hbm.3, bf16[128,4096]{1,0:T(8,128)(2,1)} %v_hbm.3), custom_call_target="tpu_custom_call" | custom-call | flops 301989888 | bytes 4194304 | tf_op jit(solution)/shard_map/pallas_call | solution.py:419
  24.5 5.9 %all-to-all-done.after_ref = bf16[64,8,128]{2,1,0:T(8,128)(2,1)S(1)} async-done(((bf16[64,8,128]{2,1,0:T(8,128)(2,1)}), bf16[64,8,128]{2,1,0:T(8,128)(2,1)S(1)}, u32[]{:S(2)}, u32[]{:S(2)}) %all-to-all-start) | async-done | bytes 131104 | tf_op jit(solution)/shard_map/all_to_all | solution.py:432
  30.4 0.6 copy-done.4
  31.1 17.0 %all-to-all-start.1 = ((bf16[768,4,128]{2,1,0:T(4,128)(2,1)}), bf16[768,4,128]{2,1,0:T(4,128)(2,1)S(1)}, u32[]{:S(2)}, u32[]{:S(2)}) async-start(bf16[768,4,128]{2,1,0:T(4,128)(2,1)} %bitcast.12), calls=%async_computation.1 | async-start | bytes 1572864 | tf_op jit(solution)/shard_map/all_to_all | solution.py:432
  48.1 0.0 all-gather.2.cloned.1.call-start
  48.1 0.7 copy.9
  48.8 8.6 %shard_map.37 = (bf16[8,128,128]{2,1,0:T(8,128)(2,1)}, f32[16,128,128]{2,1,0:T(8,128)}, f32[2,128,128]{2,1,0:T(8,128)}) custom-call(bf16[128,4096]{1,0:T(8,128)(2,1)} %q_hbm.3, bf16[128,4096]{1,0:T(8,128)(2,1)} %k_hbm.3, bf16[128,4096]{1,0:T(8,128)(2,1)} %v_hbm.3), custom_call_target="tpu_custom_call" | custom-call | flops 201326592 | bytes 5242880 | tf_op jit(solution)/shard_map/pallas_call | solution.py:419
  57.5 0.9 copy-done
  58.4 13.0 %all-to-all-done.1 = bf16[768,4,128]{2,1,0:T(4,128)(2,1)S(1)} async-done(((bf16[768,4,128]{2,1,0:T(4,128)(2,1)}), bf16[768,4,128]{2,1,0:T(4,128)(2,1)S(1)}, u32[]{:S(2)}, u32[]{:S(2)}) %all-to-all-start.1) | async-done | bytes 786464 | tf_op jit(solution)/shard_map/all_to_all | solution.py:432
  71.4 6.9 %all-to-all-start.3 = ((bf16[16,128,128]{2,1,0:T(8,128)(2,1)}), bf16[16,128,128]{2,1,0:T(8,128)(2,1)S(1)}, u32[]{:S(2)}, u32[]{:S(2)}) async-start(bf16[16,128,128]{2,1,0:T(8,128)(2,1)} %shard_map.44), calls=%async_computation.3 | async-start | bytes 1048576 | tf_op jit(solution)/shard_map/all_to_all | solution.py:432
  78.3 2.2 %collective-permute-start = (bf16[3072,128]{1,0:T(8,128)(2,1)S(1)}, bf16[3072,128]{1,0:T(8,128)(2,1)S(1)}, u32[]{:S(2)}, u32[]{:S(2)}) collective-permute-start(bf16[3072,128]{1,0:T(8,128)(2,1)S(1)} %shard_map.41.own_ref), channel_id=1, source_target_pairs={{0,1},{1,0},{2,3},{3,2},{4,5},{5,4},{6,7},{7,6},{8,9},{9,8},{10,11... | collective-permute-start | bytes 2359304 | tf_op jit(solution)/shard_map/ppermute | solution.py:604
  80.5 2.0 %collective-permute-done.other_ref = bf16[3072,128]{1,0:T(8,128)(2,1)S(1)} collective-permute-done((bf16[3072,128]{1,0:T(8,128)(2,1)S(1)}, bf16[3072,128]{1,0:T(8,128)(2,1)S(1)}, u32[]{:S(2)}, u32[]{:S(2)}) %collective-permute-start) | collective-permute-done | bytes 786464 | tf_op jit(solution)/shard_map/ppermute | solution.py:604
  82.5 4.4 %shard_map.42 = bf16[4,256,128]{2,1,0:T(8,128)(2,1)} custom-call(s32[1]{0:T(128)} %bitcast.core_ref, bf16[3072,128]{1,0:T(8,128)(2,1)S(1)} %shard_map.41.own_ref, bf16[3072,128]{1,0:T(8,128)(2,1)S(1)} %collective-permute-done.other_ref), custom_call_target="tpu_custom_call" | custom-call | flops 671088640 | bytes 2097152 | tf_op jit(solution)/shard_map/pallas_call | solution.py:419
  86.8 1.6 %all-to-all-done.3.q_hbm = bf16[16,128,128]{2,1,0:T(8,128)(2,1)S(1)} async-done(((bf16[16,128,128]{2,1,0:T(8,128)(2,1)}), bf16[16,128,128]{2,1,0:T(8,128)(2,1)S(1)}, u32[]{:S(2)}, u32[]{:S(2)}) %all-to-all-start.3) | async-done | bytes 524320 | tf_op jit(solution)/shard_map/all_to_all | solution.py:432
  88.5 10.1 %all-to-all-start.2 = ((bf16[256,4,128]{2,1,0:T(4,128)(2,1)}), bf16[256,4,128]{2,1,0:T(4,128)(2,1)S(1)}, u32[]{:S(2)}, u32[]{:S(2)}) async-start(bf16[256,4,128]{2,1,0:T(4,128)(2,1)} %bitcast.3), calls=%async_computation.2 | async-start | bytes 524288 | tf_op jit(solution)/shard_map/all_to_all | solution.py:432
  98.6 9.7 %shard_map.45 = bf16[16,144,128]{2,1,0:T(8,128)(2,1)} custom-call(s32[1]{0:T(128)} %bitcast.5.pair_ref, bf16[16,128,128]{2,1,0:T(8,128)(2,1)} %copy-done.6, bf16[8,2,256,128]{3,2,1,0:T(8,128)(2,1)} %all-gather.2.cloned.1.call-done.kv_hbm), custom_call_target="tpu_custom_call" | custom-call | flops 2147483648 | bytes 3145728 | tf_op jit(solution)/shard_map/pallas_call | solution.py:419
  108.3 3.4 %all-to-all-done.2 = bf16[256,4,128]{2,1,0:T(4,128)(2,1)S(1)} async-done(((bf16[256,4,128]{2,1,0:T(4,128)(2,1)}), bf16[256,4,128]{2,1,0:T(4,128)(2,1)S(1)}, u32[]{:S(2)}, u32[]{:S(2)}) %all-to-all-start.2) | async-done | bytes 262176 | tf_op jit(solution)/shard_map/all_to_all | solution.py:432
  111.7 5.8 %all-to-all-start.4 = ((bf16[16,144,128]{2,1,0:T(8,128)(2,1)}), bf16[16,144,128]{2,1,0:T(8,128)(2,1)S(1)}, u32[]{:S(2)}, u32[]{:S(2)}) async-start(bf16[16,144,128]{2,1,0:T(8,128)(2,1)} %shard_map.45), calls=%async_computation.4 | async-start | bytes 1179648 | tf_op jit(solution)/shard_map/all_to_all | solution.py:432
  117.5 1.1 shard_map.43.placed_hbm
  118.6 9.8 %all-to-all-done.4.far_hbm = bf16[16,144,128]{2,1,0:T(8,128)(2,1)S(1)} async-done(((bf16[16,144,128]{2,1,0:T(8,128)(2,1)}), bf16[16,144,128]{2,1,0:T(8,128)(2,1)S(1)}, u32[]{:S(2)}, u32[]{:S(2)}) %all-to-all-start.4) | async-done | bytes 589856 | tf_op jit(solution)/shard_map/all_to_all | solution.py:432
  128.5 0.8 copy-done.3
  129.3 2.9 %shard_map.46 = bf16[128,4096]{1,0:T(8,128)(2,1)} custom-call(bf16[128,4096]{1,0:T(8,128)(2,1)} %shard_map.43.placed_hbm, bf16[16,144,128]{2,1,0:T(8,128)(2,1)} %copy-done.3, f32[16,128,128]{2,1,0:T(8,128)} %get-tuple-element.14.part_hbm, f32[2,128,128]{2,1,0:T(8,128)} %get-tuple-element.10.after_ref.stat_hbm), custom_call_target="tpu_custom_call", output_to_operand_aliasing={{}: (0, {})} | custom-call | flops 33554432 | bytes 3145728 | tf_op jit(solution)/shard_map/pallas_call | solution.py:419
  (16 shorter events, 0.1 us)
Async XLA Ops:
  8.8 21.6 %all-to-all-start = ((bf16[64,8,128]{2,1,0:T(8,128)(2,1)}), bf16[64,8,128]{2,1,0:T(8,128)(2,1)S(1)}, u32[]{:S(2)}, u32[]{:S(2)}) async-start(bf16[64,8,128]{2,1,0:T(8,128)(2,1)} %shard_map.38), calls=%async_computation | async-start | bytes 262144 | tf_op jit(solution)/shard_map/all_to_all | solution.py:432
  30.4 0.6 copy-start.4
  31.1 17.1 %copy-start.5 = (bf16[64,8,128]{2,1,0:T(8,128)(2,1)S(1)}, bf16[64,8,128]{2,1,0:T(8,128)(2,1)}, u32[]{:S(2)}) copy-start(bf16[64,8,128]{2,1,0:T(8,128)(2,1)} %copy-done.4) | copy-start | bytes 393220
  31.1 40.3 %all-to-all-start.1 = ((bf16[768,4,128]{2,1,0:T(4,128)(2,1)}), bf16[768,4,128]{2,1,0:T(4,128)(2,1)S(1)}, u32[]{:S(2)}, u32[]{:S(2)}) async-start(bf16[768,4,128]{2,1,0:T(4,128)(2,1)} %bitcast.12), calls=%async_computation.1 | async-start | bytes 1572864 | tf_op jit(solution)/shard_map/all_to_all | solution.py:432
  48.1 50.5 %all-gather.2.cloned.1.call-start = ((), (), s32[]{:S(2)}) async-start(), calls=%async_computation.5 | async-start | bytes 1179648 | tf_op jit(solution)/shard_map/all_gather | solution.py:599
  57.5 0.9 copy-start
  58.4 19.9 %copy-start.1 = (f32[2,128,128]{2,1,0:T(8,128)S(1)}, f32[2,128,128]{2,1,0:T(8,128)}, u32[]{:S(2)}) copy-start(f32[2,128,128]{2,1,0:T(8,128)} %get-tuple-element.10.after_ref.stat_hbm) | copy-start | bytes 393220
  71.4 17.1 %all-to-all-start.3 = ((bf16[16,128,128]{2,1,0:T(8,128)(2,1)}), bf16[16,128,128]{2,1,0:T(8,128)(2,1)S(1)}, u32[]{:S(2)}, u32[]{:S(2)}) async-start(bf16[16,128,128]{2,1,0:T(8,128)(2,1)} %shard_map.44), calls=%async_computation.3 | async-start | bytes 1048576 | tf_op jit(solution)/shard_map/all_to_all | solution.py:432
  78.3 4.2 %collective-permute-start = (bf16[3072,128]{1,0:T(8,128)(2,1)S(1)}, bf16[3072,128]{1,0:T(8,128)(2,1)S(1)}, u32[]{:S(2)}, u32[]{:S(2)}) collective-permute-start(bf16[3072,128]{1,0:T(8,128)(2,1)S(1)} %shard_map.41.own_ref), channel_id=1, source_target_pairs={{0,1},{1,0},{2,3},{3,2},{4,5},{5,4},{6,7},{7,6},{8,9},{9,8},{10,11... | collective-permute-start | bytes 2359304 | tf_op jit(solution)/shard_map/ppermute | solution.py:604
  88.5 10.1 %copy-start.6 = (bf16[16,128,128]{2,1,0:T(8,128)(2,1)}, bf16[16,128,128]{2,1,0:T(8,128)(2,1)S(1)}, u32[]{:S(2)}) copy-start(bf16[16,128,128]{2,1,0:T(8,128)(2,1)S(1)} %all-to-all-done.3.q_hbm) | copy-start | bytes 1572868
  88.5 23.3 %all-to-all-start.2 = ((bf16[256,4,128]{2,1,0:T(4,128)(2,1)}), bf16[256,4,128]{2,1,0:T(4,128)(2,1)S(1)}, u32[]{:S(2)}, u32[]{:S(2)}) async-start(bf16[256,4,128]{2,1,0:T(4,128)(2,1)} %bitcast.3), calls=%async_computation.2 | async-start | bytes 524288 | tf_op jit(solution)/shard_map/all_to_all | solution.py:432
  108.3 9.2 %copy-start.2 = (bf16[8,128,128]{2,1,0:T(8,128)(2,1)S(1)}, bf16[8,128,128]{2,1,0:T(8,128)(2,1)}, u32[]{:S(2)}) copy-start(bf16[8,128,128]{2,1,0:T(8,128)(2,1)} %get-tuple-element.12.row_hbm) | copy-start | bytes 786436
  111.7 16.7 %all-to-all-start.4 = ((bf16[16,144,128]{2,1,0:T(8,128)(2,1)}), bf16[16,144,128]{2,1,0:T(8,128)(2,1)S(1)}, u32[]{:S(2)}, u32[]{:S(2)}) async-start(bf16[16,144,128]{2,1,0:T(8,128)(2,1)} %shard_map.45), calls=%async_computation.4 | async-start | bytes 1179648 | tf_op jit(solution)/shard_map/all_to_all | solution.py:432
  128.4 0.8 copy-start.3
Sparse Core Ops, SparseCore 0:
  51.0 38.0 all-gather.1

commit v11 on v9

--- a/solution.py
+++ b/solution.py
@@ -581,7 +581,7 @@
             dma(14),
         ],
         alias={0: 0},
-        room=900_000,
+        room=46_000_000,
         flops=2 * 8 * 128 * 128 * 128,
         moved=3 * mib,
     )

time: 140 us -> 138 us (0.986)
  no operation moved by 1% of the time
where the time goes in v11:
time: 138 us
  starting transfers between devices  53.6 us (39%)
  waiting for transfers between devices  35.8 us (26%)
  Pallas kernels  32.2 us (23%)
  between operations  13.6 us (10%)
  local copies, waits for them, and re-layouts  2.26 us (2%)
    all_to_all x5, starting transfers between devices, exchange(): return lax.all_to_all(array, axes, split_axis=0, concat_axis=0, tiled=True)  51.4 us
    all_to_all x5, waiting for transfers between devices, exchange(): return lax.all_to_all(array, axes, split_axis=0, concat_axis=0, tiled=True)  33.8 us
    pallas_call x10, Pallas kernels, call(): pl.pallas_call(kernel, out_shape=shapes if many else shapes[0], in_specs=...  32.2 us
  transfers between devices with their start and end apart: 7, of which 6 were waited for; matrix products, arithmetic and copies ran while one was open for 1% of the time, Pallas kernels for 20%

profile of v11, /device:TPU:1, one launch (start us, length us, event | category | flops | bytes accessed | tf_op | source)
XLA Modules:
  0.0 137.5 jit_solution(16808607622225056013)
XLA Ops:
  6.5 2.3 %shard_map.38 = bf16[64,8,128]{2,1,0:T(8,128)(2,1)} custom-call(bf16[128,4096]{1,0:T(8,128)(2,1)} %k_hbm.3, bf16[128,4096]{1,0:T(8,128)(2,1)} %v_hbm.3), custom_call_target="tpu_custom_call" | custom-call | flops 8388608 | bytes 1048576 | tf_op jit(solution)/shard_map/pallas_call | solution.py:419
  8.8 11.6 %all-to-all-start = ((bf16[64,8,128]{2,1,0:T(8,128)(2,1)}), bf16[64,8,128]{2,1,0:T(8,128)(2,1)S(1)}, u32[]{:S(2)}, u32[]{:S(2)}) async-start(bf16[64,8,128]{2,1,0:T(8,128)(2,1)} %shard_map.38), calls=%async_computation | async-start | bytes 262144 | tf_op jit(solution)/shard_map/all_to_all | solution.py:432
  20.5 4.0 %shard_map.39 = (bf16[8,384,128]{2,1,0:T(8,128)(2,1)}, bf16[16,128,128]{2,1,0:T(8,128)(2,1)}) custom-call(bf16[128,4096]{1,0:T(8,128)(2,1)} %q_hbm.3, bf16[128,4096]{1,0:T(8,128)(2,1)} %k_hbm.3, bf16[128,4096]{1,0:T(8,128)(2,1)} %v_hbm.3), custom_call_target="tpu_custom_call" | custom-call | flops 301989888 | bytes 4194304 | tf_op jit(solution)/shard_map/pallas_call | solution.py:419
  24.5 5.9 %all-to-all-done.after_ref = bf16[64,8,128]{2,1,0:T(8,128)(2,1)S(1)} async-done(((bf16[64,8,128]{2,1,0:T(8,128)(2,1)}), bf16[64,8,128]{2,1,0:T(8,128)(2,1)S(1)}, u32[]{:S(2)}, u32[]{:S(2)}) %all-to-all-start) | async-done | bytes 131104 | tf_op jit(solution)/shard_map/all_to_all | solution.py:432
  30.4 0.6 copy-done.4
  31.1 17.0 %all-to-all-start.1 = ((bf16[768,4,128]{2,1,0:T(4,128)(2,1)}), bf16[768,4,128]{2,1,0:T(4,128)(2,1)S(1)}, u32[]{:S(2)}, u32[]{:S(2)}) async-start(bf16[768,4,128]{2,1,0:T(4,128)(2,1)} %bitcast.12), calls=%async_computation.1 | async-start | bytes 1572864 | tf_op jit(solution)/shard_map/all_to_all | solution.py:432
  48.1 0.0 all-gather.2.cloned.1.call-start
  48.1 0.7 copy.9
  48.8 8.6 %shard_map.37 = (bf16[8,128,128]{2,1,0:T(8,128)(2,1)}, f32[16,128,128]{2,1,0:T(8,128)}, f32[2,128,128]{2,1,0:T(8,128)}) custom-call(bf16[128,4096]{1,0:T(8,128)(2,1)} %q_hbm.3, bf16[128,4096]{1,0:T(8,128)(2,1)} %k_hbm.3, bf16[128,4096]{1,0:T(8,128)(2,1)} %v_hbm.3), custom_call_target="tpu_custom_call" | custom-call | flops 201326592 | bytes 5242880 | tf_op jit(solution)/shard_map/pallas_call | solution.py:419
  57.5 0.9 copy-done
  58.4 13.0 %all-to-all-done.1 = bf16[768,4,128]{2,1,0:T(4,128)(2,1)S(1)} async-done(((bf16[768,4,128]{2,1,0:T(4,128)(2,1)}), bf16[768,4,128]{2,1,0:T(4,128)(2,1)S(1)}, u32[]{:S(2)}, u32[]{:S(2)}) %all-to-all-start.1) | async-done | bytes 786464 | tf_op jit(solution)/shard_map/all_to_all | solution.py:432
  71.4 6.9 %all-to-all-start.3 = ((bf16[16,128,128]{2,1,0:T(8,128)(2,1)}), bf16[16,128,128]{2,1,0:T(8,128)(2,1)S(1)}, u32[]{:S(2)}, u32[]{:S(2)}) async-start(bf16[16,128,128]{2,1,0:T(8,128)(2,1)} %shard_map.44), calls=%async_computation.3 | async-start | bytes 1048576 | tf_op jit(solution)/shard_map/all_to_all | solution.py:432
  78.3 2.2 %collective-permute-start = (bf16[3072,128]{1,0:T(8,128)(2,1)S(1)}, bf16[3072,128]{1,0:T(8,128)(2,1)S(1)}, u32[]{:S(2)}, u32[]{:S(2)}) collective-permute-start(bf16[3072,128]{1,0:T(8,128)(2,1)S(1)} %shard_map.41.own_ref), channel_id=1, source_target_pairs={{0,1},{1,0},{2,3},{3,2},{4,5},{5,4},{6,7},{7,6},{8,9},{9,8},{10,11... | collective-permute-start | bytes 2359304 | tf_op jit(solution)/shard_map/ppermute | solution.py:604
  80.5 2.0 %collective-permute-done.other_ref = bf16[3072,128]{1,0:T(8,128)(2,1)S(1)} collective-permute-done((bf16[3072,128]{1,0:T(8,128)(2,1)S(1)}, bf16[3072,128]{1,0:T(8,128)(2,1)S(1)}, u32[]{:S(2)}, u32[]{:S(2)}) %collective-permute-start) | collective-permute-done | bytes 786464 | tf_op jit(solution)/shard_map/ppermute | solution.py:604
  82.5 4.4 %shard_map.42 = bf16[4,256,128]{2,1,0:T(8,128)(2,1)} custom-call(s32[1]{0:T(128)} %bitcast.core_ref, bf16[3072,128]{1,0:T(8,128)(2,1)S(1)} %shard_map.41.own_ref, bf16[3072,128]{1,0:T(8,128)(2,1)S(1)} %collective-permute-done.other_ref), custom_call_target="tpu_custom_call" | custom-call | flops 671088640 | bytes 2097152 | tf_op jit(solution)/shard_map/pallas_call | solution.py:419
  86.8 1.6 %all-to-all-done.3.q_hbm = bf16[16,128,128]{2,1,0:T(8,128)(2,1)S(1)} async-done(((bf16[16,128,128]{2,1,0:T(8,128)(2,1)}), bf16[16,128,128]{2,1,0:T(8,128)(2,1)S(1)}, u32[]{:S(2)}, u32[]{:S(2)}) %all-to-all-start.3) | async-done | bytes 524320 | tf_op jit(solution)/shard_map/all_to_all | solution.py:432
  88.5 10.1 %all-to-all-start.2 = ((bf16[256,4,128]{2,1,0:T(4,128)(2,1)}), bf16[256,4,128]{2,1,0:T(4,128)(2,1)S(1)}, u32[]{:S(2)}, u32[]{:S(2)}) async-start(bf16[256,4,128]{2,1,0:T(4,128)(2,1)} %bitcast.3), calls=%async_computation.2 | async-start | bytes 524288 | tf_op jit(solution)/shard_map/all_to_all | solution.py:432
  98.5 0.0 all-gather.2.cloned.1.call-done.kv_hbm
  98.6 9.7 %shard_map.45 = bf16[16,144,128]{2,1,0:T(8,128)(2,1)} custom-call(s32[1]{0:T(128)} %bitcast.5.pair_ref, bf16[16,128,128]{2,1,0:T(8,128)(2,1)} %copy-done.6, bf16[8,2,256,128]{3,2,1,0:T(8,128)(2,1)} %all-gather.2.cloned.1.call-done.kv_hbm), custom_call_target="tpu_custom_call" | custom-call | flops 2147483648 | bytes 3145728 | tf_op jit(solution)/shard_map/pallas_call | solution.py:419
  108.3 3.4 %all-to-all-done.2 = bf16[256,4,128]{2,1,0:T(4,128)(2,1)S(1)} async-done(((bf16[256,4,128]{2,1,0:T(4,128)(2,1)}), bf16[256,4,128]{2,1,0:T(4,128)(2,1)S(1)}, u32[]{:S(2)}, u32[]{:S(2)}) %all-to-all-start.2) | async-done | bytes 262176 | tf_op jit(solution)/shard_map/all_to_all | solution.py:432
  111.7 5.8 %all-to-all-start.4 = ((bf16[16,144,128]{2,1,0:T(8,128)(2,1)}), bf16[16,144,128]{2,1,0:T(8,128)(2,1)S(1)}, u32[]{:S(2)}, u32[]{:S(2)}) async-start(bf16[16,144,128]{2,1,0:T(8,128)(2,1)} %shard_map.45), calls=%async_computation.4 | async-start | bytes 1179648 | tf_op jit(solution)/shard_map/all_to_all | solution.py:432
  117.5 1.1 shard_map.43.placed_hbm
  118.6 9.8 %all-to-all-done.4.far_hbm = bf16[16,144,128]{2,1,0:T(8,128)(2,1)S(1)} async-done(((bf16[16,144,128]{2,1,0:T(8,128)(2,1)}), bf16[16,144,128]{2,1,0:T(8,128)(2,1)S(1)}, u32[]{:S(2)}, u32[]{:S(2)}) %all-to-all-start.4) | async-done | bytes 589856 | tf_op jit(solution)/shard_map/all_to_all | solution.py:432
  128.5 2.2 %shard_map.46 = bf16[128,4096]{1,0:T(8,128)(2,1)} custom-call(bf16[128,4096]{1,0:T(8,128)(2,1)} %shard_map.43.placed_hbm, bf16[16,144,128]{2,1,0:T(8,128)(2,1)S(1)} %all-to-all-done.4.far_hbm, f32[16,128,128]{2,1,0:T(8,128)S(1)} %copy-done.2, f32[2,128,128]{2,1,0:T(8,128)S(1)} %copy-done.1), custom_call_target="tpu_custom_call", output_to_operand_aliasing={{}: (0, {})} | custom-call | flops 33554432 | bytes 3145728 | tf_op jit(solution)/shard_map/pallas_call | solution.py:419
  (16 shorter events, 0.0 us)
Async XLA Ops:
  8.8 21.6 %all-to-all-start = ((bf16[64,8,128]{2,1,0:T(8,128)(2,1)}), bf16[64,8,128]{2,1,0:T(8,128)(2,1)S(1)}, u32[]{:S(2)}, u32[]{:S(2)}) async-start(bf16[64,8,128]{2,1,0:T(8,128)(2,1)} %shard_map.38), calls=%async_computation | async-start | bytes 262144 | tf_op jit(solution)/shard_map/all_to_all | solution.py:432
  30.4 0.6 copy-start.4
  31.1 17.1 %copy-start.5 = (bf16[64,8,128]{2,1,0:T(8,128)(2,1)S(1)}, bf16[64,8,128]{2,1,0:T(8,128)(2,1)}, u32[]{:S(2)}) copy-start(bf16[64,8,128]{2,1,0:T(8,128)(2,1)} %copy-done.4) | copy-start | bytes 393220
  31.1 40.3 %all-to-all-start.1 = ((bf16[768,4,128]{2,1,0:T(4,128)(2,1)}), bf16[768,4,128]{2,1,0:T(4,128)(2,1)S(1)}, u32[]{:S(2)}, u32[]{:S(2)}) async-start(bf16[768,4,128]{2,1,0:T(4,128)(2,1)} %bitcast.12), calls=%async_computation.1 | async-start | bytes 1572864 | tf_op jit(solution)/shard_map/all_to_all | solution.py:432
  48.1 50.5 %all-gather.2.cloned.1.call-start = ((), (), s32[]{:S(2)}) async-start(), calls=%async_computation.5 | async-start | bytes 1179648 | tf_op jit(solution)/shard_map/all_gather | solution.py:599
  57.5 0.9 copy-start
  58.4 19.9 %copy-start.1 = (f32[2,128,128]{2,1,0:T(8,128)S(1)}, f32[2,128,128]{2,1,0:T(8,128)}, u32[]{:S(2)}) copy-start(f32[2,128,128]{2,1,0:T(8,128)} %get-tuple-element.10.after_ref.stat_hbm) | copy-start | bytes 393220
  71.4 17.1 %all-to-all-start.3 = ((bf16[16,128,128]{2,1,0:T(8,128)(2,1)}), bf16[16,128,128]{2,1,0:T(8,128)(2,1)S(1)}, u32[]{:S(2)}, u32[]{:S(2)}) async-start(bf16[16,128,128]{2,1,0:T(8,128)(2,1)} %shard_map.44), calls=%async_computation.3 | async-start | bytes 1048576 | tf_op jit(solution)/shard_map/all_to_all | solution.py:432
  78.3 4.2 %collective-permute-start = (bf16[3072,128]{1,0:T(8,128)(2,1)S(1)}, bf16[3072,128]{1,0:T(8,128)(2,1)S(1)}, u32[]{:S(2)}, u32[]{:S(2)}) collective-permute-start(bf16[3072,128]{1,0:T(8,128)(2,1)S(1)} %shard_map.41.own_ref), channel_id=1, source_target_pairs={{0,1},{1,0},{2,3},{3,2},{4,5},{5,4},{6,7},{7,6},{8,9},{9,8},{10,11... | collective-permute-start | bytes 2359304 | tf_op jit(solution)/shard_map/ppermute | solution.py:604
  88.5 10.1 %copy-start.6 = (bf16[16,128,128]{2,1,0:T(8,128)(2,1)}, bf16[16,128,128]{2,1,0:T(8,128)(2,1)S(1)}, u32[]{:S(2)}) copy-start(bf16[16,128,128]{2,1,0:T(8,128)(2,1)S(1)} %all-to-all-done.3.q_hbm) | copy-start | bytes 1572868
  88.5 23.3 %all-to-all-start.2 = ((bf16[256,4,128]{2,1,0:T(4,128)(2,1)}), bf16[256,4,128]{2,1,0:T(4,128)(2,1)S(1)}, u32[]{:S(2)}, u32[]{:S(2)}) async-start(bf16[256,4,128]{2,1,0:T(4,128)(2,1)} %bitcast.3), calls=%async_computation.2 | async-start | bytes 524288 | tf_op jit(solution)/shard_map/all_to_all | solution.py:432
  108.3 9.3 %copy-start.3 = (bf16[8,128,128]{2,1,0:T(8,128)(2,1)S(1)}, bf16[8,128,128]{2,1,0:T(8,128)(2,1)}, u32[]{:S(2)}) copy-start(bf16[8,128,128]{2,1,0:T(8,128)(2,1)} %get-tuple-element.12.row_hbm) | copy-start | bytes 786436
  111.7 16.7 %all-to-all-start.4 = ((bf16[16,144,128]{2,1,0:T(8,128)(2,1)}), bf16[16,144,128]{2,1,0:T(8,128)(2,1)S(1)}, u32[]{:S(2)}, u32[]{:S(2)}) async-start(bf16[16,144,128]{2,1,0:T(8,128)(2,1)} %shard_map.45), calls=%async_computation.4 | async-start | bytes 1179648 | tf_op jit(solution)/shard_map/all_to_all | solution.py:432
  117.5 10.9 %copy-start.2 = (f32[16,128,128]{2,1,0:T(8,128)S(1)}, f32[16,128,128]{2,1,0:T(8,128)}, u32[]{:S(2)}) copy-start(f32[16,128,128]{2,1,0:T(8,128)} %get-tuple-element.14.part_hbm) | copy-start | bytes 3145732
Sparse Core Ops, SparseCore 0:
  51.0 38.0 all-gather.1
